TPU v7x, 128 devices: a whole 4x4x4 slice. The times are simulated.
128 devices in a mesh: gx: 16 (over y, x_hi, core), gy: 8 (over x_lo, z).
Axes of the slice: x: 4 (x_hi: 2, x_lo: 2; x = x_hi * 2 + x_lo), y: 4, z: 4, core: 2. Of those that a mesh axis runs over, the one named last changes fastest.
Arguments:
- particle_count: int32 [8, 1024, 2048], P(None, ('gx', 'gy')), may hold values from 0 to 12
- drag_coeff: float32 [8, 1024, 2048], P(None, ('gx', 'gy')), may hold values from 0.05 to 2
- particle_velocity: float32 [3, 8, 1024, 2048], P(None, None, ('gx', 'gy')), may hold values from -6 to 6
- fluid_velocity: float32 [3, 8, 1024, 2048], P(None, None, 'gy', 'gx'), may hold values from -6 to 6
Outputs:
- pressure: float32 [8, 1024, 2048], P(None, 'gy', 'gx')
- new_velocity: float32 [3, 8, 1024, 2048], P(None, None, ('gx', 'gy'))
- pressure_gradient: float32 [3, 8, 1024, 2048], P(None, None, ('gx', 'gy'))
All inputs are finite; a program needn't handle non-finite values.
Results may differ from a plain program's by a relative error of at most 0.00002.
Values sent between devices are 32-bit elements; how exact they have to be, the bound alone decides.
No kernel may reach another device: no remote copies, remote signals or barrier semaphores. Data moves between devices by JAX's collectives and lax.ppermute only.
A program may use at most 64 MiB of HBM per device.

v0:
```python
import jax
import jax.numpy as jnp
from jax import lax
from jax.sharding import PartitionSpec as P

SWEEPS = 8


particle_volume = 0.05
time_step = 0.5
viscosity = 0.1


def padded_2(shard, sides, width):
    edges = {}
    for axis, dim in sides:
        devices, length = (lax.axis_size(axis), shard.shape[dim])
        up = [(i, (i + 1) % devices) for i in range(devices - 1)]
        last = lax.slice_in_dim(shard, length - width, length, axis=dim)
        first = lax.slice_in_dim(shard, 0, width, axis=dim)
        edges[dim] = (
            lax.ppermute(last, axis, up),
            lax.ppermute(first, axis, [(b, a) for a, b in up]),
        )
    done = []
    for _, dim in sides:
        low, high = edges[dim]
        around = [(width, width) if d in done else (0, 0) for d in range(shard.ndim)]
        shard = jnp.concatenate([jnp.pad(low, around), shard, jnp.pad(high, around)], axis=dim)
        done.append(dim)
    return shard


def pad_depth(values):
    widths = [(0, 0)] * (values.ndim - 3) + [(1, 1), (0, 0), (0, 0)]
    return jnp.pad(values, widths)


def pad_plane(values):
    widths = [(0, 0)] * (values.ndim - 2) + [(1, 1), (1, 1)]
    return jnp.pad(values, widths)


def pad_second(values):
    widths = [(0, 0)] * (values.ndim - 1) + [(1, 1)]
    return jnp.pad(values, widths)


def middle(values):
    return values[..., 1:-1, 1:-1, 1:-1]


def neighbour(values, which):
    if which == 0:
        return values[..., 2:, 1:-1, 1:-1]
    if which == 1:
        return values[..., :-2, 1:-1, 1:-1]
    if which == 2:
        return values[..., 1:-1, 2:, 1:-1]
    if which == 3:
        return values[..., 1:-1, :-2, 1:-1]
    if which == 4:
        return values[..., 1:-1, 1:-1, 2:]
    return values[..., 1:-1, 1:-1, :-2]


def face_weights(voids_wide):
    padded = pad_depth(voids_wide)
    centre = middle(padded)
    weights = jnp.stack([0.5 * (centre + neighbour(padded, which)) for which in range(6)])
    weight_sum = weights[0]
    for which in range(1, 6):
        weight_sum = weight_sum + weights[which]
    return (weights, weight_sum)


def momentum(velocity_wide, weights, voids, drag, drag_force):
    padded = pad_depth(velocity_wide)
    centre = middle(padded)
    diffusion = jnp.zeros_like(centre)
    for which in range(6):
        diffusion = diffusion + weights[which][None] * (neighbour(padded, which) - centre)
    return (voids[None] * centre + time_step * viscosity * diffusion + time_step * drag_force) / (
        voids[None] + time_step * drag[None]
    )


def divergence(flux_wide):
    first = flux_wide[0][:, 2:, 1:-1] - flux_wide[0][:, :-2, 1:-1]
    second = flux_wide[1][:, 1:-1, 2:] - flux_wide[1][:, 1:-1, :-2]
    normal = pad_depth(flux_wide[2])[:, 1:-1, 1:-1]
    third = normal[2:] - normal[:-2]
    return 0.5 * (first + second + third) / time_step


def jacobi_sweep(pressure_wide, weights, weight_sum, source):
    padded = pad_depth(pressure_wide)
    total = weights[0] * neighbour(padded, 0)
    for which in range(1, 6):
        total = total + weights[which] * neighbour(padded, which)
    return (total - source) / weight_sum


def gradient_of(pressure_wide):
    padded = pad_depth(pressure_wide)
    first = 0.5 * (padded[1:-1, 2:, 1:-1] - padded[1:-1, :-2, 1:-1])
    second = 0.5 * (padded[1:-1, 1:-1, 2:] - padded[1:-1, 1:-1, :-2])
    third = 0.5 * (padded[2:, 1:-1, 1:-1] - padded[:-2, 1:-1, 1:-1])
    return jnp.stack([first, second, third])


def order_inward(values, across, along):
    fields, planes, x_rows, y_cols = values.shape
    groups = across // along
    rows_each = x_rows // across
    shaped = values.reshape(fields, planes, along, groups, rows_each, y_cols)
    return jnp.swapaxes(shaped, 2, 3).reshape(fields, planes, x_rows, y_cols)


def order_outward(values, across, along):
    fields, planes, x_rows, y_cols = values.shape
    groups = across // along
    rows_each = x_rows // across
    shaped = values.reshape(fields, planes, groups, along, rows_each, y_cols)
    return jnp.swapaxes(shaped, 2, 3).reshape(fields, planes, x_rows, y_cols)


def to_fluid(fields):
    moved = lax.all_to_all(
        lax.all_to_all(fields, "gx", split_axis=3, concat_axis=2, tiled=True),
        "gy",
        split_axis=2,
        concat_axis=2,
        tiled=True,
    )
    return order_inward(moved, lax.axis_size("gx"), lax.axis_size("gy"))


def to_particles(fields):
    ordered = order_outward(fields, lax.axis_size("gx"), lax.axis_size("gy"))
    return lax.all_to_all(
        lax.all_to_all(ordered, "gy", split_axis=2, concat_axis=2, tiled=True),
        "gx",
        split_axis=2,
        concat_axis=3,
        tiled=True,
    )


def shards(particle_count, drag_coeff, particle_velocity, fluid_velocity):
    voids = 1.0 - particle_count.astype(jnp.float32) * particle_volume
    drag_force = drag_coeff[None] * particle_velocity
    slab_velocity = to_particles(fluid_velocity)
    stacked = jnp.concatenate([slab_velocity, voids[None]], axis=0)
    widened = pad_second(padded_2(stacked, ((("gx", "gy"), 2),), 1))
    weights, weight_sum = face_weights(widened[3])
    predicted = momentum(widened[:3], weights, voids, drag_coeff, drag_force)
    flux = voids[None] * predicted
    flux_first = pad_second(padded_2(flux[0:1], ((("gx", "gy"), 2),), 1))
    flux_wide = jnp.concatenate([flux_first, pad_plane(flux[1:3])], axis=0)
    source = divergence(flux_wide)
    pressure = -source / weight_sum
    for sweep_index in range(SWEEPS - 1):
        pressure_wide = pad_second(padded_2(pressure, ((("gx", "gy"), 1),), 1))
        pressure = jacobi_sweep(pressure_wide, weights, weight_sum, source)
    final_wide = pad_second(padded_2(pressure, ((("gx", "gy"), 1),), 1))
    slopes = gradient_of(final_wide)
    velocity = predicted - time_step * slopes
    pressure_out = to_fluid(pressure[None])[0]
    return (pressure_out, velocity, slopes)


def solution(mesh):
    placed = (
        P(None, ("gx", "gy"), None),
        P(None, ("gx", "gy"), None),
        P(None, None, ("gx", "gy"), None),
        P(None, None, "gy", "gx"),
    )
    return jax.shard_map(
        shards,
        mesh=mesh,
        in_specs=placed,
        out_specs=(
            P(None, "gy", "gx"),
            P(None, None, ("gx", "gy"), None),
            P(None, None, ("gx", "gy"), None),
        ),
        check_vma=False,
    )
```

profile of v0, /device:TPU:0, one launch (start us, length us, event | category | flops | bytes accessed | tf_op | source)
XLA Modules:
  0.0 257.8 jit_solution(13661601666566487653)
XLA Ops:
  3.1 27.7 %all_to_all.46 = f32[3,8,128,128]{3,1,0,2:T(8,128)} all-to-all(f32[3,8,128,128]{3,1,0,2:T(8,128)S(1)} %copy.52), channel_id=1, replica_groups=mesh['gx'=16,'gy'=8] {'gy'}, dimensions={2} | all-to-all | bytes 3145728 | tf_op jit(solution)/shard_map/all_to_all | solution.py:142
  30.8 6.9 %all-to-all-start.1 = ((f32[3,8,128,128]{3,1,0,2:T(8,128)}), f32[3,8,128,128]{3,1,0,2:T(8,128)S(1)}, u32[]{:S(2)}, u32[]{:S(2)}) async-start(f32[3,8,128,128]{3,1,0,2:T(8,128)} %all_to_all.46), calls=%async_computation.1 | async-start | bytes 3145728 | tf_op jit(solution)/shard_map/all_to_all | solution.py:141
  39.4 22.0 %all-to-all-done.1 = f32[3,8,128,128]{3,1,0,2:T(8,128)S(1)} async-done(((f32[3,8,128,128]{3,1,0,2:T(8,128)}), f32[3,8,128,128]{3,1,0,2:T(8,128)S(1)}, u32[]{:S(2)}, u32[]{:S(2)}) %all-to-all-start.1) | async-done | bytes 1572896 | tf_op jit(solution)/shard_map/all_to_all | solution.py:141
  61.6 2.1 collective-permute-start
  65.0 4.1 %collective-permute-done = f32[4,8,1,2048]{3,1,2,0:T(8,128)S(1)} collective-permute-done((f32[4,8,1,2048]{3,1,2,0:T(8,128)S(1)}, f32[4,8,1,2048]{3,1,2,0:T(8,128)S(1)}, u32[]{:S(2)}, u32[]{:S(2)}) %collective-permute-start) | collective-permute-done | bytes 262176 | tf_op jit(solution)/shard_map/ppermute | solution.py:22
  69.1 4.1 %collective-permute-done.1 = f32[4,8,1,2048]{3,1,2,0:T(8,128)S(1)} collective-permute-done((f32[4,8,1,2048]{3,1,2,0:T(8,128)S(1)}, f32[4,8,1,2048]{3,1,2,0:T(8,128)S(1)}, u32[]{:S(2)}, u32[]{:S(2)}) %collective-permute-start.1) | collective-permute-done | bytes 262176 | tf_op jit(solution)/shard_map/ppermute | solution.py:23
  76.3 4.0 %broadcast_multiply_fusion = (f32[3,8,8,2048]{3,1,2,0:T(8,128)S(1)}, f32[3,8,8,2048]{3,1,2,0:T(8,128)}) fusion(f32[8,8,2048]{2,0,1:T(8,128)S(1)} %copy-done.7, f32[8,8,2048]{2,0,1:T(8,128)S(1)} %copy-done.6, f32[3,8,8,2048]{3,2,1,0:T(8,128)S(1)} %copy-done.8, f32[8,8,2048]{2,0,1:T(8,128)S(1)} %copy-done.5, f32[3,8,8,2048]{3,1,2,0:T(8,128)S(1)} %bitcast.41, ...), kind=kLoop, calls=%fused_computation.64 | loop fusion | flops 11403264 | bytes 17172352 | tf_op jit(solution)/shard_map/mul | solution.py:158
  80.3 2.5 collective-permute-start.2
  84.8 4.2 %collective-permute-done.3 = f32[1,8,1,2048]{3,1,2,0:T(8,128)S(1)} collective-permute-done((f32[1,8,1,2048]{3,1,2,0:T(8,128)S(1)}, f32[1,8,1,2048]{3,1,2,0:T(8,128)S(1)}, u32[]{:S(2)}, u32[]{:S(2)}) %collective-permute-start.3) | collective-permute-done | bytes 65568 | tf_op jit(solution)/shard_map/ppermute | solution.py:23
  90.1 5.3 %collective-permute-start.4 = (f32[8,1,2048]{2,0,1:T(8,128)S(1)}, f32[8,1,2048]{2,0,1:T(8,128)S(1)}, u32[]{:S(2)}, u32[]{:S(2)}) collective-permute-start(f32[8,1,2048]{2,0,1:T(8,128)S(1)} %get-tuple-element.46), channel_id=1, source_target_pairs={{0,1},{1,2},{2,3},{3,4},{4,5},{5,6},{6,7},{7,8},{8,9},{9,10},{10,1... | collective-permute-start | bytes 196616 | tf_op jit(solution)/shard_map/ppermute | solution.py:22
  97.3 4.3 %collective-permute-done.5 = f32[8,1,2048]{2,0,1:T(8,128)S(1)} collective-permute-done((f32[8,1,2048]{2,0,1:T(8,128)S(1)}, f32[8,1,2048]{2,0,1:T(8,128)S(1)}, u32[]{:S(2)}, u32[]{:S(2)}) %collective-permute-start.5) | collective-permute-done | bytes 65568 | tf_op jit(solution)/shard_map/ppermute | solution.py:23
  102.6 4.0 %collective-permute-start.6 = (f32[8,1,2048]{2,0,1:T(8,128)S(1)}, f32[8,1,2048]{2,0,1:T(8,128)S(1)}, u32[]{:S(2)}, u32[]{:S(2)}) collective-permute-start(f32[8,1,2048]{2,0,1:T(8,128)S(1)} %get-tuple-element.44), channel_id=1, source_target_pairs={{0,1},{1,2},{2,3},{3,4},{4,5},{5,6},{6,7},{7,8},{8,9},{9,10},{10,1... | collective-permute-start | bytes 196616 | tf_op jit(solution)/shard_map/ppermute | solution.py:22
  108.5 4.3 %collective-permute-done.7 = f32[8,1,2048]{2,0,1:T(8,128)S(1)} collective-permute-done((f32[8,1,2048]{2,0,1:T(8,128)S(1)}, f32[8,1,2048]{2,0,1:T(8,128)S(1)}, u32[]{:S(2)}, u32[]{:S(2)}) %collective-permute-start.7) | collective-permute-done | bytes 65568 | tf_op jit(solution)/shard_map/ppermute | solution.py:23
  113.8 4.0 %collective-permute-start.8 = (f32[8,1,2048]{2,0,1:T(8,128)S(1)}, f32[8,1,2048]{2,0,1:T(8,128)S(1)}, u32[]{:S(2)}, u32[]{:S(2)}) collective-permute-start(f32[8,1,2048]{2,0,1:T(8,128)S(1)} %get-tuple-element.42), channel_id=1, source_target_pairs={{0,1},{1,2},{2,3},{3,4},{4,5},{5,6},{6,7},{7,8},{8,9},{9,10},{10,1... | collective-permute-start | bytes 196616 | tf_op jit(solution)/shard_map/ppermute | solution.py:22
  119.8 4.3 %collective-permute-done.9 = f32[8,1,2048]{2,0,1:T(8,128)S(1)} collective-permute-done((f32[8,1,2048]{2,0,1:T(8,128)S(1)}, f32[8,1,2048]{2,0,1:T(8,128)S(1)}, u32[]{:S(2)}, u32[]{:S(2)}) %collective-permute-start.9) | collective-permute-done | bytes 65568 | tf_op jit(solution)/shard_map/ppermute | solution.py:23
  125.1 4.0 %collective-permute-start.10 = (f32[8,1,2048]{2,0,1:T(8,128)S(1)}, f32[8,1,2048]{2,0,1:T(8,128)S(1)}, u32[]{:S(2)}, u32[]{:S(2)}) collective-permute-start(f32[8,1,2048]{2,0,1:T(8,128)S(1)} %get-tuple-element.40), channel_id=1, source_target_pairs={{0,1},{1,2},{2,3},{3,4},{4,5},{5,6},{6,7},{7,8},{8,9},{9,10},{10,1... | collective-permute-start | bytes 196616 | tf_op jit(solution)/shard_map/ppermute | solution.py:22
  131.0 4.3 %collective-permute-done.11 = f32[8,1,2048]{2,0,1:T(8,128)S(1)} collective-permute-done((f32[8,1,2048]{2,0,1:T(8,128)S(1)}, f32[8,1,2048]{2,0,1:T(8,128)S(1)}, u32[]{:S(2)}, u32[]{:S(2)}) %collective-permute-start.11) | collective-permute-done | bytes 65568 | tf_op jit(solution)/shard_map/ppermute | solution.py:23
  136.4 4.0 %collective-permute-start.12 = (f32[8,1,2048]{2,0,1:T(8,128)S(1)}, f32[8,1,2048]{2,0,1:T(8,128)S(1)}, u32[]{:S(2)}, u32[]{:S(2)}) collective-permute-start(f32[8,1,2048]{2,0,1:T(8,128)S(1)} %get-tuple-element.38), channel_id=1, source_target_pairs={{0,1},{1,2},{2,3},{3,4},{4,5},{5,6},{6,7},{7,8},{8,9},{9,10},{10,1... | collective-permute-start | bytes 196616 | tf_op jit(solution)/shard_map/ppermute | solution.py:22
  142.3 4.3 %collective-permute-done.13 = f32[8,1,2048]{2,0,1:T(8,128)S(1)} collective-permute-done((f32[8,1,2048]{2,0,1:T(8,128)S(1)}, f32[8,1,2048]{2,0,1:T(8,128)S(1)}, u32[]{:S(2)}, u32[]{:S(2)}) %collective-permute-start.13) | collective-permute-done | bytes 65568 | tf_op jit(solution)/shard_map/ppermute | solution.py:23
  147.6 4.0 %collective-permute-start.14 = (f32[8,1,2048]{2,0,1:T(8,128)S(1)}, f32[8,1,2048]{2,0,1:T(8,128)S(1)}, u32[]{:S(2)}, u32[]{:S(2)}) collective-permute-start(f32[8,1,2048]{2,0,1:T(8,128)S(1)} %get-tuple-element.36), channel_id=1, source_target_pairs={{0,1},{1,2},{2,3},{3,4},{4,5},{5,6},{6,7},{7,8},{8,9},{9,10},{10,1... | collective-permute-start | bytes 196616 | tf_op jit(solution)/shard_map/ppermute | solution.py:22
  153.5 4.3 %collective-permute-done.15 = f32[8,1,2048]{2,0,1:T(8,128)S(1)} collective-permute-done((f32[8,1,2048]{2,0,1:T(8,128)S(1)}, f32[8,1,2048]{2,0,1:T(8,128)S(1)}, u32[]{:S(2)}, u32[]{:S(2)}) %collective-permute-start.15) | collective-permute-done | bytes 65568 | tf_op jit(solution)/shard_map/ppermute | solution.py:23
  158.9 4.0 %collective-permute-start.16 = (f32[8,1,2048]{2,0,1:T(8,128)S(1)}, f32[8,1,2048]{2,0,1:T(8,128)S(1)}, u32[]{:S(2)}, u32[]{:S(2)}) collective-permute-start(f32[8,1,2048]{2,0,1:T(8,128)S(1)} %get-tuple-element.34), channel_id=1, source_target_pairs={{0,1},{1,2},{2,3},{3,4},{4,5},{5,6},{6,7},{7,8},{8,9},{9,10},{10,1... | collective-permute-start | bytes 196616 | tf_op jit(solution)/shard_map/ppermute | solution.py:22
  164.8 4.3 %collective-permute-done.17 = f32[8,1,2048]{2,0,1:T(8,128)S(1)} collective-permute-done((f32[8,1,2048]{2,0,1:T(8,128)S(1)}, f32[8,1,2048]{2,0,1:T(8,128)S(1)}, u32[]{:S(2)}, u32[]{:S(2)}) %collective-permute-start.17) | collective-permute-done | bytes 65568 | tf_op jit(solution)/shard_map/ppermute | solution.py:23
  172.2 4.7 %collective-permute-start.19 = (f32[8,1,2048]{2,0,1:T(8,128)S(1)}, f32[8,1,2048]{2,0,1:T(8,128)S(1)}, u32[]{:S(2)}, u32[]{:S(2)}) collective-permute-start(f32[8,1,2048]{2,0,1:T(8,128)S(1)} %get-tuple-element.32), channel_id=1, source_target_pairs={{0,1},{1,2},{2,3},{3,4},{4,5},{5,6},{6,7},{7,8},{8,9},{9,10},{10,1... | collective-permute-start | bytes 196616 | tf_op jit(solution)/shard_map/ppermute | solution.py:22
  176.9 5.9 %copy.58 = f32[1,8,8,2048]{2,1,0,3:T(8,128)} copy(f32[1,8,8,2048]{3,1,2,0:T(8,128)} %bitcast.42) | data formatting | bytes 1048576 | tf_op jit(solution)/shard_map/broadcast_in_dim | solution.py:169
  182.8 7.4 %reshape.29 = f32[16,1,8192]{2,1,0:T(1,128)} reshape(f32[2048,1,8,8]{3,2,1,0:T(8,128)} %bitcast.38) | data formatting | bytes 1048576
  190.2 21.4 %all-to-all-start.2 = ((f32[16,1,8192]{2,1,0:T(1,128)}), f32[16,1,8192]{2,1,0:T(1,128)S(1)}, u32[]{:S(2)}, u32[]{:S(2)}) async-start(f32[16,1,8192]{2,1,0:T(1,128)} %reshape.29), calls=%async_computation.2 | async-start | bytes 1048576 | tf_op jit(solution)/shard_map/all_to_all | solution.py:130
  213.5 10.4 %all-to-all-done.2 = f32[16,1,8192]{2,1,0:T(1,128)S(1)} async-done(((f32[16,1,8192]{2,1,0:T(1,128)}), f32[16,1,8192]{2,1,0:T(1,128)S(1)}, u32[]{:S(2)}, u32[]{:S(2)}) %all-to-all-start.2) | async-done | bytes 524320 | tf_op jit(solution)/shard_map/all_to_all | solution.py:130
  226.4 6.7 %reshape.30 = f32[2048,1,8,8]{3,2,1,0:T(8,128)} reshape(f32[16,8192]{1,0:T(8,128)S(1)} %reduce) | data formatting | bytes 1048576
  233.0 6.0 %copy.59 = f32[1,8,16,8,128]{4,1,3,2,0:T(8,128)} copy(f32[1,8,16,8,128]{3,1,4,2,0:T(8,128)} %bitcast.37) | data formatting | bytes 1048576 | tf_op jit(solution)/shard_map/all_to_all | solution.py:130
  239.0 7.5 %all-to-all-start.3 = ((f32[1,8,128,128]{3,1,0,2:T(8,128)}), f32[1,8,128,128]{3,1,0,2:T(8,128)}, u32[]{:S(2)}, u32[]{:S(2)}) async-start(f32[1,8,128,128]{3,1,0,2:T(8,128)} %bitcast.14), calls=%async_computation.3 | async-start | bytes 1048576 | tf_op jit(solution)/shard_map/all_to_all | solution.py:129
  252.3 3.5 %all-to-all-done.3 = f32[1,8,128,128]{3,1,0,2:T(8,128)} async-done(((f32[1,8,128,128]{3,1,0,2:T(8,128)}), f32[1,8,128,128]{3,1,0,2:T(8,128)}, u32[]{:S(2)}, u32[]{:S(2)}) %all-to-all-start.3) | async-done | bytes 524320 | tf_op jit(solution)/shard_map/all_to_all | solution.py:129
  (88 shorter events, 46.3 us)
Async XLA Ops:
  30.8 6.9 %copy-start.9 = (f32[8,8,2048]{2,1,0:T(8,128)S(1)}, f32[8,8,2048]{2,1,0:T(8,128)}, u32[]{:S(2)}) copy-start(f32[8,8,2048]{2,1,0:T(8,128)} %param.5) | copy-start | bytes 1572868
  30.8 6.9 %copy-start.10 = (s32[8,8,2048]{2,1,0:T(8,128)S(1)}, s32[8,8,2048]{2,1,0:T(8,128)}, u32[]{:S(2)}) copy-start(s32[8,8,2048]{2,1,0:T(8,128)} %param.4) | copy-start | bytes 1572868
  30.8 30.6 %all-to-all-start.1 = ((f32[3,8,128,128]{3,1,0,2:T(8,128)}), f32[3,8,128,128]{3,1,0,2:T(8,128)S(1)}, u32[]{:S(2)}, u32[]{:S(2)}) async-start(f32[3,8,128,128]{3,1,0,2:T(8,128)} %all_to_all.46), calls=%async_computation.1 | async-start | bytes 3145728 | tf_op jit(solution)/shard_map/all_to_all | solution.py:141
  39.4 33.8 %copy-start.2 = (f32[1,8,8,2048]{3,1,2,0:T(8,128)}, f32[1,8,8,2048]{3,1,2,0:T(8,128)S(1)}, u32[]{:S(2)}) copy-start(f32[1,8,8,2048]{3,1,2,0:T(8,128)S(1)} %get-tuple-element.50) | copy-start | bytes 1572868
  61.6 7.5 %collective-permute-start = (f32[4,8,1,2048]{3,1,2,0:T(8,128)S(1)}, f32[4,8,1,2048]{3,1,2,0:T(8,128)S(1)}, u32[]{:S(2)}, u32[]{:S(2)}) collective-permute-start(f32[4,8,1,2048]{3,1,2,0:T(8,128)S(1)} %get-tuple-element.16), channel_id=1, source_target_pairs={{0,1},{1,2},{2,3},{3,4},{4,5},{5,6},{6,7},{7,8},{8,9},{9,10},{10,1... | collective-permute-start | bytes 786440 | tf_op jit(solution)/shard_map/ppermute | solution.py:22
  63.7 9.5 %collective-permute-start.1 = (f32[4,8,1,2048]{3,1,2,0:T(8,128)S(1)}, f32[4,8,1,2048]{3,1,2,0:T(8,128)S(1)}, u32[]{:S(2)}, u32[]{:S(2)}) collective-permute-start(f32[4,8,1,2048]{3,1,2,0:T(8,128)S(1)} %get-tuple-element.17), channel_id=1, source_target_pairs={{1,0},{2,1},{3,2},{4,3},{5,4},{6,5},{7,6},{8,7},{9,8},{10,9},{11,1... | collective-permute-start | bytes 786440 | tf_op jit(solution)/shard_map/ppermute | solution.py:23
  74.2 1.2 copy-start.5
  74.2 1.3 copy-start.6
  74.2 1.5 copy-start.7
  74.3 2.0 copy-start.8
  80.3 4.4 %collective-permute-start.2 = (f32[1,8,1,2048]{3,1,2,0:T(8,128)S(1)}, f32[1,8,1,2048]{3,1,2,0:T(8,128)S(1)}, u32[]{:S(2)}, u32[]{:S(2)}) collective-permute-start(f32[1,8,1,2048]{3,1,2,0:T(8,128)S(1)} %get-tuple-element.20), channel_id=1, source_target_pairs={{0,1},{1,2},{2,3},{3,4},{4,5},{5,6},{6,7},{7,8},{8,9},{9,10},{10,1... | collective-permute-start | bytes 196616 | tf_op jit(solution)/shard_map/ppermute | solution.py:22
  82.8 6.2 %collective-permute-start.3 = (f32[1,8,1,2048]{3,1,2,0:T(8,128)S(1)}, f32[1,8,1,2048]{3,1,2,0:T(8,128)S(1)}, u32[]{:S(2)}, u32[]{:S(2)}) collective-permute-start(f32[1,8,1,2048]{3,1,2,0:T(8,128)S(1)} %get-tuple-element.21), channel_id=1, source_target_pairs={{1,0},{2,1},{3,2},{4,3},{5,4},{6,5},{7,6},{8,7},{9,8},{10,9},{11,1... | collective-permute-start | bytes 196616 | tf_op jit(solution)/shard_map/ppermute | solution.py:23
  90.1 7.2 %collective-permute-start.4 = (f32[8,1,2048]{2,0,1:T(8,128)S(1)}, f32[8,1,2048]{2,0,1:T(8,128)S(1)}, u32[]{:S(2)}, u32[]{:S(2)}) collective-permute-start(f32[8,1,2048]{2,0,1:T(8,128)S(1)} %get-tuple-element.46), channel_id=1, source_target_pairs={{0,1},{1,2},{2,3},{3,4},{4,5},{5,6},{6,7},{7,8},{8,9},{9,10},{10,1... | collective-permute-start | bytes 196616 | tf_op jit(solution)/shard_map/ppermute | solution.py:22
  95.4 6.2 %collective-permute-start.5 = (f32[8,1,2048]{2,0,1:T(8,128)S(1)}, f32[8,1,2048]{2,0,1:T(8,128)S(1)}, u32[]{:S(2)}, u32[]{:S(2)}) collective-permute-start(f32[8,1,2048]{2,0,1:T(8,128)S(1)} %get-tuple-element.47), channel_id=1, source_target_pairs={{1,0},{2,1},{3,2},{4,3},{5,4},{6,5},{7,6},{8,7},{9,8},{10,9},{11,1... | collective-permute-start | bytes 196616 | tf_op jit(solution)/shard_map/ppermute | solution.py:23
  102.6 5.9 %collective-permute-start.6 = (f32[8,1,2048]{2,0,1:T(8,128)S(1)}, f32[8,1,2048]{2,0,1:T(8,128)S(1)}, u32[]{:S(2)}, u32[]{:S(2)}) collective-permute-start(f32[8,1,2048]{2,0,1:T(8,128)S(1)} %get-tuple-element.44), channel_id=1, source_target_pairs={{0,1},{1,2},{2,3},{3,4},{4,5},{5,6},{6,7},{7,8},{8,9},{9,10},{10,1... | collective-permute-start | bytes 196616 | tf_op jit(solution)/shard_map/ppermute | solution.py:22
  106.6 6.2 %collective-permute-start.7 = (f32[8,1,2048]{2,0,1:T(8,128)S(1)}, f32[8,1,2048]{2,0,1:T(8,128)S(1)}, u32[]{:S(2)}, u32[]{:S(2)}) collective-permute-start(f32[8,1,2048]{2,0,1:T(8,128)S(1)} %get-tuple-element.45), channel_id=1, source_target_pairs={{1,0},{2,1},{3,2},{4,3},{5,4},{6,5},{7,6},{8,7},{9,8},{10,9},{11,1... | collective-permute-start | bytes 196616 | tf_op jit(solution)/shard_map/ppermute | solution.py:23
  113.8 5.9 %collective-permute-start.8 = (f32[8,1,2048]{2,0,1:T(8,128)S(1)}, f32[8,1,2048]{2,0,1:T(8,128)S(1)}, u32[]{:S(2)}, u32[]{:S(2)}) collective-permute-start(f32[8,1,2048]{2,0,1:T(8,128)S(1)} %get-tuple-element.42), channel_id=1, source_target_pairs={{0,1},{1,2},{2,3},{3,4},{4,5},{5,6},{6,7},{7,8},{8,9},{9,10},{10,1... | collective-permute-start | bytes 196616 | tf_op jit(solution)/shard_map/ppermute | solution.py:22
  117.9 6.2 %collective-permute-start.9 = (f32[8,1,2048]{2,0,1:T(8,128)S(1)}, f32[8,1,2048]{2,0,1:T(8,128)S(1)}, u32[]{:S(2)}, u32[]{:S(2)}) collective-permute-start(f32[8,1,2048]{2,0,1:T(8,128)S(1)} %get-tuple-element.43), channel_id=1, source_target_pairs={{1,0},{2,1},{3,2},{4,3},{5,4},{6,5},{7,6},{8,7},{9,8},{10,9},{11,1... | collective-permute-start | bytes 196616 | tf_op jit(solution)/shard_map/ppermute | solution.py:23
  125.1 5.9 %collective-permute-start.10 = (f32[8,1,2048]{2,0,1:T(8,128)S(1)}, f32[8,1,2048]{2,0,1:T(8,128)S(1)}, u32[]{:S(2)}, u32[]{:S(2)}) collective-permute-start(f32[8,1,2048]{2,0,1:T(8,128)S(1)} %get-tuple-element.40), channel_id=1, source_target_pairs={{0,1},{1,2},{2,3},{3,4},{4,5},{5,6},{6,7},{7,8},{8,9},{9,10},{10,1... | collective-permute-start | bytes 196616 | tf_op jit(solution)/shard_map/ppermute | solution.py:22
  129.1 6.2 %collective-permute-start.11 = (f32[8,1,2048]{2,0,1:T(8,128)S(1)}, f32[8,1,2048]{2,0,1:T(8,128)S(1)}, u32[]{:S(2)}, u32[]{:S(2)}) collective-permute-start(f32[8,1,2048]{2,0,1:T(8,128)S(1)} %get-tuple-element.41), channel_id=1, source_target_pairs={{1,0},{2,1},{3,2},{4,3},{5,4},{6,5},{7,6},{8,7},{9,8},{10,9},{11,1... | collective-permute-start | bytes 196616 | tf_op jit(solution)/shard_map/ppermute | solution.py:23
  136.4 5.9 %collective-permute-start.12 = (f32[8,1,2048]{2,0,1:T(8,128)S(1)}, f32[8,1,2048]{2,0,1:T(8,128)S(1)}, u32[]{:S(2)}, u32[]{:S(2)}) collective-permute-start(f32[8,1,2048]{2,0,1:T(8,128)S(1)} %get-tuple-element.38), channel_id=1, source_target_pairs={{0,1},{1,2},{2,3},{3,4},{4,5},{5,6},{6,7},{7,8},{8,9},{9,10},{10,1... | collective-permute-start | bytes 196616 | tf_op jit(solution)/shard_map/ppermute | solution.py:22
  140.4 6.2 %collective-permute-start.13 = (f32[8,1,2048]{2,0,1:T(8,128)S(1)}, f32[8,1,2048]{2,0,1:T(8,128)S(1)}, u32[]{:S(2)}, u32[]{:S(2)}) collective-permute-start(f32[8,1,2048]{2,0,1:T(8,128)S(1)} %get-tuple-element.39), channel_id=1, source_target_pairs={{1,0},{2,1},{3,2},{4,3},{5,4},{6,5},{7,6},{8,7},{9,8},{10,9},{11,1... | collective-permute-start | bytes 196616 | tf_op jit(solution)/shard_map/ppermute | solution.py:23
  147.6 5.9 %collective-permute-start.14 = (f32[8,1,2048]{2,0,1:T(8,128)S(1)}, f32[8,1,2048]{2,0,1:T(8,128)S(1)}, u32[]{:S(2)}, u32[]{:S(2)}) collective-permute-start(f32[8,1,2048]{2,0,1:T(8,128)S(1)} %get-tuple-element.36), channel_id=1, source_target_pairs={{0,1},{1,2},{2,3},{3,4},{4,5},{5,6},{6,7},{7,8},{8,9},{9,10},{10,1... | collective-permute-start | bytes 196616 | tf_op jit(solution)/shard_map/ppermute | solution.py:22
  151.7 6.2 %collective-permute-start.15 = (f32[8,1,2048]{2,0,1:T(8,128)S(1)}, f32[8,1,2048]{2,0,1:T(8,128)S(1)}, u32[]{:S(2)}, u32[]{:S(2)}) collective-permute-start(f32[8,1,2048]{2,0,1:T(8,128)S(1)} %get-tuple-element.37), channel_id=1, source_target_pairs={{1,0},{2,1},{3,2},{4,3},{5,4},{6,5},{7,6},{8,7},{9,8},{10,9},{11,1... | collective-permute-start | bytes 196616 | tf_op jit(solution)/shard_map/ppermute | solution.py:23
  158.9 5.9 %collective-permute-start.16 = (f32[8,1,2048]{2,0,1:T(8,128)S(1)}, f32[8,1,2048]{2,0,1:T(8,128)S(1)}, u32[]{:S(2)}, u32[]{:S(2)}) collective-permute-start(f32[8,1,2048]{2,0,1:T(8,128)S(1)} %get-tuple-element.34), channel_id=1, source_target_pairs={{0,1},{1,2},{2,3},{3,4},{4,5},{5,6},{6,7},{7,8},{8,9},{9,10},{10,1... | collective-permute-start | bytes 196616 | tf_op jit(solution)/shard_map/ppermute | solution.py:22
  162.9 6.2 %collective-permute-start.17 = (f32[8,1,2048]{2,0,1:T(8,128)S(1)}, f32[8,1,2048]{2,0,1:T(8,128)S(1)}, u32[]{:S(2)}, u32[]{:S(2)}) collective-permute-start(f32[8,1,2048]{2,0,1:T(8,128)S(1)} %get-tuple-element.35), channel_id=1, source_target_pairs={{1,0},{2,1},{3,2},{4,3},{5,4},{6,5},{7,6},{8,7},{9,8},{10,9},{11,1... | collective-permute-start | bytes 196616 | tf_op jit(solution)/shard_map/ppermute | solution.py:23
  170.9 40.7 %collective-permute-start.18 = (f32[8,1,2048]{2,0,1:T(8,128)S(1)}, f32[8,1,2048]{2,0,1:T(8,128)S(1)}, u32[]{:S(2)}, u32[]{:S(2)}) collective-permute-start(f32[8,1,2048]{2,0,1:T(8,128)S(1)} %get-tuple-element.33), channel_id=1, source_target_pairs={{1,0},{2,1},{3,2},{4,3},{5,4},{6,5},{7,6},{8,7},{9,8},{10,9},{11,1... | collective-permute-start | bytes 196616 | tf_op jit(solution)/shard_map/ppermute | solution.py:23
  172.2 39.4 %collective-permute-start.19 = (f32[8,1,2048]{2,0,1:T(8,128)S(1)}, f32[8,1,2048]{2,0,1:T(8,128)S(1)}, u32[]{:S(2)}, u32[]{:S(2)}) collective-permute-start(f32[8,1,2048]{2,0,1:T(8,128)S(1)} %get-tuple-element.32), channel_id=1, source_target_pairs={{0,1},{1,2},{2,3},{3,4},{4,5},{5,6},{6,7},{7,8},{8,9},{9,10},{10,1... | collective-permute-start | bytes 196616 | tf_op jit(solution)/shard_map/ppermute | solution.py:22
  182.8 28.8 %copy-start.1 = (f32[8,8,2048]{2,0,1:T(8,128)S(1)}, f32[8,8,2048]{2,0,1:T(8,128)}, u32[]{:S(2)}) copy-start(f32[8,8,2048]{2,0,1:T(8,128)} %copy-done) | copy-start | bytes 1572868
  190.2 33.8 %all-to-all-start.2 = ((f32[16,1,8192]{2,1,0:T(1,128)}), f32[16,1,8192]{2,1,0:T(1,128)S(1)}, u32[]{:S(2)}, u32[]{:S(2)}) async-start(f32[16,1,8192]{2,1,0:T(1,128)} %reshape.29), calls=%async_computation.2 | async-start | bytes 1048576 | tf_op jit(solution)/shard_map/all_to_all | solution.py:130
  233.0 13.5 %copy-start.4 = (f32[3,8,8,2048]{3,1,2,0:T(8,128)S(1)}, f32[3,8,8,2048]{3,1,2,0:T(8,128)}, u32[]{:S(2)}) copy-start(f32[3,8,8,2048]{3,1,2,0:T(8,128)} %get-tuple-element.15) | copy-start | bytes 4718596
  239.0 16.8 %all-to-all-start.3 = ((f32[1,8,128,128]{3,1,0,2:T(8,128)}), f32[1,8,128,128]{3,1,0,2:T(8,128)}, u32[]{:S(2)}, u32[]{:S(2)}) async-start(f32[1,8,128,128]{3,1,0,2:T(8,128)} %bitcast.14), calls=%async_computation.3 | async-start | bytes 1048576 | tf_op jit(solution)/shard_map/all_to_all | solution.py:129
  (2 other events, 1.8 us)
where the time goes:
time: 259 us; the launch traced here: 258 us
  starting transfers between devices  87.6 us (34%)
  waiting for transfers between devices  82.4 us (32%)
  local copies, waits for them, and re-layouts  37.9 us (15%)
  blocking collectives  27.7 us (11%)
  other arithmetic  21.1 us (8%)
    ppermute x10, starting transfers between devices, padded_2(): lax.ppermute(last, axis, up)  38.7 us
    ppermute x10, waiting for transfers between devices, padded_2(): lax.ppermute(first, axis, [(b, a) for a, b in up])  38.3 us
    all_to_all x1, blocking collectives, to_particles(): lax.all_to_all(ordered, 'gy', split_axis=2, concat_axis=2, tiled=True)  27.7 us
    all_to_all x1, waiting for transfers between devices, to_particles(): lax.all_to_all(lax.all_to_all(ordered, 'gy', split_axis=2, concat_axis=2,...  22 us
    all_to_all x1, starting transfers between devices, to_fluid(): lax.all_to_all(fields, 'gx', split_axis=3, concat_axis=2, tiled=True)  21.4 us
    unnamed x26, local copies, waits for them, and re-layouts  20.1 us
    ppermute x10, starting transfers between devices, padded_2(): lax.ppermute(first, axis, [(b, a) for a, b in up])  13.1 us
    all_to_all x1, waiting for transfers between devices, to_fluid(): lax.all_to_all(fields, 'gx', split_axis=3, concat_axis=2, tiled=True)  10.4 us
  transfers between devices with their start and end apart: 23, of which 21 were waited for; matrix products, arithmetic and copies ran while one was open for 9% of the time, Pallas kernels for 0%

commit v1 on v0

v1 whole, which is shorter than its diff:
```python
import functools

import jax
import jax.numpy as jnp
from jax import lax
from jax.experimental import pallas as pl
from jax.experimental.pallas import tpu as pltpu
from jax.sharding import PartitionSpec as P

SWEEPS = 8

particle_volume = 0.05
time_step = 0.5
viscosity = 0.1

ROWS = 8
PLANES = 8
GROUPS = 16
LANES = 128
TILE = (PLANES, LANES)
WIDE = 3 * ROWS
AXES = ("gx", "gy")
f32 = jnp.float32


def place():
    return lax.axis_index("gx") * lax.axis_size("gy") + lax.axis_index("gy")


def lane_ids():
    return lax.broadcasted_iota(jnp.int32, TILE, 1)


def plane_ids():
    return lax.broadcasted_iota(jnp.int32, TILE, 0)


def plane_up(tile):
    return pltpu.roll(tile, PLANES - 1, 0)


def plane_down(tile):
    return pltpu.roll(tile, 1, 0)


def column_neighbours(tiles):
    lanes = lane_ids()
    last, first = lanes == LANES - 1, lanes == 0
    ahead = [pltpu.roll(tile, LANES - 1, 1) for tile in tiles]
    behind = [pltpu.roll(tile, 1, 1) for tile in tiles]
    n = len(tiles)
    up = [jnp.where(last, ahead[g + 1], ahead[g]) if g < n - 1 else ahead[g] for g in range(n)]
    down = [jnp.where(first, behind[g - 1], behind[g]) if g > 0 else behind[g] for g in range(n)]
    return up, down


def no_column_up(g, tile):
    return jnp.where(lane_ids() == LANES - 1, 0.0, tile) if g == GROUPS - 1 else tile


def no_column_down(g, tile):
    return jnp.where(lane_ids() == 0, 0.0, tile) if g == 0 else tile


def weighted_sum(weights, row, g, tile, up, down, row_up, row_down):
    total = weights[row, 0, g] * plane_up(tile) + weights[row, 1, g] * plane_down(tile)
    total = total + (weights[row, 2, g] * row_up + weights[row, 3, g] * row_down)
    return total + (weights[row, 4, g] * up + weights[row, 5, g] * down)


def particle_kernel(count, drag, velocity, voids, drag_out, force, first_message, second_message):
    even = lax.rem(lax.axis_index("gy"), 2) == 0
    first_row = jnp.where(even, ROWS - 1, 0)
    second_row = ROWS - 1 - first_row
    for g in range(GROUPS):
        columns = pl.ds(g * LANES, LANES)
        void = jnp.swapaxes(1.0 - count[:, :, columns].astype(f32) * particle_volume, 0, 1)
        voids[:, g] = void
        first_message[0:ROWS, g] = void
        second_message[0:ROWS, g] = void
        drags = drag[:, :, columns]
        drag_out[:, g] = jnp.swapaxes(drags, 0, 1)
        for k in range(3):
            force[k, :, g] = jnp.swapaxes(time_step * drags * velocity[k, :, :, columns], 0, 1)
    for message, row in ((first_message, first_row), (second_message, second_row)):
        message[ROWS] = drag_out[row]
        message[ROWS + 1] = force[0, row]


def coefficient_kernel(
    voids, drag, force, first, second, weights, inverse_sum, centre, spread, given, voids_near, voids_wide
):
    device = place()
    even = lax.rem(lax.axis_index("gy"), 2) == 0
    devices = lax.axis_size("gx") * lax.axis_size("gy")
    low_there = (device > 0).astype(f32)
    high_there = (device < devices - 1).astype(f32)
    first_at = jnp.where(even, 2 * ROWS, 0)
    second_at = 2 * ROWS - first_at
    first_there = jnp.where(even, high_there, low_there)
    second_there = jnp.where(even, low_there, high_there)

    @pl.loop(0, ROWS)
    def _(row):
        voids_wide[first_at + row] = first[row] * first_there
        voids_wide[second_at + row] = second[row] * second_there
        voids_wide[ROWS + row] = voids[row]

    planes = plane_ids()

    def row_weights(row):
        tiles = [voids_wide[row, g] for g in range(GROUPS)]
        ups, downs = column_neighbours(tiles)
        for g in range(GROUPS):
            tile = tiles[g]
            near = [
                jnp.where(planes == PLANES - 1, 0.0, plane_up(tile)),
                jnp.where(planes == 0, 0.0, plane_down(tile)),
                voids_wide[row + 1, g],
                voids_wide[row - 1, g],
                no_column_up(g, ups[g]),
                no_column_down(g, downs[g]),
            ]
            faces = [0.5 * (tile + other) for other in near]
            total = faces[0]
            for face in faces[1:]:
                total = total + face
            inverse = jnp.where(tile > 0.0, 1.0 / total, 0.0)
            scaled = [face * inverse for face in faces]
            scaled[0] = jnp.where(planes == PLANES - 1, 0.0, scaled[0])
            scaled[1] = jnp.where(planes == 0, 0.0, scaled[1])
            scaled[4] = no_column_up(g, scaled[4])
            scaled[5] = no_column_down(g, scaled[5])
            for n in range(6):
                weights[row - 1, n, g] = scaled[n]
            yield g, tile, total, inverse

    @pl.loop(1, ROWS - 1)
    def _(row):
        for _ in row_weights(row):
            pass

    @pl.loop(2 * ROWS + 1, WIDE - 1)
    def _(row):
        for _ in row_weights(row):
            pass

    def momentum_row(row, drag_at, force_at):
        for g, tile, total, inverse in row_weights(row):
            scale = 1.0 / (tile + time_step * drag_at(g))
            near = row - (ROWS - 1)
            voids_near[near, g] = tile
            centre[near, g] = (tile - time_step * viscosity * total) * scale
            spread[near, g] = (time_step * viscosity * total) * scale
            for k, value in enumerate(force_at(g)):
                given[k, near, g] = value * scale
            yield g, inverse

    @pl.loop(0, ROWS)
    def _(row):
        for g, inverse in momentum_row(
            row + ROWS, lambda g: drag[row, g], lambda g: [force[k, row, g] for k in range(3)]
        ):
            inverse_sum[row, g] = inverse

    for message, at in ((first, first_at), (second, second_at)):
        row = jnp.where(at == 0, ROWS - 1, 2 * ROWS)
        for _ in momentum_row(row, lambda g: message[ROWS, g], lambda g: [message[ROWS + 1, g]]):
            pass


def edge_kernel(velocity, first, second):
    even = lax.rem(lax.axis_index("gy"), 2) == 0
    first_row = jnp.where(even, ROWS - 2, 0)
    for message, pair, single in (
        (first, first_row, jnp.where(even, ROWS - 1, 0)),
        (second, ROWS - 2 - first_row, jnp.where(even, 0, ROWS - 1)),
    ):
        for g in range(GROUPS):
            message[0, g] = velocity[g, 0, pair]
            message[1, g] = velocity[g, 0, pair + 1]
            message[2, g] = velocity[g, 1, single]
            message[3, g] = velocity[g, 2, single]


def momentum_kernel(
    velocity, first, second, weights, inverse_sum, centre, spread, given, voids_near, predicted, source, wide, flux
):
    device = place()
    even = lax.rem(lax.axis_index("gy"), 2) == 0
    devices = lax.axis_size("gx") * lax.axis_size("gy")
    low_there = (device > 0).astype(f32)
    high_there = (device < devices - 1).astype(f32)
    for message, is_high in ((first, even), (second, jnp.logical_not(even))):
        there = jnp.where(is_high, high_there, low_there)
        pair = jnp.where(is_high, ROWS + 2, 0)
        single = jnp.where(is_high, ROWS + 2, 1)
        for g in range(GROUPS):
            wide[0, pair, g] = message[0, g] * there
            wide[0, pair + 1, g] = message[1, g] * there
            wide[1, single, g] = message[2, g] * there
            wide[2, single, g] = message[3, g] * there

    @pl.loop(0, ROWS)
    def _(row):
        for g in range(GROUPS):
            for k in range(3):
                wide[k, row + 2, g] = velocity[g, k, row]

    planes = plane_ids()

    def predict(k, near):
        tiles = [wide[k, near + 1, g] for g in range(GROUPS)]
        ups, downs = column_neighbours(tiles)
        for g in range(GROUPS):
            around = weighted_sum(
                weights, near + (ROWS - 2), g, tiles[g], ups[g], downs[g], wide[k, near + 2, g], wide[k, near, g]
            )
            yield centre[near, g] * tiles[g] + spread[near, g] * around + given[k, near, g]

    @pl.loop(0, ROWS + 2)
    def _(near):
        for g, value in enumerate(predict(0, near)):
            flux[near, g] = voids_near[near, g] * value
            wide[0, near, g] = value

    @pl.loop(0, ROWS)
    def _(row):
        near = row + 1
        second_flux = []
        for g, value in enumerate(predict(1, near)):
            predicted[1, row, g] = value
            second_flux.append(voids_near[near, g] * value)
        ups, downs = column_neighbours(second_flux)
        for g, value in enumerate(predict(2, near)):
            predicted[2, row, g] = value
            predicted[0, row, g] = wide[0, near, g]
            third_flux = voids_near[near, g] * value
            change = flux[near + 1, g] - flux[near - 1, g]
            change = change + (no_column_up(g, ups[g]) - no_column_down(g, downs[g]))
            change = change + (
                jnp.where(planes == PLANES - 1, 0.0, plane_up(third_flux))
                - jnp.where(planes == 0, 0.0, plane_down(third_flux))
            )
            source[row, g] = change * inverse_sum[row, g]


def sweep_kernel(source, first, second, weights, pressure, near_pressure, source_wide, one, other):
    device = place()
    even = lax.rem(lax.axis_index("gy"), 2) == 0
    devices = lax.axis_size("gx") * lax.axis_size("gy")
    low_there = (device > 0).astype(f32)
    high_there = (device < devices - 1).astype(f32)
    first_at = jnp.where(even, 2 * ROWS, 0)
    second_at = 2 * ROWS - first_at
    first_there = jnp.where(even, high_there, low_there)
    second_there = jnp.where(even, low_there, high_there)

    @pl.loop(0, ROWS)
    def _(row):
        for at, value in (
            (first_at + row, first[row] * first_there),
            (second_at + row, second[row] * second_there),
            (ROWS + row, source[row]),
        ):
            source_wide[at] = value
            one[at] = -value

    now, later = one, other
    for sweep in range(1, SWEEPS):

        def sweep_row(row, now=now, later=later):
            tiles = [now[row, g] for g in range(GROUPS)]
            ups, downs = column_neighbours(tiles)
            for g in range(GROUPS):
                around = weighted_sum(
                    weights, row - 1, g, tiles[g], ups[g], downs[g], now[row + 1, g], now[row - 1, g]
                )
                later[row, g] = around - source_wide[row, g]

        pl.loop(sweep, WIDE - sweep)(sweep_row)
        now, later = later, now

    @pl.loop(0, ROWS)
    def _(row):
        for g in range(GROUPS):
            pressure[g, row] = now[row + ROWS, g]

    @pl.loop(0, ROWS + 2)
    def _(row):
        near_pressure[row] = now[row + ROWS - 1]


def correct_kernel(near_pressure, predicted, velocity, slopes):
    planes = plane_ids()
    held = [[[None] * ROWS for _ in range(GROUPS)] for _ in range(3)]
    for row in range(ROWS):
        tiles = [near_pressure[row + 1, g] for g in range(GROUPS)]
        ups, downs = column_neighbours(tiles)
        for g in range(GROUPS):
            tile = tiles[g]
            held[0][g][row] = 0.5 * (near_pressure[row + 2, g] - near_pressure[row, g])
            held[1][g][row] = 0.5 * (no_column_up(g, ups[g]) - no_column_down(g, downs[g]))
            held[2][g][row] = 0.5 * (
                jnp.where(planes == PLANES - 1, 0.0, plane_up(tile)) - jnp.where(planes == 0, 0.0, plane_down(tile))
            )
    for g in range(GROUPS):
        columns = pl.ds(g * LANES, LANES)
        for k in range(3):
            slope = jnp.stack(held[k][g])
            slopes[k, :, :, columns] = jnp.swapaxes(slope, 0, 1)
            velocity[k, :, :, columns] = jnp.swapaxes(predicted[k, :, g] - time_step * slope, 0, 1)


def call(kernel, args, outs, scratch=(), flops=0):
    vmem = pl.BlockSpec(memory_space=pltpu.VMEM)
    shapes = [jax.ShapeDtypeStruct(shape, f32) for shape in outs]
    moved = sum(arg.size for arg in args) * 4 + sum(shape.size for shape in shapes) * 4
    return pl.pallas_call(
        kernel,
        out_shape=shapes,
        in_specs=[vmem] * len(args),
        out_specs=[vmem] * len(outs),
        scratch_shapes=[pltpu.VMEM(shape, f32) for shape in scratch],
        cost_estimate=pl.CostEstimate(flops=flops, bytes_accessed=moved, transcendentals=0),
        compiler_params=pltpu.CompilerParams(vmem_limit_bytes=40 * 1024 * 1024),
        name=kernel.__name__,
    )(*args)


def swap(first, second):
    devices = lax.axis_size("gx") * lax.axis_size("gy")
    inner = [(d, d ^ 1) for d in range(devices)]
    outer = [(d, (((d + 1) % devices) ^ 1) - 1) for d in range(devices)]
    outer = [(a, b % devices) for a, b in outer]
    return lax.ppermute(first, AXES, inner), lax.ppermute(second, AXES, outer)


def shards(particle_count, drag_coeff, particle_velocity, fluid_velocity):
    along, across = lax.axis_size("gy"), lax.axis_size("gx")
    field = (GROUPS, PLANES, LANES)
    own = (ROWS,) + field
    near = (ROWS + 2,) + field

    voids, drag, force, first, second = call(
        particle_kernel,
        (particle_count, drag_coeff, particle_velocity),
        [own, own, (3,) + own, near, near],
    )

    blocks = fluid_velocity.reshape(3, PLANES, across // along, along, ROWS, LANES)
    blocks = blocks.transpose(3, 2, 0, 4, 1, 5)
    blocks = lax.all_to_all(blocks, "gy", split_axis=0, concat_axis=0, tiled=True)
    blocks = blocks.reshape(across, 3, ROWS, PLANES, LANES)
    blocks, first, second = lax.optimization_barrier((blocks, first, second))
    first, second = swap(first, second)
    slab = lax.all_to_all(blocks, "gx", split_axis=0, concat_axis=0, tiled=True)

    weights, inverse_sum, centre, spread, given, voids_near = call(
        coefficient_kernel,
        (voids, drag, force, first, second),
        [(WIDE - 2, 6) + field, own, near, near, (3,) + near, near],
        [(WIDE,) + field],
    )

    edges = call(edge_kernel, (slab,), [(4,) + field] * 2)
    first, second = swap(*edges)
    predicted, source = call(
        momentum_kernel,
        (slab, first, second, weights, inverse_sum, centre, spread, given, voids_near),
        [(3,) + own, own],
        [(3, ROWS + 4) + field, near],
    )
    first, second = swap(source, source)
    pressure, near_pressure = call(
        sweep_kernel,
        (source, first, second, weights),
        [(GROUPS, ROWS, PLANES, LANES), near],
        [(WIDE,) + field] * 3,
    )

    velocity, slopes = call(
        correct_kernel, (near_pressure, predicted), [(3, PLANES, ROWS, GROUPS * LANES)] * 2
    )

    pressure = lax.all_to_all(pressure, "gx", split_axis=0, concat_axis=0, tiled=True)
    pressure = lax.all_to_all(pressure, "gy", split_axis=0, concat_axis=0, tiled=True)
    pressure = pressure.reshape(along, across // along, ROWS, PLANES, LANES)
    pressure = pressure.transpose(3, 1, 0, 2, 4).reshape(PLANES, across * ROWS, LANES)
    return (pressure, velocity, slopes)


def solution(mesh):
    placed = (
        P(None, ("gx", "gy"), None),
        P(None, ("gx", "gy"), None),
        P(None, None, ("gx", "gy"), None),
        P(None, None, "gy", "gx"),
    )
    return jax.shard_map(
        shards,
        mesh=mesh,
        in_specs=placed,
        out_specs=(
            P(None, "gy", "gx"),
            P(None, None, ("gx", "gy"), None),
            P(None, None, ("gx", "gy"), None),
        ),
        check_vma=False,
    )
```

time: 259 us -> 149 us (0.58)
  starting transfers between devices: 87.6 us -> 26.3 us
  Pallas kernels: 0 us -> 30.1 us
  local copies, waits for them, and re-layouts: 37.9 us -> 9.72 us
  other arithmetic: 21.1 us -> 0 us
  waiting for transfers between devices: 82.4 us -> 63.3 us
  blocking collectives: 27.7 us -> 18.3 us
    ppermute x20 -> x6, starting transfers between devices: 51.8 us -> 7.91 us  [swap(): return (lax.ppermute(first, AXES, inner), lax.ppermute(second, AXES, outer))]
    pallas_call x0 -> x6, Pallas kernels: none -> 30.1 us  [call(): pl.pallas_call(kernel, out_shape=shapes, in_specs=[vmem] * len(args), out...]
    ppermute x20 -> x6, waiting for transfers between devices: 46.5 us -> 24.4 us  [swap(): return (lax.ppermute(first, AXES, inner), lax.ppermute(second, AXES, outer))]
    all_to_all x3, starting transfers between devices: 35.8 us -> 18.4 us  [the longest x1 6.74 us: shards(): slab = lax.all_to_all(blocks, 'gx', split_axis=0, concat_axis=0, tiled=True)]
    unnamed x26 -> x20, local copies, waits for them, and re-layouts: 20.1 us -> 5.36 us
    all_to_all x1, blocking collectives: 27.7 us -> 18.3 us  [shards(): lax.all_to_all(pressure, 'gx', split_axis=0, concat_axis=0, tiled=True)]
    all_to_all x4 -> x0, local copies, waits for them, and re-layouts: 7.79 us -> none  [the longest x2 6.48 us: to_fluid(): lax.all_to_all(fields, 'gx', split_axis=3, concat_axis=2, tiled=True)]
    div x8 -> x0, other arithmetic: 6.34 us -> none  [the longest x7 5.53 us: jacobi_sweep(): return (total - source) / weight_sum]
  transfers between devices with their start and end apart: 23 -> 9, of which waited for: 21 -> 6; matrix products, arithmetic and copies ran while one was open for 9% -> 0% of each run, Pallas kernels for 0% -> 8%
where the time goes in v1:
time: 149 us; the launch traced here: 148 us
  waiting for transfers between devices  63.3 us (42%)
  Pallas kernels  30.1 us (20%)
  starting transfers between devices  26.3 us (18%)
  blocking collectives  18.3 us (12%)
  local copies, waits for them, and re-layouts  9.72 us (7%)
    pallas_call x6, Pallas kernels, call(): pl.pallas_call(kernel, out_shape=shapes, in_specs=[vmem] * len(args), out...  30.1 us
    ppermute x6, waiting for transfers between devices, swap(): return (lax.ppermute(first, AXES, inner), lax.ppermute(second, AXES, outer))  24.4 us
    all_to_all x1, blocking collectives, shards(): lax.all_to_all(pressure, 'gx', split_axis=0, concat_axis=0, tiled=True)  18.3 us
    all_to_all x1, waiting for transfers between devices, shards(): slab = lax.all_to_all(blocks, 'gx', split_axis=0, concat_axis=0, tiled=True)  17.8 us
    all_to_all x1, waiting for transfers between devices, shards(): lax.all_to_all(blocks, 'gy', split_axis=0, concat_axis=0, tiled=True)  14.4 us
    ppermute x6, starting transfers between devices, swap(): return (lax.ppermute(first, AXES, inner), lax.ppermute(second, AXES, outer))  7.91 us
    all_to_all x1, starting transfers between devices, shards(): slab = lax.all_to_all(blocks, 'gx', split_axis=0, concat_axis=0, tiled=True)  6.74 us
    all_to_all x1, waiting for transfers between devices, shards(): lax.all_to_all(pressure, 'gy', split_axis=0, concat_axis=0, tiled=True)  6.58 us
  transfers between devices with their start and end apart: 9, of which 6 were waited for; matrix products, arithmetic and copies ran while one was open for 0% of the time, Pallas kernels for 8%

profile of v1, /device:TPU:0, one launch (start us, length us, event | category | flops | bytes accessed | tf_op | source)
XLA Modules:
  0.0 148.5 jit_solution(6692187063454681519)
XLA Ops:
  0.6 3.5 %copy.10 = f32[3,8,2,8,8,128]{5,1,4,0,2,3:T(8,128)} copy(f32[3,8,2,8,8,128]{5,4,3,2,1,0:T(8,128)} %bitcast.10) | data formatting | bytes 3145728 | tf_op jit(solution)/shard_map/reshape | solution.py:351
  4.1 6.5 %all-to-all-start = ((f32[8,2,3,8,8,128]{5,4,3,2,1,0:T(8,128)}), f32[8,2,3,8,8,128]{5,4,3,2,1,0:T(8,128)}, u32[]{:S(2)}, u32[]{:S(2)}) async-start(f32[8,2,3,8,8,128]{5,4,3,2,1,0:T(8,128)} %bitcast.8), calls=%async_computation | async-start | bytes 3145728 | tf_op jit(solution)/shard_map/all_to_all | solution.py:353
  10.6 0.0 copy-start.2
  10.6 1.0 copy-done.2
  11.6 1.0 copy-done.3
  12.6 0.7 particle_kernel.1
  13.4 0.0 copy-start.4
  13.4 0.8 copy-done.4
  14.2 0.8 copy-done.6
  15.0 0.8 copy-done.8
  15.8 0.8 copy-done.9
  16.6 14.4 %all-to-all-done = f32[8,2,3,8,8,128]{5,4,3,2,1,0:T(8,128)} async-done(((f32[8,2,3,8,8,128]{5,4,3,2,1,0:T(8,128)}), f32[8,2,3,8,8,128]{5,4,3,2,1,0:T(8,128)}, u32[]{:S(2)}, u32[]{:S(2)}) %all-to-all-start) | async-done | bytes 1572896 | tf_op jit(solution)/shard_map/all_to_all | solution.py:353
  31.1 6.7 %all-to-all-start.1 = ((f32[16,3,8,8,128]{4,3,2,1,0:T(8,128)}), f32[16,3,8,8,128]{4,3,2,1,0:T(8,128)S(1)}, u32[]{:S(2)}, u32[]{:S(2)}) async-start(f32[16,3,8,8,128]{4,3,2,1,0:T(8,128)} %bitcast.2), calls=%async_computation.1 | async-start | bytes 3145728 | tf_op jit(solution)/shard_map/all_to_all | solution.py:357
  37.8 0.9 collective-permute-start.2
  38.8 5.4 %collective-permute-start.3 = (f32[10,16,8,128]{3,2,1,0:T(8,128)}, f32[10,16,8,128]{3,2,1,0:T(8,128)}, u32[]{:S(2)}, u32[]{:S(2)}) collective-permute-start(f32[10,16,8,128]{3,2,1,0:T(8,128)} %copy-done.8), channel_id=1, source_target_pairs={{0,127},{1,2},{2,1},{3,4},{4,3},{5,6},{6,5},{7,8},{8,7},{9,10},{10... | collective-permute-start | bytes 1966088 | tf_op jit(solution)/shard_map/ppermute | solution.py:336
  44.1 17.8 %all-to-all-done.1.velocity = f32[16,3,8,8,128]{4,3,2,1,0:T(8,128)S(1)} async-done(((f32[16,3,8,8,128]{4,3,2,1,0:T(8,128)}), f32[16,3,8,8,128]{4,3,2,1,0:T(8,128)S(1)}, u32[]{:S(2)}, u32[]{:S(2)}) %all-to-all-start.1) | async-done | bytes 1572896 | tf_op jit(solution)/shard_map/all_to_all | solution.py:357
  61.9 0.1 edge_kernel.1
  62.0 0.5 collective-permute-start
  62.5 0.3 collective-permute-start.1
  62.8 11.0 %collective-permute-done.3.second = f32[10,16,8,128]{3,2,1,0:T(8,128)} collective-permute-done((f32[10,16,8,128]{3,2,1,0:T(8,128)}, f32[10,16,8,128]{3,2,1,0:T(8,128)}, u32[]{:S(2)}, u32[]{:S(2)}) %collective-permute-start.3) | collective-permute-done | bytes 655392 | tf_op jit(solution)/shard_map/ppermute | solution.py:336
  73.9 7.8 %coefficient_kernel.1 = (f32[22,6,16,8,128]{4,3,2,1,0:T(8,128)}, f32[8,16,8,128]{3,2,1,0:T(8,128)S(1)}, f32[10,16,8,128]{3,2,1,0:T(8,128)S(1)}, f32[10,16,8,128]...) custom-call(f32[8,16,8,128]{3,2,1,0:T(8,128)S(1)} %copy-done.5, ...), custom_call_target="tpu_custom_call" | custom-call | bytes 17039360 | tf_op jit(solution)/shard_map/coefficient_kernel/pallas_call | solution.py:319
  81.7 6.7 %momentum_kernel.1 = (f32[3,8,16,8,128]{4,3,2,1,0:T(8,128)S(1)}, f32[8,16,8,128]{3,2,1,0:T(8,128)S(1)}) custom-call(f32[16,3,8,8,128]{4,3,2,1,0:T(8,128)S(1)} %all-to-all-done.1.velocity, f32[4,16,8,128]{3,2,1,0:T(8,128)S(1)} %collective-permute-done.first, f32[4,16,8,128]{3,2,1,0:T(8,128)S(1)} %collective-permute-done.1.second, ...), custom_call_target="tpu_custom_call" | custom-call | bytes 17301504 | tf_op jit(solution)/shard_map/momentum_kernel/pallas_call | solution.py:319
  88.4 0.1 collective-permute-start.4
  88.5 0.7 collective-permute-start.5
  89.2 8.5 %collective-permute-done.4.first = f32[8,16,8,128]{3,2,1,0:T(8,128)S(1)} collective-permute-done((f32[8,16,8,128]{3,2,1,0:T(8,128)S(1)}, f32[8,16,8,128]{3,2,1,0:T(8,128)S(1)}, u32[]{:S(2)}, u32[]{:S(2)}) %collective-permute-start.4) | collective-permute-done | bytes 524320 | tf_op jit(solution)/shard_map/ppermute | solution.py:336
  97.6 4.9 %collective-permute-done.5.second = f32[8,16,8,128]{3,2,1,0:T(8,128)S(1)} collective-permute-done((f32[8,16,8,128]{3,2,1,0:T(8,128)S(1)}, f32[8,16,8,128]{3,2,1,0:T(8,128)S(1)}, u32[]{:S(2)}, u32[]{:S(2)}) %collective-permute-start.5) | collective-permute-done | bytes 524320 | tf_op jit(solution)/shard_map/ppermute | solution.py:336
  102.6 12.3 %sweep_kernel.1 = (f32[16,8,8,128]{3,2,1,0:T(8,128)S(1)}, f32[10,16,8,128]{3,2,1,0:T(8,128)S(1)}) custom-call(f32[8,16,8,128]{3,2,1,0:T(8,128)S(1)} %get-tuple-element.41.source, f32[8,16,8,128]{3,2,1,0:T(8,128)S(1)} %collective-permute-done.4.first, f32[8,16,8,128]{3,2,1,0:T(8,128)S(1)} %collective-permute-done.5.second, f32[22,6,16,8,128]{4,3,2,1,0:T(8,128)S(1)} %copy-done), custom_call_target="tpu_custom_call" | custom-call | bytes 11403264 | tf_op jit(solution)/shard_map/sweep_kernel/pallas_call | solution.py:319
  114.9 18.3 %all_to_all.20 = f32[16,8,8,128]{3,2,1,0:T(8,128)} all-to-all(f32[16,8,8,128]{3,2,1,0:T(8,128)S(1)} %get-tuple-element.42), channel_id=1, replica_groups=mesh['gx'=16,'gy'=8] {'gx'}, dimensions={0} | all-to-all | bytes 1048576 | tf_op jit(solution)/shard_map/all_to_all | solution.py:386
  133.2 5.2 %all-to-all-start.3 = ((f32[16,8,8,128]{3,2,1,0:T(8,128)}), f32[16,8,8,128]{3,2,1,0:T(8,128)S(1)}, u32[]{:S(2)}, u32[]{:S(2)}) async-start(f32[16,8,8,128]{3,2,1,0:T(8,128)} %all_to_all.20), calls=%async_computation.3 | async-start | bytes 1048576 | tf_op jit(solution)/shard_map/all_to_all | solution.py:387
  138.4 2.6 %correct_kernel.1 = (f32[3,8,8,2048]{3,2,1,0:T(8,128)}, f32[3,8,8,2048]{3,2,1,0:T(8,128)}) custom-call(f32[10,16,8,128]{3,2,1,0:T(8,128)S(1)} %get-tuple-element.43.near_pressure, f32[3,8,16,8,128]{4,3,2,1,0:T(8,128)S(1)} %get-tuple-element.44.predicted), custom_call_target="tpu_custom_call" | custom-call | bytes 5373952 | tf_op jit(solution)/shard_map/correct_kernel/pallas_call | solution.py:319
  141.0 6.6 %all-to-all-done.3 = f32[16,8,8,128]{3,2,1,0:T(8,128)S(1)} async-done(((f32[16,8,8,128]{3,2,1,0:T(8,128)}), f32[16,8,8,128]{3,2,1,0:T(8,128)S(1)}, u32[]{:S(2)}, u32[]{:S(2)}) %all-to-all-start.3) | async-done | bytes 524320 | tf_op jit(solution)/shard_map/all_to_all | solution.py:387
  147.6 0.9 copy.8
  (15 shorter events, 0.0 us)
Async XLA Ops:
  4.1 6.5 %copy-start.1 = (f32[3,8,8,2048]{3,2,1,0:T(8,128)S(1)}, f32[3,8,8,2048]{3,2,1,0:T(8,128)}, u32[]{:S(2)}) copy-start(f32[3,8,8,2048]{3,2,1,0:T(8,128)} %velocity.1) | copy-start | bytes 4718596
  4.1 27.0 %all-to-all-start = ((f32[8,2,3,8,8,128]{5,4,3,2,1,0:T(8,128)}), f32[8,2,3,8,8,128]{5,4,3,2,1,0:T(8,128)}, u32[]{:S(2)}, u32[]{:S(2)}) async-start(f32[8,2,3,8,8,128]{5,4,3,2,1,0:T(8,128)} %bitcast.8), calls=%async_computation | async-start | bytes 3145728 | tf_op jit(solution)/shard_map/all_to_all | solution.py:353
  10.6 1.0 copy-start.2
  11.6 1.0 copy-start.3
  13.4 0.8 copy-start.4
  14.2 0.8 copy-start.6
  15.0 0.8 copy-start.8
  15.8 0.8 copy-start.9
  31.1 30.9 %all-to-all-start.1 = ((f32[16,3,8,8,128]{4,3,2,1,0:T(8,128)}), f32[16,3,8,8,128]{4,3,2,1,0:T(8,128)S(1)}, u32[]{:S(2)}, u32[]{:S(2)}) async-start(f32[16,3,8,8,128]{4,3,2,1,0:T(8,128)} %bitcast.2), calls=%async_computation.1 | async-start | bytes 3145728 | tf_op jit(solution)/shard_map/all_to_all | solution.py:357
  37.8 25.0 %collective-permute-start.2 = (f32[10,16,8,128]{3,2,1,0:T(8,128)}, f32[10,16,8,128]{3,2,1,0:T(8,128)}, u32[]{:S(2)}, u32[]{:S(2)}) collective-permute-start(f32[10,16,8,128]{3,2,1,0:T(8,128)} %copy-done.9), channel_id=1, source_target_pairs={{0,1},{1,0},{2,3},{3,2},{4,5},{5,4},{6,7},{7,6},{8,9},{9,8},{10,11... | collective-permute-start | bytes 1966088 | tf_op jit(solution)/shard_map/ppermute | solution.py:336
  38.8 35.1 %collective-permute-start.3 = (f32[10,16,8,128]{3,2,1,0:T(8,128)}, f32[10,16,8,128]{3,2,1,0:T(8,128)}, u32[]{:S(2)}, u32[]{:S(2)}) collective-permute-start(f32[10,16,8,128]{3,2,1,0:T(8,128)} %copy-done.8), channel_id=1, source_target_pairs={{0,127},{1,2},{2,1},{3,4},{4,3},{5,6},{6,5},{7,8},{8,7},{9,10},{10... | collective-permute-start | bytes 1966088 | tf_op jit(solution)/shard_map/ppermute | solution.py:336
  61.9 11.9 %copy-start.5 = (f32[8,16,8,128]{3,2,1,0:T(8,128)S(1)}, f32[8,16,8,128]{3,2,1,0:T(8,128)}, u32[]{:S(2)}) copy-start(f32[8,16,8,128]{3,2,1,0:T(8,128)} %copy-done.4) | copy-start | bytes 1572868
  61.9 11.9 %copy-start.7 = (f32[8,16,8,128]{3,2,1,0:T(8,128)S(1)}, f32[8,16,8,128]{3,2,1,0:T(8,128)}, u32[]{:S(2)}) copy-start(f32[8,16,8,128]{3,2,1,0:T(8,128)} %copy-done.6) | copy-start | bytes 1572868
  62.0 19.7 %collective-permute-start = (f32[4,16,8,128]{3,2,1,0:T(8,128)S(1)}, f32[4,16,8,128]{3,2,1,0:T(8,128)S(1)}, u32[]{:S(2)}, u32[]{:S(2)}) collective-permute-start(f32[4,16,8,128]{3,2,1,0:T(8,128)S(1)} %get-tuple-element.28), channel_id=1, source_target_pairs={{0,1},{1,0},{2,3},{3,2},{4,5},{5,4},{6,7},{7,6},{8,9},{9,8},{10,11... | collective-permute-start | bytes 786440 | tf_op jit(solution)/shard_map/ppermute | solution.py:336
  62.5 19.2 %collective-permute-start.1 = (f32[4,16,8,128]{3,2,1,0:T(8,128)S(1)}, f32[4,16,8,128]{3,2,1,0:T(8,128)S(1)}, u32[]{:S(2)}, u32[]{:S(2)}) collective-permute-start(f32[4,16,8,128]{3,2,1,0:T(8,128)S(1)} %get-tuple-element.29), channel_id=1, source_target_pairs={{0,127},{1,2},{2,1},{3,4},{4,3},{5,6},{6,5},{7,8},{8,7},{9,10},{10... | collective-permute-start | bytes 786440 | tf_op jit(solution)/shard_map/ppermute | solution.py:336
  81.7 20.9 %copy-start = (f32[22,6,16,8,128]{4,3,2,1,0:T(8,128)S(1)}, f32[22,6,16,8,128]{4,3,2,1,0:T(8,128)}, u32[]{:S(2)}) copy-start(f32[22,6,16,8,128]{4,3,2,1,0:T(8,128)} %get-tuple-element.35.weights) | copy-start | bytes 25952260
  88.4 9.3 %collective-permute-start.4 = (f32[8,16,8,128]{3,2,1,0:T(8,128)S(1)}, f32[8,16,8,128]{3,2,1,0:T(8,128)S(1)}, u32[]{:S(2)}, u32[]{:S(2)}) collective-permute-start(f32[8,16,8,128]{3,2,1,0:T(8,128)S(1)} %get-tuple-element.41.source), channel_id=1, source_target_pairs={{0,1},{1,0},{2,3},{3,2},{4,5},{5,4},{6,7},{7,6},{8,9},{9,8},{10,11... | collective-permute-start | bytes 1572872 | tf_op jit(solution)/shard_map/ppermute | solution.py:336
  88.5 14.1 %collective-permute-start.5 = (f32[8,16,8,128]{3,2,1,0:T(8,128)S(1)}, f32[8,16,8,128]{3,2,1,0:T(8,128)S(1)}, u32[]{:S(2)}, u32[]{:S(2)}) collective-permute-start(f32[8,16,8,128]{3,2,1,0:T(8,128)S(1)} %get-tuple-element.41.source), channel_id=1, source_target_pairs={{0,127},{1,2},{2,1},{3,4},{4,3},{5,6},{6,5},{7,8},{8,7},{9,10},{10... | collective-permute-start | bytes 1572872 | tf_op jit(solution)/shard_map/ppermute | solution.py:336
  133.2 14.4 %all-to-all-start.3 = ((f32[16,8,8,128]{3,2,1,0:T(8,128)}), f32[16,8,8,128]{3,2,1,0:T(8,128)S(1)}, u32[]{:S(2)}, u32[]{:S(2)}) async-start(f32[16,8,8,128]{3,2,1,0:T(8,128)} %all_to_all.20), calls=%async_computation.3 | async-start | bytes 1048576 | tf_op jit(solution)/shard_map/all_to_all | solution.py:387

commit v2 on v1

v2 whole, which is shorter than its diff:
```python
import functools

import jax
import jax.numpy as jnp
from jax import lax
from jax.experimental import pallas as pl
from jax.experimental.pallas import tpu as pltpu
from jax.sharding import PartitionSpec as P

SWEEPS = 8

particle_volume = 0.05
time_step = 0.5
viscosity = 0.1

ROWS = 8
PLANES = 8
GROUPS = 16
LANES = 128
TILE = (PLANES, LANES)
WIDE = 3 * ROWS
AXES = ("gx", "gy")
f32 = jnp.float32


def place():
    return lax.axis_index("gx") * lax.axis_size("gy") + lax.axis_index("gy")


def lane_ids():
    return lax.broadcasted_iota(jnp.int32, TILE, 1)


def plane_ids():
    return lax.broadcasted_iota(jnp.int32, TILE, 0)


def plane_up(tile):
    return pltpu.roll(tile, PLANES - 1, 0)


def plane_down(tile):
    return pltpu.roll(tile, 1, 0)


def column_neighbours(tiles):
    lanes = lane_ids()
    last, first = lanes == LANES - 1, lanes == 0
    ahead = [pltpu.roll(tile, LANES - 1, 1) for tile in tiles]
    behind = [pltpu.roll(tile, 1, 1) for tile in tiles]
    n = len(tiles)
    up = [jnp.where(last, ahead[g + 1], ahead[g]) if g < n - 1 else ahead[g] for g in range(n)]
    down = [jnp.where(first, behind[g - 1], behind[g]) if g > 0 else behind[g] for g in range(n)]
    return up, down


def no_column_up(g, tile):
    return jnp.where(lane_ids() == LANES - 1, 0.0, tile) if g == GROUPS - 1 else tile


def no_column_down(g, tile):
    return jnp.where(lane_ids() == 0, 0.0, tile) if g == 0 else tile


def weighted_sum(weights, row, g, tile, up, down, row_up, row_down):
    total = weights[row, 0, g] * plane_up(tile) + weights[row, 1, g] * plane_down(tile)
    total = total + (weights[row, 2, g] * row_up + weights[row, 3, g] * row_down)
    return total + (weights[row, 4, g] * up + weights[row, 5, g] * down)


def block_kernel(velocity, blocks, staged, arrived):
    copies = []
    for k in range(3):
        for z in range(0, PLANES, 2):
            planes = pl.ds(z, 2)
            copy = pltpu.make_async_copy(
                velocity.at[k, planes], staged.at[k, planes], arrived.at[k * (PLANES // 2) + z // 2]
            )
            copy.start()
            copies.append(copy)
    along, groups = blocks.shape[:2]
    for k in range(3):
        for copy in copies[k * (PLANES // 2) : (k + 1) * (PLANES // 2)]:
            copy.wait()
        for chunk in range(along * groups):
            rows = staged[k, :, pl.ds(chunk * ROWS, ROWS), :]
            blocks[chunk % along, chunk // along, k] = jnp.swapaxes(rows, 0, 1)


def particle_kernel(count, drag, velocity, voids, drag_out, force, first_near, second_near, first_far, second_far):
    even = lax.rem(lax.axis_index("gy"), 2) == 0
    for g in range(GROUPS):
        columns = pl.ds(g * LANES, LANES)
        voids[:, g] = jnp.swapaxes(1.0 - count[:, :, columns].astype(f32) * particle_volume, 0, 1)
        drags = drag[:, :, columns]
        drag_out[:, g] = jnp.swapaxes(drags, 0, 1)
        for k in range(3):
            force[k, :, g] = jnp.swapaxes(time_step * drags * velocity[k, :, :, columns], 0, 1)
    for near, far, last in ((first_near, first_far, even), (second_near, second_far, jnp.logical_not(even))):
        pair = jnp.where(last, ROWS - 2, 0)
        single = jnp.where(last, ROWS - 1, 0)
        rest = jnp.where(last, 0, 2)
        near[0:2] = voids[pl.ds(pair, 2)]
        near[2] = drag_out[single]
        near[3] = force[0, single]
        far[...] = voids[pl.ds(rest, ROWS - 2)]


class Side:
    def __init__(self, first):
        even = lax.rem(lax.axis_index("gy"), 2) == 0
        self.high = even if first else jnp.logical_not(even)
        devices = lax.axis_size("gx") * lax.axis_size("gy")
        low_there = (place() > 0).astype(f32)
        high_there = (place() < devices - 1).astype(f32)
        self.there = jnp.where(self.high, high_there, low_there)

    def at(self, high, low):
        return jnp.where(self.high, high, low)


def face_row(voids, row, store):
    planes = plane_ids()
    tiles = [voids[row, g] for g in range(GROUPS)]
    ups, downs = column_neighbours(tiles)
    for g in range(GROUPS):
        tile = tiles[g]
        near = [
            jnp.where(planes == PLANES - 1, 0.0, plane_up(tile)),
            jnp.where(planes == 0, 0.0, plane_down(tile)),
            voids[row + 1, g],
            voids[row - 1, g],
            no_column_up(g, ups[g]),
            no_column_down(g, downs[g]),
        ]
        faces = [0.5 * (tile + other) for other in near]
        total = faces[0]
        for face in faces[1:]:
            total = total + face
        inverse = jnp.where(tile > 0.0, 1.0 / total, 0.0)
        scaled = [face * inverse for face in faces]
        scaled[0] = jnp.where(planes == PLANES - 1, 0.0, scaled[0])
        scaled[1] = jnp.where(planes == 0, 0.0, scaled[1])
        scaled[4] = no_column_up(g, scaled[4])
        scaled[5] = no_column_down(g, scaled[5])
        store(g, scaled, tile, total, inverse)


def coefficient_kernel(voids, drag, force, first, second, weights, inverse_sum, centre, spread, given, voids_near):
    for message, side in ((first, Side(True)), (second, Side(False))):
        at = side.at(ROWS + 2, 0)
        for n in range(2):
            voids_near[at + n] = message[n] * side.there

    @pl.loop(0, ROWS)
    def _(row):
        voids_near[row + 2] = voids[row]

    def momentum_row(near, drag_at, force_at, own=None):
        def store(g, scaled, void, total, inverse):
            for n in range(6):
                weights[near, n, g] = scaled[n]
            scale = 1.0 / (void + time_step * drag_at(g))
            centre[near, g] = (void - time_step * viscosity * total) * scale
            spread[near, g] = (time_step * viscosity * total) * scale
            for k, value in enumerate(force_at(g)):
                given[k, near, g] = value * scale
            if own is not None:
                inverse_sum[own, g] = inverse

        face_row(voids_near, near + 1, store)

    @pl.loop(0, ROWS, step=2)
    def _(start):
        for row in (start, start + 1):
            momentum_row(
                row + 1,
                lambda g, row=row: drag[row, g],
                lambda g, row=row: [force[k, row, g] for k in range(3)],
                row,
            )

    for message, side in ((first, Side(True)), (second, Side(False))):
        momentum_row(
            side.at(ROWS + 1, 0), lambda g, m=message: m[2, g], lambda g, m=message: [m[3, g]]
        )


def outer_kernel(voids_near, first, second, near_weights, weights, wide):
    for message, side in ((first, Side(True)), (second, Side(False))):
        at = side.at(2 * ROWS + 2, 0)
        for n in range(ROWS - 2):
            wide[at + n] = message[n] * side.there

    @pl.loop(0, ROWS + 4)
    def _(row):
        wide[row + ROWS - 2] = voids_near[row]

    @pl.loop(0, ROWS + 2)
    def _(row):
        weights[row + ROWS - 2] = near_weights[row]

    def outer_row(row):
        def store(g, scaled, void, total, inverse):
            for n in range(6):
                weights[row - 1, n, g] = scaled[n]

        face_row(wide, row, store)

    @pl.loop(1, ROWS - 1, step=2)
    def _(start):
        for row in (start, start + 1, start + 2 * ROWS, start + 2 * ROWS + 1):
            outer_row(row)


def edge_kernel(velocity, first, second):
    even = lax.rem(lax.axis_index("gy"), 2) == 0
    first_row = jnp.where(even, ROWS - 2, 0)
    for message, pair, single in (
        (first, first_row, jnp.where(even, ROWS - 1, 0)),
        (second, ROWS - 2 - first_row, jnp.where(even, 0, ROWS - 1)),
    ):
        for g in range(GROUPS):
            message[0, g] = velocity[g, 0, pair]
            message[1, g] = velocity[g, 0, pair + 1]
            message[2, g] = velocity[g, 1, single]
            message[3, g] = velocity[g, 2, single]


def momentum_kernel(
    velocity, first, second, weights, inverse_sum, centre, spread, given, voids_near, predicted, source, wide, flux
):
    for message, side in ((first, Side(True)), (second, Side(False))):
        pair = side.at(ROWS + 2, 0)
        single = side.at(ROWS + 2, 1)
        for g in range(GROUPS):
            wide[0, pair, g] = message[0, g] * side.there
            wide[0, pair + 1, g] = message[1, g] * side.there
            wide[1, single, g] = message[2, g] * side.there
            wide[2, single, g] = message[3, g] * side.there

    @pl.loop(0, ROWS, step=2)
    def _(start):
        for row in (start, start + 1):
            for g in range(GROUPS):
                for k in range(3):
                    wide[k, row + 2, g] = velocity[g, k, row]

    planes = plane_ids()

    def predict(k, near):
        tiles = [wide[k, near + 1, g] for g in range(GROUPS)]
        ups, downs = column_neighbours(tiles)
        for g in range(GROUPS):
            around = weighted_sum(
                weights, near, g, tiles[g], ups[g], downs[g], wide[k, near + 2, g], wide[k, near, g]
            )
            yield centre[near, g] * tiles[g] + spread[near, g] * around + given[k, near, g]

    @pl.loop(0, ROWS + 2, step=5)
    def _(start):
        for near in range(5):
            for g, value in enumerate(predict(0, start + near)):
                flux[0, start + near, g] = value
                flux[1, start + near, g] = voids_near[start + near + 1, g] * value

    @pl.loop(0, ROWS, step=4)
    def _(start):
        for row in range(4):
            row = start + row
            near = row + 1
            second_flux = []
            for g, value in enumerate(predict(1, near)):
                predicted[1, row, g] = value
                second_flux.append(voids_near[near + 1, g] * value)
            ups, downs = column_neighbours(second_flux)
            for g, value in enumerate(predict(2, near)):
                predicted[2, row, g] = value
                predicted[0, row, g] = flux[0, near, g]
                third_flux = voids_near[near + 1, g] * value
                change = flux[1, near + 1, g] - flux[1, near - 1, g]
                change = change + (no_column_up(g, ups[g]) - no_column_down(g, downs[g]))
                change = change + (
                    jnp.where(planes == PLANES - 1, 0.0, plane_up(third_flux))
                    - jnp.where(planes == 0, 0.0, plane_down(third_flux))
                )
                source[row, g] = change * inverse_sum[row, g]


def sweep_kernel(source, first, second, weights, pressure, near_pressure, source_wide, one, other):
    sides = Side(True).at(2 * ROWS, 0), Side(False).at(2 * ROWS, 0)
    there = Side(True).there, Side(False).there

    @pl.loop(0, ROWS, step=2)
    def _(start):
        for row in (start, start + 1):
            for at, value in (
                (sides[0] + row, first[row] * there[0]),
                (sides[1] + row, second[row] * there[1]),
                (ROWS + row, source[row]),
            ):
                source_wide[at] = value
                one[at] = -value

    def sweep_row(row, now, store):
        tiles = [now[row, g] for g in range(GROUPS)]
        ups, downs = column_neighbours(tiles)
        for g in range(GROUPS):
            around = weighted_sum(weights, row - 1, g, tiles[g], ups[g], downs[g], now[row + 1, g], now[row - 1, g])
            store(row, g, around - source_wide[row, g])

    now, later = one, other
    for sweep in range(1, SWEEPS - 1):
        half = (WIDE - 2 * sweep) // 2

        def half_sweep(start, now=now, later=later, half=half):
            def store(row, g, value):
                later[row, g] = value

            for row in range(half):
                sweep_row(start + row, now, store)

        pl.loop(sweep, WIDE - sweep, step=half)(half_sweep)
        now, later = later, now

    def keep(row, g, value):
        near_pressure[row - (ROWS - 1), g] = value

    @pl.loop(0, ROWS, step=4)
    def _(start):
        def store(row, g, value):
            keep(row, g, value)
            pressure[g, row - ROWS] = value

        for row in range(4):
            sweep_row(ROWS + start + row, now, store)

    for row in (ROWS - 1, 2 * ROWS):
        sweep_row(row, now, keep)


def correct_kernel(near_pressure, predicted, velocity, slopes):
    planes = plane_ids()
    held = [[[None] * ROWS for _ in range(GROUPS)] for _ in range(3)]
    for row in range(ROWS):
        tiles = [near_pressure[row + 1, g] for g in range(GROUPS)]
        ups, downs = column_neighbours(tiles)
        for g in range(GROUPS):
            tile = tiles[g]
            held[0][g][row] = 0.5 * (near_pressure[row + 2, g] - near_pressure[row, g])
            held[1][g][row] = 0.5 * (no_column_up(g, ups[g]) - no_column_down(g, downs[g]))
            held[2][g][row] = 0.5 * (
                jnp.where(planes == PLANES - 1, 0.0, plane_up(tile)) - jnp.where(planes == 0, 0.0, plane_down(tile))
            )
    for g in range(GROUPS):
        columns = pl.ds(g * LANES, LANES)
        for k in range(3):
            slope = jnp.stack(held[k][g])
            slopes[k, :, :, columns] = jnp.swapaxes(slope, 0, 1)
            velocity[k, :, :, columns] = jnp.swapaxes(predicted[k, :, g] - time_step * slope, 0, 1)


def call(kernel, args, outs, scratch=(), vmem=16, spaces=None):
    spec = pl.BlockSpec(memory_space=pltpu.VMEM)
    shapes = [jax.ShapeDtypeStruct(shape, f32) for shape in outs]
    moved = sum(arg.size for arg in args) * 4 + sum(shape.size for shape in shapes) * 4
    return pl.pallas_call(
        kernel,
        out_shape=shapes,
        in_specs=spaces or [spec] * len(args),
        out_specs=[spec] * len(outs),
        scratch_shapes=[pltpu.VMEM(shape, f32) if isinstance(shape, tuple) else shape for shape in scratch],
        cost_estimate=pl.CostEstimate(flops=0, bytes_accessed=moved, transcendentals=0),
        compiler_params=pltpu.CompilerParams(vmem_limit_bytes=vmem * 1024 * 1024),
        name=kernel.__name__,
    )(*args)


def swap(first, second):
    devices = lax.axis_size("gx") * lax.axis_size("gy")
    inner = [(d, d ^ 1) for d in range(devices)]
    outer = [(d, (((d + 1) % devices) ^ 1) - 1) for d in range(devices)]
    outer = [(a, b % devices) for a, b in outer]
    return lax.ppermute(first, AXES, inner), lax.ppermute(second, AXES, outer)


def shards(particle_count, drag_coeff, particle_velocity, fluid_velocity):
    along, across = lax.axis_size("gy"), lax.axis_size("gx")
    field = (GROUPS, PLANES, LANES)
    own = (ROWS,) + field
    near = (ROWS + 2,) + field

    voids, drag, force, first, second, first_far, second_far = call(
        particle_kernel,
        (particle_count, drag_coeff, particle_velocity),
        [own, own, (3,) + own, (4,) + field, (4,) + field, (ROWS - 2,) + field, (ROWS - 2,) + field],
    )
    (blocks,) = call(
        block_kernel,
        (fluid_velocity,),
        [(along, across // along, 3, ROWS, PLANES, LANES)],
        [(3, PLANES, across * ROWS, LANES), pltpu.SemaphoreType.DMA((3 * PLANES // 2,))],
        spaces=[pl.BlockSpec(memory_space=pl.ANY)],
    )
    first, second = swap(first, second)
    blocks = lax.all_to_all(blocks, "gy", split_axis=0, concat_axis=0, tiled=True)
    blocks = blocks.reshape(across, 3, ROWS, PLANES, LANES)
    blocks, first_far, second_far = lax.optimization_barrier((blocks, first_far, second_far))
    first_far, second_far = swap(first_far, second_far)
    slab = lax.all_to_all(blocks, "gx", split_axis=0, concat_axis=0, tiled=True)
    near_weights, inverse_sum, centre, spread, given, voids_near = call(
        coefficient_kernel,
        (voids, drag, force, first, second),
        [(ROWS + 2, 6) + field, own, near, near, (3,) + near, (ROWS + 4,) + field],
    )

    edges = call(edge_kernel, (slab,), [(4,) + field] * 2)
    first, second = swap(*edges)
    predicted, source = call(
        momentum_kernel,
        (slab, first, second, near_weights, inverse_sum, centre, spread, given, voids_near),
        [(3,) + own, own],
        [(3, ROWS + 4) + field, (2,) + near],
    )
    *_, first_far, second_far = lax.optimization_barrier((*edges, first_far, second_far))
    (weights,) = call(
        outer_kernel,
        (voids_near, first_far, second_far, near_weights),
        [(WIDE - 2, 6) + field],
        [(WIDE,) + field],
    )
    first, second = swap(source, source)
    pressure, near_pressure = call(
        sweep_kernel,
        (source, first, second, weights),
        [(GROUPS, ROWS, PLANES, LANES), near],
        [(WIDE,) + field] * 3,
    )

    velocity, slopes = call(
        correct_kernel, (near_pressure, predicted), [(3, PLANES, ROWS, GROUPS * LANES)] * 2
    )

    pressure = lax.all_to_all(pressure, "gx", split_axis=0, concat_axis=0, tiled=True)
    pressure = lax.all_to_all(pressure, "gy", split_axis=0, concat_axis=0, tiled=True)
    pressure = pressure.reshape(along, across // along, ROWS, PLANES, LANES)
    pressure = pressure.transpose(3, 1, 0, 2, 4).reshape(PLANES, across * ROWS, LANES)
    return (pressure, velocity, slopes)


def solution(mesh):
    placed = (
        P(None, ("gx", "gy"), None),
        P(None, ("gx", "gy"), None),
        P(None, None, ("gx", "gy"), None),
        P(None, None, "gy", "gx"),
    )
    return jax.shard_map(
        shards,
        mesh=mesh,
        in_specs=placed,
        out_specs=(
            P(None, "gy", "gx"),
            P(None, None, ("gx", "gy"), None),
            P(None, None, ("gx", "gy"), None),
        ),
        check_vma=False,
    )
```

time: 149 us -> 138 us (0.926)
  Pallas kernels: 30.1 us -> 18.2 us
  starting transfers between devices: 26.3 us -> 32.8 us
  waiting for transfers between devices: 63.3 us -> 60.4 us
  blocking collectives: 18.3 us -> 16.6 us
    pallas_call x6 -> x8, Pallas kernels: 30.1 us -> 18.2 us  [call(): pl.pallas_call(kernel, out_shape=shapes, in_specs=spaces or [spec] * len(...]
    ppermute x6 -> x8, starting transfers between devices: 7.91 us -> 15.8 us  [swap(): return (lax.ppermute(first, AXES, inner), lax.ppermute(second, AXES, outer))]
    reshape x1 -> x0, local copies, waits for them, and re-layouts: 3.46 us -> none  [shards(): fluid_velocity.reshape(3, PLANES, across // along, along, ROWS, LANES)]
    unnamed x20 -> x28, local copies, waits for them, and re-layouts: 5.36 us -> 8.01 us
    all_to_all x1, blocking collectives: 18.3 us -> 16.6 us  [shards(): lax.all_to_all(pressure, 'gx', split_axis=0, concat_axis=0, tiled=True)]
    ppermute x6 -> x8, waiting for transfers between devices: 24.4 us -> 22.8 us  [swap(): return (lax.ppermute(first, AXES, inner), lax.ppermute(second, AXES, outer))]
  transfers between devices with their start and end apart: 9 -> 11, of which waited for: 6 -> 7; matrix products, arithmetic and copies ran while one was open for 0% -> 0% of each run, Pallas kernels for 8% -> 5%
where the time goes in v2:
time: 138 us
  waiting for transfers between devices  60.4 us (44%)
  starting transfers between devices  32.8 us (24%)
  Pallas kernels  18.2 us (13%)
  blocking collectives  16.6 us (12%)
  local copies, waits for them, and re-layouts  8.9 us (6%)
    ppermute x8, waiting for transfers between devices, swap(): return (lax.ppermute(first, AXES, inner), lax.ppermute(second, AXES, outer))  22.8 us
    pallas_call x8, Pallas kernels, call(): pl.pallas_call(kernel, out_shape=shapes, in_specs=spaces or [spec] * len(...  18.2 us
    all_to_all x1, waiting for transfers between devices, shards(): slab = lax.all_to_all(blocks, 'gx', split_axis=0, concat_axis=0, tiled=True)  17.8 us
    all_to_all x1, blocking collectives, shards(): lax.all_to_all(pressure, 'gx', split_axis=0, concat_axis=0, tiled=True)  16.6 us
    ppermute x8, starting transfers between devices, swap(): return (lax.ppermute(first, AXES, inner), lax.ppermute(second, AXES, outer))  15.8 us
    all_to_all x1, waiting for transfers between devices, shards(): lax.all_to_all(blocks, 'gy', split_axis=0, concat_axis=0, tiled=True)  13.2 us
    unnamed x28, local copies, waits for them, and re-layouts  8.01 us
    all_to_all x1, starting transfers between devices, shards(): slab = lax.all_to_all(blocks, 'gx', split_axis=0, concat_axis=0, tiled=True)  6.74 us
  transfers between devices with their start and end apart: 11, of which 7 were waited for; matrix products, arithmetic and copies ran while one was open for 0% of the time, Pallas kernels for 5%

profile of v2, /device:TPU:0, one launch (start us, length us, event | category | flops | bytes accessed | tf_op | source)
XLA Modules:
  0.0 137.7 jit_solution(3433171791799617218)
XLA Ops:
  0.6 1.4 %copy-done = f32[3,8,128,128]{3,2,1,0:T(8,128)S(1)} copy-done((f32[3,8,128,128]{3,2,1,0:T(8,128)S(1)}, f32[3,8,128,128]{3,2,1,0:T(8,128)}, u32[]{:S(2)}) %copy-start) | copy-done | bytes 1572888
  2.0 3.6 %block_kernel.1 = f32[8,2,3,8,8,128]{5,4,3,2,1,0:T(8,128)} custom-call(f32[3,8,128,128]{3,2,1,0:T(8,128)S(1)} %copy-done), custom_call_target="tpu_custom_call" | custom-call | bytes 3145728 | tf_op jit(solution)/shard_map/block_kernel/pallas_call | solution.py:367
  5.6 6.5 %all-to-all-start = ((f32[8,2,3,8,8,128]{5,4,3,2,1,0:T(8,128)}), f32[8,2,3,8,8,128]{5,4,3,2,1,0:T(8,128)}, u32[]{:S(2)}, u32[]{:S(2)}) async-start(f32[8,2,3,8,8,128]{5,4,3,2,1,0:T(8,128)} %block_kernel.1), calls=%async_computation | async-start | bytes 3145728 | tf_op jit(solution)/shard_map/all_to_all | solution.py:406
  12.1 1.0 copy-done.2
  13.1 1.0 copy-done.3
  14.8 0.8 copy-done.4
  15.6 0.8 copy-done.6
  16.4 0.7 copy-done.8
  17.2 0.8 copy-done.10
  17.9 0.7 copy-done.12
  18.7 0.7 copy-done.13
  19.4 13.2 %all-to-all-done = f32[8,2,3,8,8,128]{5,4,3,2,1,0:T(8,128)} async-done(((f32[8,2,3,8,8,128]{5,4,3,2,1,0:T(8,128)}), f32[8,2,3,8,8,128]{5,4,3,2,1,0:T(8,128)}, u32[]{:S(2)}, u32[]{:S(2)}) %all-to-all-start) | async-done | bytes 1572896 | tf_op jit(solution)/shard_map/all_to_all | solution.py:406
  32.6 6.7 %all-to-all-start.1 = ((f32[16,3,8,8,128]{4,3,2,1,0:T(8,128)}), f32[16,3,8,8,128]{4,3,2,1,0:T(8,128)S(1)}, u32[]{:S(2)}, u32[]{:S(2)}) async-start(f32[16,3,8,8,128]{4,3,2,1,0:T(8,128)} %bitcast), calls=%async_computation.1 | async-start | bytes 3145728 | tf_op jit(solution)/shard_map/all_to_all | solution.py:410
  39.4 0.9 collective-permute-start.2
  40.3 5.3 %collective-permute-start.3 = (f32[4,16,8,128]{3,2,1,0:T(8,128)}, f32[4,16,8,128]{3,2,1,0:T(8,128)}, u32[]{:S(2)}, u32[]{:S(2)}) collective-permute-start(f32[4,16,8,128]{3,2,1,0:T(8,128)} %copy-done.12), channel_id=1, source_target_pairs={{0,127},{1,2},{2,1},{3,4},{4,3},{5,6},{6,5},{7,8},{8,7},{9,10},{10... | collective-permute-start | bytes 786440 | tf_op jit(solution)/shard_map/ppermute | solution.py:384
  45.6 17.8 %all-to-all-done.1.velocity = f32[16,3,8,8,128]{4,3,2,1,0:T(8,128)S(1)} async-done(((f32[16,3,8,8,128]{4,3,2,1,0:T(8,128)}), f32[16,3,8,8,128]{4,3,2,1,0:T(8,128)S(1)}, u32[]{:S(2)}, u32[]{:S(2)}) %all-to-all-start.1) | async-done | bytes 1572896 | tf_op jit(solution)/shard_map/all_to_all | solution.py:410
  64.4 2.8 %collective-permute-done.3.second = f32[4,16,8,128]{3,2,1,0:T(8,128)} collective-permute-done((f32[4,16,8,128]{3,2,1,0:T(8,128)}, f32[4,16,8,128]{3,2,1,0:T(8,128)}, u32[]{:S(2)}, u32[]{:S(2)}) %collective-permute-start.3) | collective-permute-done | bytes 262176 | tf_op jit(solution)/shard_map/ppermute | solution.py:384
  67.2 2.2 %coefficient_kernel.1 = (f32[10,6,16,8,128]{4,3,2,1,0:T(8,128)S(1)}, f32[8,16,8,128]{3,2,1,0:T(8,128)S(1)}, f32[10,16,8,128]{3,2,1,0:T(8,128)S(1)}, f32[10,16,8,...) custom-call(f32[8,16,8,128]{3,2,1,0:T(8,128)S(1)} %copy-done.5, ...), custom_call_target="tpu_custom_call" | custom-call | bytes 11665408 | tf_op jit(solution)/shard_map/coefficient_kernel/pallas_call | solution.py:367
  69.4 1.7 %collective-permute-done.first = f32[4,16,8,128]{3,2,1,0:T(8,128)S(1)} collective-permute-done((f32[4,16,8,128]{3,2,1,0:T(8,128)S(1)}, f32[4,16,8,128]{3,2,1,0:T(8,128)S(1)}, u32[]{:S(2)}, u32[]{:S(2)}) %collective-permute-start) | collective-permute-done | bytes 262176 | tf_op jit(solution)/shard_map/ppermute | solution.py:384
  71.1 4.2 %collective-permute-done.1.second = f32[4,16,8,128]{3,2,1,0:T(8,128)S(1)} collective-permute-done((f32[4,16,8,128]{3,2,1,0:T(8,128)S(1)}, f32[4,16,8,128]{3,2,1,0:T(8,128)S(1)}, u32[]{:S(2)}, u32[]{:S(2)}) %collective-permute-start.1) | collective-permute-done | bytes 262176 | tf_op jit(solution)/shard_map/ppermute | solution.py:384
  75.3 2.3 %momentum_kernel.1 = (f32[3,8,16,8,128]{4,3,2,1,0:T(8,128)S(1)}, f32[8,16,8,128]{3,2,1,0:T(8,128)S(1)}) custom-call(f32[16,3,8,8,128]{4,3,2,1,0:T(8,128)S(1)} %all-to-all-done.1.velocity, f32[4,16,8,128]{3,2,1,0:T(8,128)S(1)} %collective-permute-done.first, f32[4,16,8,128]{3,2,1,0:T(8,128)S(1)} %collective-permute-done.1.second, ...), custom_call_target="tpu_custom_call" | custom-call | bytes 12713984 | tf_op jit(solution)/shard_map/momentum_kernel/pallas_call | solution.py:367
  77.6 0.7 collective-permute-start.5
  78.2 2.0 %collective-permute-start.6 = (f32[6,16,8,128]{3,2,1,0:T(8,128)S(1)}, f32[6,16,8,128]{3,2,1,0:T(8,128)S(1)}, u32[]{:S(2)}, u32[]{:S(2)}) collective-permute-start(f32[6,16,8,128]{3,2,1,0:T(8,128)S(1)} %copy-done.11), channel_id=1, source_target_pairs={{0,1},{1,0},{2,3},{3,2},{4,5},{5,4},{6,7},{7,6},{8,9},{9,8},{10,11... | collective-permute-start | bytes 1179656 | tf_op jit(solution)/shard_map/ppermute | solution.py:384
  80.2 6.0 %collective-permute-start.7 = (f32[6,16,8,128]{3,2,1,0:T(8,128)S(1)}, f32[6,16,8,128]{3,2,1,0:T(8,128)S(1)}, u32[]{:S(2)}, u32[]{:S(2)}) collective-permute-start(f32[6,16,8,128]{3,2,1,0:T(8,128)S(1)} %copy-done.9), channel_id=1, source_target_pairs={{0,127},{1,2},{2,1},{3,4},{4,3},{5,6},{6,5},{7,8},{8,7},{9,10},{10... | collective-permute-start | bytes 1179656 | tf_op jit(solution)/shard_map/ppermute | solution.py:384
  86.3 14.0 %collective-permute-done.6.first = f32[6,16,8,128]{3,2,1,0:T(8,128)S(1)} collective-permute-done((f32[6,16,8,128]{3,2,1,0:T(8,128)S(1)}, f32[6,16,8,128]{3,2,1,0:T(8,128)S(1)}, u32[]{:S(2)}, u32[]{:S(2)}) %collective-permute-start.6) | collective-permute-done | bytes 393248 | tf_op jit(solution)/shard_map/ppermute | solution.py:384
  100.3 1.5 %outer_kernel.1.weights = f32[22,6,16,8,128]{4,3,2,1,0:T(8,128)S(1)} custom-call(f32[12,16,8,128]{3,2,1,0:T(8,128)S(1)} %get-tuple-element.44.voids_near, f32[6,16,8,128]{3,2,1,0:T(8,128)S(1)} %collective-permute-done.6.first, f32[6,16,8,128]{3,2,1,0:T(8,128)S(1)} %collective-permute-done.7.second, ...), custom_call_target="tpu_custom_call" | custom-call | bytes 14155776 | tf_op jit(solution)/shard_map/outer_kernel/pallas_call | solution.py:367
  101.8 5.5 %sweep_kernel.1 = (f32[16,8,8,128]{3,2,1,0:T(8,128)S(1)}, f32[10,16,8,128]{3,2,1,0:T(8,128)S(1)}) custom-call(f32[8,16,8,128]{3,2,1,0:T(8,128)S(1)} %get-tuple-element.45.source, f32[8,16,8,128]{3,2,1,0:T(8,128)S(1)} %collective-permute-done.4.first, f32[8,16,8,128]{3,2,1,0:T(8,128)S(1)} %collective-permute-done.5.second, ...), custom_call_target="tpu_custom_call" | custom-call | bytes 11403264 | tf_op jit(solution)/shard_map/sweep_kernel/pallas_call | solution.py:367
  107.3 16.6 %all_to_all.20 = f32[16,8,8,128]{3,2,1,0:T(8,128)} all-to-all(f32[16,8,8,128]{3,2,1,0:T(8,128)S(1)} %get-tuple-element.50), channel_id=1, replica_groups=mesh['gx'=16,'gy'=8] {'gx'}, dimensions={0} | all-to-all | bytes 1048576 | tf_op jit(solution)/shard_map/all_to_all | solution.py:444
  123.9 3.7 %all-to-all-start.3 = ((f32[16,8,8,128]{3,2,1,0:T(8,128)}), f32[16,8,8,128]{3,2,1,0:T(8,128)S(1)}, u32[]{:S(2)}, u32[]{:S(2)}) async-start(f32[16,8,8,128]{3,2,1,0:T(8,128)} %all_to_all.20), calls=%async_computation.3 | async-start | bytes 1048576 | tf_op jit(solution)/shard_map/all_to_all | solution.py:445
  127.7 2.6 %correct_kernel.1 = (f32[3,8,8,2048]{3,2,1,0:T(8,128)}, f32[3,8,8,2048]{3,2,1,0:T(8,128)}) custom-call(f32[10,16,8,128]{3,2,1,0:T(8,128)S(1)} %get-tuple-element.51.near_pressure, f32[3,8,16,8,128]{4,3,2,1,0:T(8,128)S(1)} %get-tuple-element.52.predicted), custom_call_target="tpu_custom_call" | custom-call | bytes 5373952 | tf_op jit(solution)/shard_map/correct_kernel/pallas_call | solution.py:367
  130.3 6.6 %all-to-all-done.3 = f32[16,8,8,128]{3,2,1,0:T(8,128)S(1)} async-done(((f32[16,8,8,128]{3,2,1,0:T(8,128)}), f32[16,8,8,128]{3,2,1,0:T(8,128)S(1)}, u32[]{:S(2)}, u32[]{:S(2)}) %all-to-all-start.3) | async-done | bytes 524320 | tf_op jit(solution)/shard_map/all_to_all | solution.py:445
  136.8 0.9 copy.7
  (28 shorter events, 1.6 us)
Async XLA Ops:
  0.6 1.4 %copy-start = (f32[3,8,128,128]{3,2,1,0:T(8,128)S(1)}, f32[3,8,128,128]{3,2,1,0:T(8,128)}, u32[]{:S(2)}) copy-start(f32[3,8,128,128]{3,2,1,0:T(8,128)} %velocity.2) | copy-start | bytes 4718596
  5.6 6.5 %copy-start.1 = (f32[3,8,8,2048]{3,2,1,0:T(8,128)S(1)}, f32[3,8,8,2048]{3,2,1,0:T(8,128)}, u32[]{:S(2)}) copy-start(f32[3,8,8,2048]{3,2,1,0:T(8,128)} %velocity.3) | copy-start | bytes 4718596
  5.6 27.0 %all-to-all-start = ((f32[8,2,3,8,8,128]{5,4,3,2,1,0:T(8,128)}), f32[8,2,3,8,8,128]{5,4,3,2,1,0:T(8,128)}, u32[]{:S(2)}, u32[]{:S(2)}) async-start(f32[8,2,3,8,8,128]{5,4,3,2,1,0:T(8,128)} %block_kernel.1), calls=%async_computation | async-start | bytes 3145728 | tf_op jit(solution)/shard_map/all_to_all | solution.py:406
  12.1 1.0 copy-start.2
  13.1 1.0 copy-start.3
  14.8 0.8 copy-start.4
  15.6 0.8 copy-start.6
  16.4 0.8 copy-start.8
  17.2 0.8 copy-start.10
  17.9 0.7 copy-start.12
  18.7 0.7 copy-start.13
  32.6 30.9 %all-to-all-start.1 = ((f32[16,3,8,8,128]{4,3,2,1,0:T(8,128)}), f32[16,3,8,8,128]{4,3,2,1,0:T(8,128)S(1)}, u32[]{:S(2)}, u32[]{:S(2)}) async-start(f32[16,3,8,8,128]{4,3,2,1,0:T(8,128)} %bitcast), calls=%async_computation.1 | async-start | bytes 3145728 | tf_op jit(solution)/shard_map/all_to_all | solution.py:410
  39.4 25.0 %collective-permute-start.2 = (f32[4,16,8,128]{3,2,1,0:T(8,128)}, f32[4,16,8,128]{3,2,1,0:T(8,128)S(1)}, u32[]{:S(2)}, u32[]{:S(2)}) collective-permute-start(f32[4,16,8,128]{3,2,1,0:T(8,128)} %copy-done.13), channel_id=1, source_target_pairs={{0,1},{1,0},{2,3},{3,2},{4,5},{5,4},{6,7},{7,6},{8,9},{9,8},{10,11... | collective-permute-start | bytes 786440 | tf_op jit(solution)/shard_map/ppermute | solution.py:384
  40.3 26.9 %collective-permute-start.3 = (f32[4,16,8,128]{3,2,1,0:T(8,128)}, f32[4,16,8,128]{3,2,1,0:T(8,128)}, u32[]{:S(2)}, u32[]{:S(2)}) collective-permute-start(f32[4,16,8,128]{3,2,1,0:T(8,128)} %copy-done.12), channel_id=1, source_target_pairs={{0,127},{1,2},{2,1},{3,4},{4,3},{5,6},{6,5},{7,8},{8,7},{9,10},{10... | collective-permute-start | bytes 786440 | tf_op jit(solution)/shard_map/ppermute | solution.py:384
  63.5 3.8 %copy-start.5 = (f32[8,16,8,128]{3,2,1,0:T(8,128)S(1)}, f32[8,16,8,128]{3,2,1,0:T(8,128)}, u32[]{:S(2)}) copy-start(f32[8,16,8,128]{3,2,1,0:T(8,128)} %copy-done.4) | copy-start | bytes 1572868
  63.5 3.8 %copy-start.7 = (f32[8,16,8,128]{3,2,1,0:T(8,128)S(1)}, f32[8,16,8,128]{3,2,1,0:T(8,128)}, u32[]{:S(2)}) copy-start(f32[8,16,8,128]{3,2,1,0:T(8,128)} %copy-done.6) | copy-start | bytes 1572868
  63.5 7.6 %collective-permute-start = (f32[4,16,8,128]{3,2,1,0:T(8,128)S(1)}, f32[4,16,8,128]{3,2,1,0:T(8,128)S(1)}, u32[]{:S(2)}, u32[]{:S(2)}) collective-permute-start(f32[4,16,8,128]{3,2,1,0:T(8,128)S(1)} %get-tuple-element.32), channel_id=1, source_target_pairs={{0,1},{1,0},{2,3},{3,2},{4,5},{5,4},{6,7},{7,6},{8,9},{9,8},{10,11... | collective-permute-start | bytes 786440 | tf_op jit(solution)/shard_map/ppermute | solution.py:384
  64.0 11.2 %collective-permute-start.1 = (f32[4,16,8,128]{3,2,1,0:T(8,128)S(1)}, f32[4,16,8,128]{3,2,1,0:T(8,128)S(1)}, u32[]{:S(2)}, u32[]{:S(2)}) collective-permute-start(f32[4,16,8,128]{3,2,1,0:T(8,128)S(1)} %get-tuple-element.33), channel_id=1, source_target_pairs={{0,127},{1,2},{2,1},{3,4},{4,3},{5,6},{6,5},{7,8},{8,7},{9,10},{10... | collective-permute-start | bytes 786440 | tf_op jit(solution)/shard_map/ppermute | solution.py:384
  75.3 2.9 %copy-start.11 = (f32[6,16,8,128]{3,2,1,0:T(8,128)S(1)}, f32[6,16,8,128]{3,2,1,0:T(8,128)}, u32[]{:S(2)}) copy-start(f32[6,16,8,128]{3,2,1,0:T(8,128)} %copy-done.10) | copy-start | bytes 1179652
  75.3 5.0 %copy-start.9 = (f32[6,16,8,128]{3,2,1,0:T(8,128)S(1)}, f32[6,16,8,128]{3,2,1,0:T(8,128)}, u32[]{:S(2)}) copy-start(f32[6,16,8,128]{3,2,1,0:T(8,128)} %copy-done.8) | copy-start | bytes 1179652
  77.6 24.2 %collective-permute-start.5 = (f32[8,16,8,128]{3,2,1,0:T(8,128)S(1)}, f32[8,16,8,128]{3,2,1,0:T(8,128)S(1)}, u32[]{:S(2)}, u32[]{:S(2)}) collective-permute-start(f32[8,16,8,128]{3,2,1,0:T(8,128)S(1)} %get-tuple-element.45.source), channel_id=1, source_target_pairs={{0,127},{1,2},{2,1},{3,4},{4,3},{5,6},{6,5},{7,8},{8,7},{9,10},{10... | collective-permute-start | bytes 1572872 | tf_op jit(solution)/shard_map/ppermute | solution.py:384
  78.2 23.6 %collective-permute-start.4 = (f32[8,16,8,128]{3,2,1,0:T(8,128)S(1)}, f32[8,16,8,128]{3,2,1,0:T(8,128)S(1)}, u32[]{:S(2)}, u32[]{:S(2)}) collective-permute-start(f32[8,16,8,128]{3,2,1,0:T(8,128)S(1)} %get-tuple-element.45.source), channel_id=1, source_target_pairs={{0,1},{1,0},{2,3},{3,2},{4,5},{5,4},{6,7},{7,6},{8,9},{9,8},{10,11... | collective-permute-start | bytes 1572872 | tf_op jit(solution)/shard_map/ppermute | solution.py:384
  78.2 22.1 %collective-permute-start.6 = (f32[6,16,8,128]{3,2,1,0:T(8,128)S(1)}, f32[6,16,8,128]{3,2,1,0:T(8,128)S(1)}, u32[]{:S(2)}, u32[]{:S(2)}) collective-permute-start(f32[6,16,8,128]{3,2,1,0:T(8,128)S(1)} %copy-done.11), channel_id=1, source_target_pairs={{0,1},{1,0},{2,3},{3,2},{4,5},{5,4},{6,7},{7,6},{8,9},{9,8},{10,11... | collective-permute-start | bytes 1179656 | tf_op jit(solution)/shard_map/ppermute | solution.py:384
  80.2 20.1 %collective-permute-start.7 = (f32[6,16,8,128]{3,2,1,0:T(8,128)S(1)}, f32[6,16,8,128]{3,2,1,0:T(8,128)S(1)}, u32[]{:S(2)}, u32[]{:S(2)}) collective-permute-start(f32[6,16,8,128]{3,2,1,0:T(8,128)S(1)} %copy-done.9), channel_id=1, source_target_pairs={{0,127},{1,2},{2,1},{3,4},{4,3},{5,6},{6,5},{7,8},{8,7},{9,10},{10... | collective-permute-start | bytes 1179656 | tf_op jit(solution)/shard_map/ppermute | solution.py:384
  123.9 12.9 %all-to-all-start.3 = ((f32[16,8,8,128]{3,2,1,0:T(8,128)}), f32[16,8,8,128]{3,2,1,0:T(8,128)S(1)}, u32[]{:S(2)}, u32[]{:S(2)}) async-start(f32[16,8,8,128]{3,2,1,0:T(8,128)} %all_to_all.20), calls=%async_computation.3 | async-start | bytes 1048576 | tf_op jit(solution)/shard_map/all_to_all | solution.py:445

commit v3 on v2

--- a/solution.py
+++ b/solution.py
@@ -19,6 +19,7 @@
 LANES = 128
 TILE = (PLANES, LANES)
 WIDE = 3 * ROWS
+COVER = 6_000_000_000
 AXES = ("gx", "gy")
 f32 = jnp.float32
 
@@ -68,23 +69,18 @@
     return total + (weights[row, 4, g] * up + weights[row, 5, g] * down)
 
 
-def block_kernel(velocity, blocks, staged, arrived):
+def block_kernel(velocity, blocks, turned, left):
+    along, groups = blocks.shape[:2]
     copies = []
     for k in range(3):
-        for z in range(0, PLANES, 2):
-            planes = pl.ds(z, 2)
-            copy = pltpu.make_async_copy(
-                velocity.at[k, planes], staged.at[k, planes], arrived.at[k * (PLANES // 2) + z // 2]
-            )
-            copy.start()
-            copies.append(copy)
-    along, groups = blocks.shape[:2]
-    for k in range(3):
-        for copy in copies[k * (PLANES // 2) : (k + 1) * (PLANES // 2)]:
-            copy.wait()
-        for chunk in range(along * groups):
-            rows = staged[k, :, pl.ds(chunk * ROWS, ROWS), :]
-            blocks[chunk % along, chunk // along, k] = jnp.swapaxes(rows, 0, 1)
+        for part in range(groups):
+            for chunk in range(along):
+                rows = velocity[k, :, pl.ds((part * along + chunk) * ROWS, ROWS), :]
+                turned[chunk, part, k] = jnp.swapaxes(rows, 0, 1)
+            copies.append(pltpu.make_async_copy(turned.at[:, part, k], blocks.at[:, part, k], left.at[k, part]))
+            copies[-1].start()
+    for copy in copies:
+        copy.wait()
 
 
 def particle_kernel(count, drag, velocity, voids, drag_out, force, first_near, second_near, first_far, second_far):
@@ -360,17 +356,17 @@
             velocity[k, :, :, columns] = jnp.swapaxes(predicted[k, :, g] - time_step * slope, 0, 1)
 
 
-def call(kernel, args, outs, scratch=(), vmem=16, spaces=None):
+def call(kernel, args, outs, scratch=(), vmem=16, to=pltpu.VMEM, flops=0):
     spec = pl.BlockSpec(memory_space=pltpu.VMEM)
     shapes = [jax.ShapeDtypeStruct(shape, f32) for shape in outs]
     moved = sum(arg.size for arg in args) * 4 + sum(shape.size for shape in shapes) * 4
     return pl.pallas_call(
         kernel,
         out_shape=shapes,
-        in_specs=spaces or [spec] * len(args),
-        out_specs=[spec] * len(outs),
+        in_specs=[spec] * len(args),
+        out_specs=[pl.BlockSpec(memory_space=to)] * len(outs),
         scratch_shapes=[pltpu.VMEM(shape, f32) if isinstance(shape, tuple) else shape for shape in scratch],
-        cost_estimate=pl.CostEstimate(flops=0, bytes_accessed=moved, transcendentals=0),
+        cost_estimate=pl.CostEstimate(flops=flops, bytes_accessed=moved, transcendentals=0),
         compiler_params=pltpu.CompilerParams(vmem_limit_bytes=vmem * 1024 * 1024),
         name=kernel.__name__,
     )(*args)
@@ -399,35 +395,40 @@
         block_kernel,
         (fluid_velocity,),
         [(along, across // along, 3, ROWS, PLANES, LANES)],
-        [(3, PLANES, across * ROWS, LANES), pltpu.SemaphoreType.DMA((3 * PLANES // 2,))],
-        spaces=[pl.BlockSpec(memory_space=pl.ANY)],
-    )
+        [
+            (along, across // along, 3, ROWS, PLANES, LANES),
+            pltpu.SemaphoreType.DMA((3, across // along)),
+        ],
+        to=pl.ANY,
+    )
+    blocks = lax.all_to_all(blocks, "gy", split_axis=0, concat_axis=0, tiled=True)
+    blocks, first, second = lax.optimization_barrier((blocks, first, second))
     first, second = swap(first, second)
-    blocks = lax.all_to_all(blocks, "gy", split_axis=0, concat_axis=0, tiled=True)
     blocks = blocks.reshape(across, 3, ROWS, PLANES, LANES)
-    blocks, first_far, second_far = lax.optimization_barrier((blocks, first_far, second_far))
-    first_far, second_far = swap(first_far, second_far)
     slab = lax.all_to_all(blocks, "gx", split_axis=0, concat_axis=0, tiled=True)
     near_weights, inverse_sum, centre, spread, given, voids_near = call(
         coefficient_kernel,
         (voids, drag, force, first, second),
         [(ROWS + 2, 6) + field, own, near, near, (3,) + near, (ROWS + 4,) + field],
+        flops=COVER,
     )
 
     edges = call(edge_kernel, (slab,), [(4,) + field] * 2)
+    *edges, first_far, second_far = lax.optimization_barrier((*edges, first_far, second_far))
     first, second = swap(*edges)
+    first_far, second_far = swap(first_far, second_far)
     predicted, source = call(
         momentum_kernel,
         (slab, first, second, near_weights, inverse_sum, centre, spread, given, voids_near),
         [(3,) + own, own],
         [(3, ROWS + 4) + field, (2,) + near],
     )
-    *_, first_far, second_far = lax.optimization_barrier((*edges, first_far, second_far))
     (weights,) = call(
         outer_kernel,
         (voids_near, first_far, second_far, near_weights),
         [(WIDE - 2, 6) + field],
         [(WIDE,) + field],
+        flops=COVER,
     )
     first, second = swap(source, source)
     pressure, near_pressure = call(

time: 138 us -> 128 us (0.928)
  waiting for transfers between devices: 60.4 us -> 53.3 us
  Pallas kernels: 18.2 us -> 16 us
    ppermute x8, waiting for transfers between devices: 22.8 us -> 13.3 us  [swap(): return (lax.ppermute(first, AXES, inner), lax.ppermute(second, AXES, outer))]
    all_to_all x1, waiting for transfers between devices: 13.2 us -> 15.7 us  [shards(): lax.all_to_all(blocks, 'gy', split_axis=0, concat_axis=0, tiled=True)]
    pallas_call x8, Pallas kernels: 18.2 us -> 16 us  [call(): pl.pallas_call(kernel, out_shape=shapes, in_specs=[spec] * len(args), out...]
    unnamed x28 -> x26, local copies, waits for them, and re-layouts: 8.01 us -> 7.64 us
  transfers between devices with their start and end apart: 11 -> 11, of which waited for: 7 -> 6; matrix products, arithmetic and copies ran while one was open for 0% -> 0% of each run, Pallas kernels for 5% -> 7%
where the time goes in v3:
time: 128 us; the launch traced here: 127 us
  waiting for transfers between devices  53.3 us (42%)
  starting transfers between devices  32.9 us (26%)
  Pallas kernels  16 us (12%)
  blocking collectives  15.7 us (12%)
  local copies, waits for them, and re-layouts  8.53 us (7%)
    all_to_all x1, waiting for transfers between devices, shards(): slab = lax.all_to_all(blocks, 'gx', split_axis=0, concat_axis=0, tiled=True)  17.7 us
    pallas_call x8, Pallas kernels, call(): pl.pallas_call(kernel, out_shape=shapes, in_specs=[spec] * len(args), out...  16 us
    all_to_all x1, blocking collectives, shards(): lax.all_to_all(pressure, 'gx', split_axis=0, concat_axis=0, tiled=True)  15.7 us
    all_to_all x1, waiting for transfers between devices, shards(): lax.all_to_all(blocks, 'gy', split_axis=0, concat_axis=0, tiled=True)  15.7 us
    ppermute x8, starting transfers between devices, swap(): return (lax.ppermute(first, AXES, inner), lax.ppermute(second, AXES, outer))  15.4 us
    ppermute x8, waiting for transfers between devices, swap(): return (lax.ppermute(first, AXES, inner), lax.ppermute(second, AXES, outer))  13.3 us
    unnamed x26, local copies, waits for them, and re-layouts  7.64 us
    all_to_all x1, starting transfers between devices, shards(): slab = lax.all_to_all(blocks, 'gx', split_axis=0, concat_axis=0, tiled=True)  6.74 us
  transfers between devices with their start and end apart: 11, of which 6 were waited for; matrix products, arithmetic and copies ran while one was open for 0% of the time, Pallas kernels for 7%

profile of v3, /device:TPU:0, one launch (start us, length us, event | category | flops | bytes accessed | tf_op | source)
XLA Modules:
  0.0 127.2 jit_solution(7438621792784657702)
XLA Ops:
  0.6 1.4 %copy-done = f32[3,8,128,128]{3,2,1,0:T(8,128)S(1)} copy-done((f32[3,8,128,128]{3,2,1,0:T(8,128)S(1)}, f32[3,8,128,128]{3,2,1,0:T(8,128)}, u32[]{:S(2)}) %copy-start) | copy-done | bytes 1572888
  2.0 1.2 block_kernel.1
  3.3 6.5 %all-to-all-start = ((f32[8,2,3,8,8,128]{5,4,3,2,1,0:T(8,128)}), f32[8,2,3,8,8,128]{5,4,3,2,1,0:T(8,128)}, u32[]{:S(2)}, u32[]{:S(2)}) async-start(f32[8,2,3,8,8,128]{5,4,3,2,1,0:T(8,128)} %block_kernel.1), calls=%async_computation | async-start | bytes 3145728 | tf_op jit(solution)/shard_map/all_to_all | solution.py:404
  9.8 0.7 particle_kernel.1
  10.5 1.1 copy-done.4
  11.6 0.8 copy-done.6
  12.4 0.8 copy-done.8
  13.2 0.7 copy-done.11
  13.9 0.7 copy-done.12
  14.6 15.7 %all-to-all-done = f32[8,2,3,8,8,128]{5,4,3,2,1,0:T(8,128)} async-done(((f32[8,2,3,8,8,128]{5,4,3,2,1,0:T(8,128)}), f32[8,2,3,8,8,128]{5,4,3,2,1,0:T(8,128)}, u32[]{:S(2)}, u32[]{:S(2)}) %all-to-all-start) | async-done | bytes 1572896 | tf_op jit(solution)/shard_map/all_to_all | solution.py:404
  30.3 6.7 %all-to-all-start.1 = ((f32[16,3,8,8,128]{4,3,2,1,0:T(8,128)}), f32[16,3,8,8,128]{4,3,2,1,0:T(8,128)S(1)}, u32[]{:S(2)}, u32[]{:S(2)}) async-start(f32[16,3,8,8,128]{4,3,2,1,0:T(8,128)} %bitcast), calls=%async_computation.1 | async-start | bytes 3145728 | tf_op jit(solution)/shard_map/all_to_all | solution.py:408
  37.1 0.9 collective-permute-start.2
  38.0 5.4 %collective-permute-start.3 = (f32[4,16,8,128]{3,2,1,0:T(8,128)}, f32[4,16,8,128]{3,2,1,0:T(8,128)}, u32[]{:S(2)}, u32[]{:S(2)}) collective-permute-start(f32[4,16,8,128]{3,2,1,0:T(8,128)} %copy-done.11), channel_id=1, source_target_pairs={{0,127},{1,2},{2,1},{3,4},{4,3},{5,6},{6,5},{7,8},{8,7},{9,10},{10... | collective-permute-start | bytes 786440 | tf_op jit(solution)/shard_map/ppermute | solution.py:380
  43.4 17.7 %all-to-all-done.1.velocity = f32[16,3,8,8,128]{4,3,2,1,0:T(8,128)S(1)} async-done(((f32[16,3,8,8,128]{4,3,2,1,0:T(8,128)}), f32[16,3,8,8,128]{4,3,2,1,0:T(8,128)S(1)}, u32[]{:S(2)}, u32[]{:S(2)}) %all-to-all-start.1) | async-done | bytes 1572896 | tf_op jit(solution)/shard_map/all_to_all | solution.py:408
  61.2 0.5 collective-permute-start
  62.1 2.6 %collective-permute-start.6 = (f32[6,16,8,128]{3,2,1,0:T(8,128)}, f32[6,16,8,128]{3,2,1,0:T(8,128)S(1)}, u32[]{:S(2)}, u32[]{:S(2)}) collective-permute-start(f32[6,16,8,128]{3,2,1,0:T(8,128)} %copy-done.10), channel_id=1, source_target_pairs={{0,1},{1,0},{2,3},{3,2},{4,5},{5,4},{6,7},{7,6},{8,9},{9,8},{10,11... | collective-permute-start | bytes 1179656 | tf_op jit(solution)/shard_map/ppermute | solution.py:380
  64.7 4.2 %collective-permute-start.7 = (f32[6,16,8,128]{3,2,1,0:T(8,128)S(1)}, f32[6,16,8,128]{3,2,1,0:T(8,128)S(1)}, u32[]{:S(2)}, u32[]{:S(2)}) collective-permute-start(f32[6,16,8,128]{3,2,1,0:T(8,128)S(1)} %get-tuple-element.53), channel_id=1, source_target_pairs={{0,127},{1,2},{2,1},{3,4},{4,3},{5,6},{6,5},{7,8},{8,7},{9,10},{10... | collective-permute-start | bytes 1179656 | tf_op jit(solution)/shard_map/ppermute | solution.py:380
  68.9 1.0 copy-done.7
  70.0 1.0 copy-done.9
  71.0 2.2 %coefficient_kernel.1 = (f32[10,6,16,8,128]{4,3,2,1,0:T(8,128)S(1)}, f32[8,16,8,128]{3,2,1,0:T(8,128)S(1)}, f32[10,16,8,128]{3,2,1,0:T(8,128)S(1)}, f32[10,16,8,...) custom-call(f32[8,16,8,128]{3,2,1,0:T(8,128)S(1)} %copy-done.7, ...), custom_call_target="tpu_custom_call" | custom-call | flops 6000000000 | bytes 11665408 | tf_op jit(solution)/shard_map/coefficient_kernel/pallas_call | solution.py:363
  73.3 1.7 %collective-permute-done.1.second = f32[4,16,8,128]{3,2,1,0:T(8,128)S(1)} collective-permute-done((f32[4,16,8,128]{3,2,1,0:T(8,128)S(1)}, f32[4,16,8,128]{3,2,1,0:T(8,128)S(1)}, u32[]{:S(2)}, u32[]{:S(2)}) %collective-permute-start.1) | collective-permute-done | bytes 262176 | tf_op jit(solution)/shard_map/ppermute | solution.py:380
  75.0 2.3 %momentum_kernel.1 = (f32[3,8,16,8,128]{4,3,2,1,0:T(8,128)S(1)}, f32[8,16,8,128]{3,2,1,0:T(8,128)S(1)}) custom-call(f32[16,3,8,8,128]{4,3,2,1,0:T(8,128)S(1)} %all-to-all-done.1.velocity, f32[4,16,8,128]{3,2,1,0:T(8,128)S(1)} %collective-permute-done.first, f32[4,16,8,128]{3,2,1,0:T(8,128)S(1)} %collective-permute-done.1.second, ...), custom_call_target="tpu_custom_call" | custom-call | bytes 12713984 | tf_op jit(solution)/shard_map/momentum_kernel/pallas_call | solution.py:363
  77.3 1.3 %collective-permute-start.5 = (f32[8,16,8,128]{3,2,1,0:T(8,128)S(1)}, f32[8,16,8,128]{3,2,1,0:T(8,128)S(1)}, u32[]{:S(2)}, u32[]{:S(2)}) collective-permute-start(f32[8,16,8,128]{3,2,1,0:T(8,128)S(1)} %get-tuple-element.51.source), channel_id=1, source_target_pairs={{0,127},{1,2},{2,1},{3,4},{4,3},{5,6},{6,5},{7,8},{8,7},{9,10},{10... | collective-permute-start | bytes 1572872 | tf_op jit(solution)/shard_map/ppermute | solution.py:380
  78.6 2.7 %collective-permute-done.7.second = f32[6,16,8,128]{3,2,1,0:T(8,128)S(1)} collective-permute-done((f32[6,16,8,128]{3,2,1,0:T(8,128)S(1)}, f32[6,16,8,128]{3,2,1,0:T(8,128)S(1)}, u32[]{:S(2)}, u32[]{:S(2)}) %collective-permute-start.7) | collective-permute-done | bytes 393248 | tf_op jit(solution)/shard_map/ppermute | solution.py:380
  81.3 1.5 %outer_kernel.1.weights = f32[22,6,16,8,128]{4,3,2,1,0:T(8,128)S(1)} custom-call(f32[12,16,8,128]{3,2,1,0:T(8,128)S(1)} %get-tuple-element.50.voids_near, f32[6,16,8,128]{3,2,1,0:T(8,128)S(1)} %collective-permute-done.6.first, f32[6,16,8,128]{3,2,1,0:T(8,128)S(1)} %collective-permute-done.7.second, ...), custom_call_target="tpu_custom_call" | custom-call | flops 6000000000 | bytes 14155776 | tf_op jit(solution)/shard_map/outer_kernel/pallas_call | solution.py:363
  82.8 8.8 %collective-permute-done.5.second = f32[8,16,8,128]{3,2,1,0:T(8,128)S(1)} collective-permute-done((f32[8,16,8,128]{3,2,1,0:T(8,128)S(1)}, f32[8,16,8,128]{3,2,1,0:T(8,128)S(1)}, u32[]{:S(2)}, u32[]{:S(2)}) %collective-permute-start.5) | collective-permute-done | bytes 524320 | tf_op jit(solution)/shard_map/ppermute | solution.py:380
  91.6 5.5 %sweep_kernel.1 = (f32[16,8,8,128]{3,2,1,0:T(8,128)S(1)}, f32[10,16,8,128]{3,2,1,0:T(8,128)S(1)}) custom-call(f32[8,16,8,128]{3,2,1,0:T(8,128)S(1)} %get-tuple-element.51.source, f32[8,16,8,128]{3,2,1,0:T(8,128)S(1)} %collective-permute-done.4.first, f32[8,16,8,128]{3,2,1,0:T(8,128)S(1)} %collective-permute-done.5.second, ...), custom_call_target="tpu_custom_call" | custom-call | bytes 11403264 | tf_op jit(solution)/shard_map/sweep_kernel/pallas_call | solution.py:363
  97.1 15.7 %all_to_all.20 = f32[16,8,8,128]{3,2,1,0:T(8,128)} all-to-all(f32[16,8,8,128]{3,2,1,0:T(8,128)S(1)} %get-tuple-element.54), channel_id=1, replica_groups=mesh['gx'=16,'gy'=8] {'gx'}, dimensions={0} | all-to-all | bytes 1048576 | tf_op jit(solution)/shard_map/all_to_all | solution.py:445
  112.8 4.3 %all-to-all-start.3 = ((f32[16,8,8,128]{3,2,1,0:T(8,128)}), f32[16,8,8,128]{3,2,1,0:T(8,128)S(1)}, u32[]{:S(2)}, u32[]{:S(2)}) async-start(f32[16,8,8,128]{3,2,1,0:T(8,128)} %all_to_all.20), calls=%async_computation.3 | async-start | bytes 1048576 | tf_op jit(solution)/shard_map/all_to_all | solution.py:446
  117.1 2.6 %correct_kernel.1 = (f32[3,8,8,2048]{3,2,1,0:T(8,128)}, f32[3,8,8,2048]{3,2,1,0:T(8,128)}) custom-call(f32[10,16,8,128]{3,2,1,0:T(8,128)S(1)} %get-tuple-element.55.near_pressure, f32[3,8,16,8,128]{4,3,2,1,0:T(8,128)S(1)} %get-tuple-element.56.predicted), custom_call_target="tpu_custom_call" | custom-call | bytes 5373952 | tf_op jit(solution)/shard_map/correct_kernel/pallas_call | solution.py:363
  119.7 6.6 %all-to-all-done.3 = f32[16,8,8,128]{3,2,1,0:T(8,128)S(1)} async-done(((f32[16,8,8,128]{3,2,1,0:T(8,128)}), f32[16,8,8,128]{3,2,1,0:T(8,128)S(1)}, u32[]{:S(2)}, u32[]{:S(2)}) %all-to-all-start.3) | async-done | bytes 524320 | tf_op jit(solution)/shard_map/all_to_all | solution.py:446
  126.3 0.9 copy.7
  (26 shorter events, 0.5 us)
Async XLA Ops:
  0.6 1.4 %copy-start = (f32[3,8,128,128]{3,2,1,0:T(8,128)S(1)}, f32[3,8,128,128]{3,2,1,0:T(8,128)}, u32[]{:S(2)}) copy-start(f32[3,8,128,128]{3,2,1,0:T(8,128)} %velocity.2) | copy-start | bytes 4718596
  3.3 6.5 %copy-start.1 = (f32[3,8,8,2048]{3,2,1,0:T(8,128)S(1)}, f32[3,8,8,2048]{3,2,1,0:T(8,128)}, u32[]{:S(2)}) copy-start(f32[3,8,8,2048]{3,2,1,0:T(8,128)} %velocity.3) | copy-start | bytes 4718596
  3.3 6.5 %copy-start.2 = (s32[8,8,2048]{2,1,0:T(8,128)S(1)}, s32[8,8,2048]{2,1,0:T(8,128)}, u32[]{:S(2)}) copy-start(s32[8,8,2048]{2,1,0:T(8,128)} %count.1) | copy-start | bytes 1572868
  3.3 6.5 %copy-start.3 = (f32[8,8,2048]{2,1,0:T(8,128)S(1)}, f32[8,8,2048]{2,1,0:T(8,128)}, u32[]{:S(2)}) copy-start(f32[8,8,2048]{2,1,0:T(8,128)} %drag.1) | copy-start | bytes 1572868
  3.3 27.0 %all-to-all-start = ((f32[8,2,3,8,8,128]{5,4,3,2,1,0:T(8,128)}), f32[8,2,3,8,8,128]{5,4,3,2,1,0:T(8,128)}, u32[]{:S(2)}, u32[]{:S(2)}) async-start(f32[8,2,3,8,8,128]{5,4,3,2,1,0:T(8,128)} %block_kernel.1), calls=%async_computation | async-start | bytes 3145728 | tf_op jit(solution)/shard_map/all_to_all | solution.py:404
  10.5 1.1 copy-start.4
  11.6 0.8 copy-start.6
  12.4 0.8 copy-start.8
  13.2 0.7 copy-start.11
  13.9 0.7 copy-start.12
  14.6 15.7 %copy-start.10 = (f32[6,16,8,128]{3,2,1,0:T(8,128)}, f32[6,16,8,128]{3,2,1,0:T(8,128)S(1)}, u32[]{:S(2)}) copy-start(f32[6,16,8,128]{3,2,1,0:T(8,128)S(1)} %get-tuple-element.52) | copy-start | bytes 1179652
  30.3 30.9 %all-to-all-start.1 = ((f32[16,3,8,8,128]{4,3,2,1,0:T(8,128)}), f32[16,3,8,8,128]{4,3,2,1,0:T(8,128)S(1)}, u32[]{:S(2)}, u32[]{:S(2)}) async-start(f32[16,3,8,8,128]{4,3,2,1,0:T(8,128)} %bitcast), calls=%async_computation.1 | async-start | bytes 3145728 | tf_op jit(solution)/shard_map/all_to_all | solution.py:408
  37.1 31.9 %copy-start.5 = (f32[3,8,16,8,128]{4,3,2,1,0:T(8,128)S(1)}, f32[3,8,16,8,128]{4,3,2,1,0:T(8,128)}, u32[]{:S(2)}) copy-start(f32[3,8,16,8,128]{4,3,2,1,0:T(8,128)} %copy-done.4) | copy-start | bytes 4718596
  37.1 27.6 %collective-permute-start.2 = (f32[4,16,8,128]{3,2,1,0:T(8,128)}, f32[4,16,8,128]{3,2,1,0:T(8,128)}, u32[]{:S(2)}, u32[]{:S(2)}) collective-permute-start(f32[4,16,8,128]{3,2,1,0:T(8,128)} %copy-done.12), channel_id=1, source_target_pairs={{0,1},{1,0},{2,3},{3,2},{4,5},{5,4},{6,7},{7,6},{8,9},{9,8},{10,11... | collective-permute-start | bytes 786440 | tf_op jit(solution)/shard_map/ppermute | solution.py:380
  38.0 30.9 %collective-permute-start.3 = (f32[4,16,8,128]{3,2,1,0:T(8,128)}, f32[4,16,8,128]{3,2,1,0:T(8,128)}, u32[]{:S(2)}, u32[]{:S(2)}) collective-permute-start(f32[4,16,8,128]{3,2,1,0:T(8,128)} %copy-done.11), channel_id=1, source_target_pairs={{0,127},{1,2},{2,1},{3,4},{4,3},{5,6},{6,5},{7,8},{8,7},{9,10},{10... | collective-permute-start | bytes 786440 | tf_op jit(solution)/shard_map/ppermute | solution.py:380
  61.2 12.0 %collective-permute-start = (f32[4,16,8,128]{3,2,1,0:T(8,128)S(1)}, f32[4,16,8,128]{3,2,1,0:T(8,128)S(1)}, u32[]{:S(2)}, u32[]{:S(2)}) collective-permute-start(f32[4,16,8,128]{3,2,1,0:T(8,128)S(1)} %get-tuple-element.38), channel_id=1, source_target_pairs={{0,1},{1,0},{2,3},{3,2},{4,5},{5,4},{6,7},{7,6},{8,9},{9,8},{10,11... | collective-permute-start | bytes 786440 | tf_op jit(solution)/shard_map/ppermute | solution.py:380
  61.7 13.2 %collective-permute-start.1 = (f32[4,16,8,128]{3,2,1,0:T(8,128)S(1)}, f32[4,16,8,128]{3,2,1,0:T(8,128)S(1)}, u32[]{:S(2)}, u32[]{:S(2)}) collective-permute-start(f32[4,16,8,128]{3,2,1,0:T(8,128)S(1)} %get-tuple-element.39), channel_id=1, source_target_pairs={{0,127},{1,2},{2,1},{3,4},{4,3},{5,6},{6,5},{7,8},{8,7},{9,10},{10... | collective-permute-start | bytes 786440 | tf_op jit(solution)/shard_map/ppermute | solution.py:380
  62.1 16.5 %collective-permute-start.6 = (f32[6,16,8,128]{3,2,1,0:T(8,128)}, f32[6,16,8,128]{3,2,1,0:T(8,128)S(1)}, u32[]{:S(2)}, u32[]{:S(2)}) collective-permute-start(f32[6,16,8,128]{3,2,1,0:T(8,128)} %copy-done.10), channel_id=1, source_target_pairs={{0,1},{1,0},{2,3},{3,2},{4,5},{5,4},{6,7},{7,6},{8,9},{9,8},{10,11... | collective-permute-start | bytes 1179656 | tf_op jit(solution)/shard_map/ppermute | solution.py:380
  64.7 16.6 %collective-permute-start.7 = (f32[6,16,8,128]{3,2,1,0:T(8,128)S(1)}, f32[6,16,8,128]{3,2,1,0:T(8,128)S(1)}, u32[]{:S(2)}, u32[]{:S(2)}) collective-permute-start(f32[6,16,8,128]{3,2,1,0:T(8,128)S(1)} %get-tuple-element.53), channel_id=1, source_target_pairs={{0,127},{1,2},{2,1},{3,4},{4,3},{5,6},{6,5},{7,8},{8,7},{9,10},{10... | collective-permute-start | bytes 1179656 | tf_op jit(solution)/shard_map/ppermute | solution.py:380
  68.9 1.0 copy-start.7
  70.0 1.0 copy-start.9
  77.3 14.3 %collective-permute-start.5 = (f32[8,16,8,128]{3,2,1,0:T(8,128)S(1)}, f32[8,16,8,128]{3,2,1,0:T(8,128)S(1)}, u32[]{:S(2)}, u32[]{:S(2)}) collective-permute-start(f32[8,16,8,128]{3,2,1,0:T(8,128)S(1)} %get-tuple-element.51.source), channel_id=1, source_target_pairs={{0,127},{1,2},{2,1},{3,4},{4,3},{5,6},{6,5},{7,8},{8,7},{9,10},{10... | collective-permute-start | bytes 1572872 | tf_op jit(solution)/shard_map/ppermute | solution.py:380
  78.6 13.0 %collective-permute-start.4 = (f32[8,16,8,128]{3,2,1,0:T(8,128)S(1)}, f32[8,16,8,128]{3,2,1,0:T(8,128)S(1)}, u32[]{:S(2)}, u32[]{:S(2)}) collective-permute-start(f32[8,16,8,128]{3,2,1,0:T(8,128)S(1)} %get-tuple-element.51.source), channel_id=1, source_target_pairs={{0,1},{1,0},{2,3},{3,2},{4,5},{5,4},{6,7},{7,6},{8,9},{9,8},{10,11... | collective-permute-start | bytes 1572872 | tf_op jit(solution)/shard_map/ppermute | solution.py:380
  112.8 13.5 %all-to-all-start.3 = ((f32[16,8,8,128]{3,2,1,0:T(8,128)}), f32[16,8,8,128]{3,2,1,0:T(8,128)S(1)}, u32[]{:S(2)}, u32[]{:S(2)}) async-start(f32[16,8,8,128]{3,2,1,0:T(8,128)} %all_to_all.20), calls=%async_computation.3 | async-start | bytes 1048576 | tf_op jit(solution)/shard_map/all_to_all | solution.py:446

commit v4 on v3

--- a/solution.py
+++ b/solution.py
@@ -1,5 +1,3 @@
-import functools
-
 import jax
 import jax.numpy as jnp
 from jax import lax
@@ -19,6 +17,7 @@
 LANES = 128
 TILE = (PLANES, LANES)
 WIDE = 3 * ROWS
+HALF = ROWS // 2
 COVER = 6_000_000_000
 AXES = ("gx", "gy")
 f32 = jnp.float32
@@ -224,7 +223,7 @@
 
 
 def momentum_kernel(
-    velocity, first, second, weights, inverse_sum, centre, spread, given, voids_near, predicted, source, wide, flux
+    velocity, first, second, weights, inverse_sum, centre, spread, given, voids_near, predicted, source, first_half, second_half, wide, flux
 ):
     for message, side in ((first, Side(True)), (second, Side(False))):
         pair = side.at(ROWS + 2, 0)
@@ -282,57 +281,93 @@
                 )
                 source[row, g] = change * inverse_sum[row, g]
 
-
-def sweep_kernel(source, first, second, weights, pressure, near_pressure, source_wide, one, other):
-    sides = Side(True).at(2 * ROWS, 0), Side(False).at(2 * ROWS, 0)
-    there = Side(True).there, Side(False).there
-
-    @pl.loop(0, ROWS, step=2)
+    upper = Side(True).at(HALF, 0)
+    first_half[...] = source[pl.ds(upper, HALF)]
+    second_half[...] = source[pl.ds(HALF - upper, HALF)]
+
+
+def sweep_row(weights, at, source, now, row, store):
+    tiles = [now[row, g] for g in range(GROUPS)]
+    ups, downs = column_neighbours(tiles)
+    for g in range(GROUPS):
+        around = weighted_sum(weights, at, g, tiles[g], ups[g], downs[g], now[row + 1, g], now[row - 1, g])
+        store(g, around - source[g])
+
+
+def inner_kernel(source, first, second, weights, near_source, edges, middle, one, other):
+    for message, side in ((first, Side(True)), (second, Side(False))):
+        at = side.at(HALF + ROWS, 0)
+        for row in range(HALF):
+            near_source[at + row] = message[row] * side.there
+    near_source[HALF : HALF + ROWS] = source[...]
+
+    @pl.loop(0, 2 * ROWS, step=2)
     def _(start):
         for row in (start, start + 1):
-            for at, value in (
-                (sides[0] + row, first[row] * there[0]),
-                (sides[1] + row, second[row] * there[1]),
-                (ROWS + row, source[row]),
-            ):
-                source_wide[at] = value
-                one[at] = -value
-
-    def sweep_row(row, now, store):
-        tiles = [now[row, g] for g in range(GROUPS)]
-        ups, downs = column_neighbours(tiles)
-        for g in range(GROUPS):
-            around = weighted_sum(weights, row - 1, g, tiles[g], ups[g], downs[g], now[row + 1, g], now[row - 1, g])
-            store(row, g, around - source_wide[row, g])
+            one[row] = -near_source[row]
 
     now, later = one, other
-    for sweep in range(1, SWEEPS - 1):
-        half = (WIDE - 2 * sweep) // 2
+    for sweep in range(1, SWEEPS):
+        edges[sweep - 1, 0:2] = now[sweep - 1 : sweep + 1]
+        edges[sweep - 1, 2:4] = now[2 * ROWS - 1 - sweep : 2 * ROWS + 1 - sweep]
+        half = ROWS - sweep
 
         def half_sweep(start, now=now, later=later, half=half):
-            def store(row, g, value):
-                later[row, g] = value
-
-            for row in range(half):
-                sweep_row(start + row, now, store)
-
-        pl.loop(sweep, WIDE - sweep, step=half)(half_sweep)
+            for n in range(half):
+                row = start + n
+
+                def store(g, value, row=row):
+                    later[row, g] = value
+
+                sweep_row(weights, row + HALF - 1, near_source.at[row], now, row, store)
+
+        pl.loop(sweep, 2 * ROWS - sweep, step=half)(half_sweep)
         now, later = later, now
-
-    def keep(row, g, value):
-        near_pressure[row - (ROWS - 1), g] = value
-
-    @pl.loop(0, ROWS, step=4)
-    def _(start):
-        def store(row, g, value):
-            keep(row, g, value)
-            pressure[g, row - ROWS] = value
-
-        for row in range(4):
-            sweep_row(ROWS + start + row, now, store)
-
-    for row in (ROWS - 1, 2 * ROWS):
-        sweep_row(row, now, keep)
+    middle[...] = now[ROWS - 1 : ROWS + 1]
+
+
+def rim_kernel(near_source, first, second, edges, middle, weights, pressure, near_pressure, source_wide, low, high):
+    for message, side in ((first, Side(True)), (second, Side(False))):
+        at = side.at(HALF + 2 * ROWS, 0)
+        for row in range(HALF):
+            source_wide[at + row] = message[row] * side.there
+
+    @pl.loop(0, 2 * ROWS, step=2)
+    def _(start):
+        for row in (start, start + 1):
+            source_wide[HALF + row] = near_source[row]
+
+    for row in range(HALF):
+        low[0, row] = -source_wide[row]
+        high[0, row + 2] = -source_wide[WIDE - HALF + row]
+
+    @pl.loop(1, SWEEPS)
+    def _(sweep):
+        now = lax.rem(sweep + 1, 2)
+        later = 1 - now
+        for n in range(2):
+            low[now, HALF + n] = edges[sweep - 1, n]
+            high[now, n] = edges[sweep - 1, 2 + n]
+        for n in range(HALF):
+
+            def store_low(g, value, n=n):
+                low[later, n, g] = value
+
+            def store_high(g, value, n=n):
+                high[later, n + 2, g] = value
+
+            row = sweep + n
+            sweep_row(weights, row - 1, source_wide.at[row], low.at[now], n + 1, store_low)
+            row = WIDE - HALF - sweep + n
+            sweep_row(weights, row - 1, source_wide.at[row], high.at[now], n + 1, store_high)
+
+    last = (SWEEPS - 1) % 2
+    rows = [low.at[last, n] for n in range(HALF)] + [middle.at[n] for n in range(2)]
+    rows = rows + [high.at[last, n + 2] for n in range(HALF)]
+    for n, row in enumerate(rows):
+        near_pressure[n] = row[...]
+        if 0 < n <= ROWS:
+            pressure[:, n - 1] = row[...]
 
 
 def correct_kernel(near_pressure, predicted, velocity, slopes):
@@ -375,8 +410,7 @@
 def swap(first, second):
     devices = lax.axis_size("gx") * lax.axis_size("gy")
     inner = [(d, d ^ 1) for d in range(devices)]
-    outer = [(d, (((d + 1) % devices) ^ 1) - 1) for d in range(devices)]
-    outer = [(a, b % devices) for a, b in outer]
+    outer = [(d, ((((d + 1) % devices) ^ 1) - 1) % devices) for d in range(devices)]
     return lax.ppermute(first, AXES, inner), lax.ppermute(second, AXES, outer)
 
 
@@ -417,10 +451,10 @@
     *edges, first_far, second_far = lax.optimization_barrier((*edges, first_far, second_far))
     first, second = swap(*edges)
     first_far, second_far = swap(first_far, second_far)
-    predicted, source = call(
+    predicted, source, first_half, second_half = call(
         momentum_kernel,
         (slab, first, second, near_weights, inverse_sum, centre, spread, given, voids_near),
-        [(3,) + own, own],
+        [(3,) + own, own, (HALF,) + field, (HALF,) + field],
         [(3, ROWS + 4) + field, (2,) + near],
     )
     (weights,) = call(
@@ -430,12 +464,21 @@
         [(WIDE,) + field],
         flops=COVER,
     )
-    first, second = swap(source, source)
+    first, second = swap(first_half, second_half)
+    second_half, first_half, weights = lax.optimization_barrier((second_half, first_half, weights))
+    first_far, second_far = swap(second_half, first_half)
+    near_source, edges, middle = call(
+        inner_kernel,
+        (source, first, second, weights),
+        [(2 * ROWS,) + field, (SWEEPS - 1, 4) + field, (2,) + field],
+        [(2 * ROWS,) + field] * 2,
+        flops=COVER,
+    )
     pressure, near_pressure = call(
-        sweep_kernel,
-        (source, first, second, weights),
+        rim_kernel,
+        (near_source, first_far, second_far, edges, middle, weights),
         [(GROUPS, ROWS, PLANES, LANES), near],
-        [(WIDE,) + field] * 3,
+        [(WIDE,) + field, (2, HALF + 2) + field, (2, HALF + 2) + field],
     )
 
     velocity, slopes = call(

time: 128 us -> 128 us (level)
  waiting for transfers between devices: 53.3 us -> 49 us
  starting transfers between devices: 32.9 us -> 35.7 us
  Pallas kernels: 16 us -> 17.7 us
    ppermute x8 -> x10, waiting for transfers between devices: 13.3 us -> 8.83 us  [swap(): return (lax.ppermute(first, AXES, inner), lax.ppermute(second, AXES, outer))]
    ppermute x8 -> x10, starting transfers between devices: 15.4 us -> 19 us  [swap(): return (lax.ppermute(first, AXES, inner), lax.ppermute(second, AXES, outer))]
    pallas_call x8 -> x9, Pallas kernels: 16 us -> 17.7 us  [call(): pl.pallas_call(kernel, out_shape=shapes, in_specs=[spec] * len(args), out...]
  transfers between devices with their start and end apart: 11 -> 13, of which waited for: 6 -> 7; matrix products, arithmetic and copies ran while one was open for 0% -> 0% of each run, Pallas kernels for 7% -> 10%
where the time goes in v4:
time: 128 us; the launch traced here: 127 us
  waiting for transfers between devices  49 us (38%)
  starting transfers between devices  35.7 us (28%)
  Pallas kernels  17.7 us (14%)
  blocking collectives  15.6 us (12%)
  local copies, waits for them, and re-layouts  8.55 us (7%)
    ppermute x10, starting transfers between devices, swap(): return (lax.ppermute(first, AXES, inner), lax.ppermute(second, AXES, outer))  19 us
    all_to_all x1, waiting for transfers between devices, shards(): slab = lax.all_to_all(blocks, 'gx', split_axis=0, concat_axis=0, tiled=True)  17.7 us
    pallas_call x9, Pallas kernels, call(): pl.pallas_call(kernel, out_shape=shapes, in_specs=[spec] * len(args), out...  17.7 us
    all_to_all x1, waiting for transfers between devices, shards(): lax.all_to_all(blocks, 'gy', split_axis=0, concat_axis=0, tiled=True)  15.7 us
    all_to_all x1, blocking collectives, shards(): lax.all_to_all(pressure, 'gx', split_axis=0, concat_axis=0, tiled=True)  15.6 us
    ppermute x10, waiting for transfers between devices, swap(): return (lax.ppermute(first, AXES, inner), lax.ppermute(second, AXES, outer))  8.83 us
    unnamed x26, local copies, waits for them, and re-layouts  7.67 us
    all_to_all x1, waiting for transfers between devices, shards(): lax.all_to_all(pressure, 'gy', split_axis=0, concat_axis=0, tiled=True)  6.79 us
  transfers between devices with their start and end apart: 13, of which 7 were waited for; matrix products, arithmetic and copies ran while one was open for 0% of the time, Pallas kernels for 10%

profile of v4, /device:TPU:0, one launch (start us, length us, event | category | flops | bytes accessed | tf_op | source)
XLA Modules:
  0.0 127.4 jit_solution(5998080610740053975)
XLA Ops:
  0.6 1.4 %copy-done = f32[3,8,128,128]{3,2,1,0:T(8,128)S(1)} copy-done((f32[3,8,128,128]{3,2,1,0:T(8,128)S(1)}, f32[3,8,128,128]{3,2,1,0:T(8,128)}, u32[]{:S(2)}) %copy-start) | copy-done | bytes 1572888
  2.0 1.2 block_kernel.1
  3.3 6.5 %all-to-all-start = ((f32[8,2,3,8,8,128]{5,4,3,2,1,0:T(8,128)}), f32[8,2,3,8,8,128]{5,4,3,2,1,0:T(8,128)}, u32[]{:S(2)}, u32[]{:S(2)}) async-start(f32[8,2,3,8,8,128]{5,4,3,2,1,0:T(8,128)} %block_kernel.1), calls=%async_computation | async-start | bytes 3145728 | tf_op jit(solution)/shard_map/all_to_all | solution.py:438
  10.5 1.1 copy-done.4
  11.6 0.8 copy-done.6
  12.4 0.8 copy-done.8
  13.2 0.7 copy-done.11
  13.9 0.7 copy-done.12
  14.6 15.7 %all-to-all-done = f32[8,2,3,8,8,128]{5,4,3,2,1,0:T(8,128)} async-done(((f32[8,2,3,8,8,128]{5,4,3,2,1,0:T(8,128)}), f32[8,2,3,8,8,128]{5,4,3,2,1,0:T(8,128)}, u32[]{:S(2)}, u32[]{:S(2)}) %all-to-all-start) | async-done | bytes 1572896 | tf_op jit(solution)/shard_map/all_to_all | solution.py:438
  30.3 6.7 %all-to-all-start.1 = ((f32[16,3,8,8,128]{4,3,2,1,0:T(8,128)}), f32[16,3,8,8,128]{4,3,2,1,0:T(8,128)S(1)}, u32[]{:S(2)}, u32[]{:S(2)}) async-start(f32[16,3,8,8,128]{4,3,2,1,0:T(8,128)} %bitcast), calls=%async_computation.1 | async-start | bytes 3145728 | tf_op jit(solution)/shard_map/all_to_all | solution.py:442
  37.1 0.9 collective-permute-start.2
  38.0 5.4 %collective-permute-start.3 = (f32[4,16,8,128]{3,2,1,0:T(8,128)}, f32[4,16,8,128]{3,2,1,0:T(8,128)}, u32[]{:S(2)}, u32[]{:S(2)}) collective-permute-start(f32[4,16,8,128]{3,2,1,0:T(8,128)} %copy-done.11), channel_id=1, source_target_pairs={{0,127},{1,2},{2,1},{3,4},{4,3},{5,6},{6,5},{7,8},{8,7},{9,10},{10... | collective-permute-start | bytes 786440 | tf_op jit(solution)/shard_map/ppermute | solution.py:414
  43.4 17.7 %all-to-all-done.1.velocity = f32[16,3,8,8,128]{4,3,2,1,0:T(8,128)S(1)} async-done(((f32[16,3,8,8,128]{4,3,2,1,0:T(8,128)}), f32[16,3,8,8,128]{4,3,2,1,0:T(8,128)S(1)}, u32[]{:S(2)}, u32[]{:S(2)}) %all-to-all-start.1) | async-done | bytes 1572896 | tf_op jit(solution)/shard_map/all_to_all | solution.py:442
  62.1 2.6 %collective-permute-start.6 = (f32[6,16,8,128]{3,2,1,0:T(8,128)}, f32[6,16,8,128]{3,2,1,0:T(8,128)S(1)}, u32[]{:S(2)}, u32[]{:S(2)}) collective-permute-start(f32[6,16,8,128]{3,2,1,0:T(8,128)} %copy-done.10), channel_id=1, source_target_pairs={{0,1},{1,0},{2,3},{3,2},{4,5},{5,4},{6,7},{7,6},{8,9},{9,8},{10,11... | collective-permute-start | bytes 1179656 | tf_op jit(solution)/shard_map/ppermute | solution.py:414
  64.7 4.2 %collective-permute-start.7 = (f32[6,16,8,128]{3,2,1,0:T(8,128)S(1)}, f32[6,16,8,128]{3,2,1,0:T(8,128)S(1)}, u32[]{:S(2)}, u32[]{:S(2)}) collective-permute-start(f32[6,16,8,128]{3,2,1,0:T(8,128)S(1)} %get-tuple-element.63), channel_id=1, source_target_pairs={{0,127},{1,2},{2,1},{3,4},{4,3},{5,6},{6,5},{7,8},{8,7},{9,10},{10... | collective-permute-start | bytes 1179656 | tf_op jit(solution)/shard_map/ppermute | solution.py:414
  68.9 1.0 copy-done.7
  70.0 1.0 copy-done.9
  71.0 2.2 %coefficient_kernel.1 = (f32[10,6,16,8,128]{4,3,2,1,0:T(8,128)S(1)}, f32[8,16,8,128]{3,2,1,0:T(8,128)S(1)}, f32[10,16,8,128]{3,2,1,0:T(8,128)S(1)}, f32[10,16,8,...) custom-call(f32[8,16,8,128]{3,2,1,0:T(8,128)S(1)} %copy-done.7, ...), custom_call_target="tpu_custom_call" | custom-call | flops 6000000000 | bytes 11665408 | tf_op jit(solution)/shard_map/coefficient_kernel/pallas_call | solution.py:398
  73.3 1.7 %collective-permute-done.1.second = f32[4,16,8,128]{3,2,1,0:T(8,128)S(1)} collective-permute-done((f32[4,16,8,128]{3,2,1,0:T(8,128)S(1)}, f32[4,16,8,128]{3,2,1,0:T(8,128)S(1)}, u32[]{:S(2)}, u32[]{:S(2)}) %collective-permute-start.1) | collective-permute-done | bytes 262176 | tf_op jit(solution)/shard_map/ppermute | solution.py:414
  75.0 2.3 %momentum_kernel.1 = (f32[3,8,16,8,128]{4,3,2,1,0:T(8,128)S(1)}, f32[8,16,8,128]{3,2,1,0:T(8,128)S(1)}, f32[4,16,8,128]{3,2,1,0:T(8,128)S(1)}, f32[4,16,8,128]{3,2,1,0:T(8,128)S(1)}) custom-call(f32[16,3,8,8,128]{4,3,2,1,0:T(8,128)S(1)} %all-to-all-done.1.velocity, f32[4,16,8,128]{3,2,1,0:T(8,128)S(1)} %collective-permute-done.first, ...), custom_call_target="tpu_custom_call" | custom-call | bytes 13238272 | tf_op jit(solution)/shard_map/momentum_kernel/pallas_call | solution.py:398
  77.4 1.3 %collective-permute-start.5 = (f32[4,16,8,128]{3,2,1,0:T(8,128)S(1)}, f32[4,16,8,128]{3,2,1,0:T(8,128)S(1)}, u32[]{:S(2)}, u32[]{:S(2)}) collective-permute-start(f32[4,16,8,128]{3,2,1,0:T(8,128)S(1)} %get-tuple-element.66), channel_id=1, source_target_pairs={{0,127},{1,2},{2,1},{3,4},{4,3},{5,6},{6,5},{7,8},{8,7},{9,10},{10... | collective-permute-start | bytes 786440 | tf_op jit(solution)/shard_map/ppermute | solution.py:414
  78.7 2.6 %collective-permute-done.7.second = f32[6,16,8,128]{3,2,1,0:T(8,128)S(1)} collective-permute-done((f32[6,16,8,128]{3,2,1,0:T(8,128)S(1)}, f32[6,16,8,128]{3,2,1,0:T(8,128)S(1)}, u32[]{:S(2)}, u32[]{:S(2)}) %collective-permute-start.7) | collective-permute-done | bytes 393248 | tf_op jit(solution)/shard_map/ppermute | solution.py:414
  81.3 1.5 %outer_kernel.1.weights = f32[22,6,16,8,128]{4,3,2,1,0:T(8,128)S(1)} custom-call(f32[12,16,8,128]{3,2,1,0:T(8,128)S(1)} %get-tuple-element.58.voids_near, f32[6,16,8,128]{3,2,1,0:T(8,128)S(1)} %collective-permute-done.6.first, f32[6,16,8,128]{3,2,1,0:T(8,128)S(1)} %collective-permute-done.7.second, ...), custom_call_target="tpu_custom_call" | custom-call | flops 6000000000 | bytes 14155776 | tf_op jit(solution)/shard_map/outer_kernel/pallas_call | solution.py:398
  82.9 3.4 %collective-permute-start.9 = (f32[4,16,8,128]{3,2,1,0:T(8,128)S(1)}, f32[4,16,8,128]{3,2,1,0:T(8,128)S(1)}, u32[]{:S(2)}, u32[]{:S(2)}) collective-permute-start(f32[4,16,8,128]{3,2,1,0:T(8,128)S(1)} %get-tuple-element.67), channel_id=1, source_target_pairs={{0,127},{1,2},{2,1},{3,4},{4,3},{5,6},{6,5},{7,8},{8,7},{9,10},{10... | collective-permute-start | bytes 786440 | tf_op jit(solution)/shard_map/ppermute | solution.py:414
  86.3 4.4 %collective-permute-done.5.second = f32[4,16,8,128]{3,2,1,0:T(8,128)S(1)} collective-permute-done((f32[4,16,8,128]{3,2,1,0:T(8,128)S(1)}, f32[4,16,8,128]{3,2,1,0:T(8,128)S(1)}, u32[]{:S(2)}, u32[]{:S(2)}) %collective-permute-start.5) | collective-permute-done | bytes 262176 | tf_op jit(solution)/shard_map/ppermute | solution.py:414
  90.7 3.4 %inner_kernel.1 = (f32[16,16,8,128]{3,2,1,0:T(8,128)S(1)}, f32[7,4,16,8,128]{4,3,2,1,0:T(8,128)S(1)}, f32[2,16,8,128]{3,2,1,0:T(8,128)S(1)}) custom-call(f32[8,16,8,128]{3,2,1,0:T(8,128)S(1)} %get-tuple-element.59.source, f32[4,16,8,128]{3,2,1,0:T(8,128)S(1)} %collective-permute-done.4.first, f32[4,16,8,128]{3,2,1,0:T(8,128)S(1)} %collective-permute-done.5.second, ...), custom_call_target="tpu_custom_call" | custom-call | flops 6000000000 | bytes 12713984 | tf_op jit(solution)/shard_map/inner_kernel/pallas_call | solution.py:398
  94.2 3.8 %rim_kernel.1 = (f32[16,8,8,128]{3,2,1,0:T(8,128)S(1)}, f32[10,16,8,128]{3,2,1,0:T(8,128)S(1)}) custom-call(f32[16,16,8,128]{3,2,1,0:T(8,128)S(1)} %get-tuple-element.65.near_source, f32[4,16,8,128]{3,2,1,0:T(8,128)S(1)} %collective-permute-done.8.first, f32[4,16,8,128]{3,2,1,0:T(8,128)S(1)} %collective-permute-done.9.second, ...), custom_call_target="tpu_custom_call" | custom-call | bytes 13369344 | tf_op jit(solution)/shard_map/rim_kernel/pallas_call | solution.py:398
  98.0 15.6 %all_to_all.20 = f32[16,8,8,128]{3,2,1,0:T(8,128)} all-to-all(f32[16,8,8,128]{3,2,1,0:T(8,128)S(1)} %get-tuple-element.70), channel_id=1, replica_groups=mesh['gx'=16,'gy'=8] {'gx'}, dimensions={0} | all-to-all | bytes 1048576 | tf_op jit(solution)/shard_map/all_to_all | solution.py:488
  113.6 3.5 %all-to-all-start.3 = ((f32[16,8,8,128]{3,2,1,0:T(8,128)}), f32[16,8,8,128]{3,2,1,0:T(8,128)S(1)}, u32[]{:S(2)}, u32[]{:S(2)}) async-start(f32[16,8,8,128]{3,2,1,0:T(8,128)} %all_to_all.20), calls=%async_computation.3 | async-start | bytes 1048576 | tf_op jit(solution)/shard_map/all_to_all | solution.py:489
  117.2 2.6 %correct_kernel.1 = (f32[3,8,8,2048]{3,2,1,0:T(8,128)}, f32[3,8,8,2048]{3,2,1,0:T(8,128)}) custom-call(f32[10,16,8,128]{3,2,1,0:T(8,128)S(1)} %get-tuple-element.71.near_pressure, f32[3,8,16,8,128]{4,3,2,1,0:T(8,128)S(1)} %get-tuple-element.72.predicted), custom_call_target="tpu_custom_call" | custom-call | bytes 5373952 | tf_op jit(solution)/shard_map/correct_kernel/pallas_call | solution.py:398
  119.7 6.8 %all-to-all-done.3 = f32[16,8,8,128]{3,2,1,0:T(8,128)S(1)} async-done(((f32[16,8,8,128]{3,2,1,0:T(8,128)}), f32[16,8,8,128]{3,2,1,0:T(8,128)S(1)}, u32[]{:S(2)}, u32[]{:S(2)}) %all-to-all-start.3) | async-done | bytes 524320 | tf_op jit(solution)/shard_map/all_to_all | solution.py:489
  126.5 0.9 copy.7
  (31 shorter events, 1.9 us)
Async XLA Ops:
  0.6 1.4 %copy-start = (f32[3,8,128,128]{3,2,1,0:T(8,128)S(1)}, f32[3,8,128,128]{3,2,1,0:T(8,128)}, u32[]{:S(2)}) copy-start(f32[3,8,128,128]{3,2,1,0:T(8,128)} %velocity.2) | copy-start | bytes 4718596
  3.3 6.5 %copy-start.1 = (f32[3,8,8,2048]{3,2,1,0:T(8,128)S(1)}, f32[3,8,8,2048]{3,2,1,0:T(8,128)}, u32[]{:S(2)}) copy-start(f32[3,8,8,2048]{3,2,1,0:T(8,128)} %velocity.3) | copy-start | bytes 4718596
  3.3 6.5 %copy-start.2 = (s32[8,8,2048]{2,1,0:T(8,128)S(1)}, s32[8,8,2048]{2,1,0:T(8,128)}, u32[]{:S(2)}) copy-start(s32[8,8,2048]{2,1,0:T(8,128)} %count.1) | copy-start | bytes 1572868
  3.3 6.5 %copy-start.3 = (f32[8,8,2048]{2,1,0:T(8,128)S(1)}, f32[8,8,2048]{2,1,0:T(8,128)}, u32[]{:S(2)}) copy-start(f32[8,8,2048]{2,1,0:T(8,128)} %drag.1) | copy-start | bytes 1572868
  3.3 27.0 %all-to-all-start = ((f32[8,2,3,8,8,128]{5,4,3,2,1,0:T(8,128)}), f32[8,2,3,8,8,128]{5,4,3,2,1,0:T(8,128)}, u32[]{:S(2)}, u32[]{:S(2)}) async-start(f32[8,2,3,8,8,128]{5,4,3,2,1,0:T(8,128)} %block_kernel.1), calls=%async_computation | async-start | bytes 3145728 | tf_op jit(solution)/shard_map/all_to_all | solution.py:438
  10.5 1.1 copy-start.4
  11.6 0.8 copy-start.6
  12.4 0.8 copy-start.8
  13.2 0.7 copy-start.11
  13.9 0.7 copy-start.12
  14.6 15.7 %copy-start.10 = (f32[6,16,8,128]{3,2,1,0:T(8,128)}, f32[6,16,8,128]{3,2,1,0:T(8,128)S(1)}, u32[]{:S(2)}) copy-start(f32[6,16,8,128]{3,2,1,0:T(8,128)S(1)} %get-tuple-element.62) | copy-start | bytes 1179652
  30.3 30.9 %all-to-all-start.1 = ((f32[16,3,8,8,128]{4,3,2,1,0:T(8,128)}), f32[16,3,8,8,128]{4,3,2,1,0:T(8,128)S(1)}, u32[]{:S(2)}, u32[]{:S(2)}) async-start(f32[16,3,8,8,128]{4,3,2,1,0:T(8,128)} %bitcast), calls=%async_computation.1 | async-start | bytes 3145728 | tf_op jit(solution)/shard_map/all_to_all | solution.py:442
  37.1 31.9 %copy-start.5 = (f32[3,8,16,8,128]{4,3,2,1,0:T(8,128)S(1)}, f32[3,8,16,8,128]{4,3,2,1,0:T(8,128)}, u32[]{:S(2)}) copy-start(f32[3,8,16,8,128]{4,3,2,1,0:T(8,128)} %copy-done.4) | copy-start | bytes 4718596
  37.1 27.6 %collective-permute-start.2 = (f32[4,16,8,128]{3,2,1,0:T(8,128)}, f32[4,16,8,128]{3,2,1,0:T(8,128)}, u32[]{:S(2)}, u32[]{:S(2)}) collective-permute-start(f32[4,16,8,128]{3,2,1,0:T(8,128)} %copy-done.12), channel_id=1, source_target_pairs={{0,1},{1,0},{2,3},{3,2},{4,5},{5,4},{6,7},{7,6},{8,9},{9,8},{10,11... | collective-permute-start | bytes 786440 | tf_op jit(solution)/shard_map/ppermute | solution.py:414
  38.0 30.9 %collective-permute-start.3 = (f32[4,16,8,128]{3,2,1,0:T(8,128)}, f32[4,16,8,128]{3,2,1,0:T(8,128)}, u32[]{:S(2)}, u32[]{:S(2)}) collective-permute-start(f32[4,16,8,128]{3,2,1,0:T(8,128)} %copy-done.11), channel_id=1, source_target_pairs={{0,127},{1,2},{2,1},{3,4},{4,3},{5,6},{6,5},{7,8},{8,7},{9,10},{10... | collective-permute-start | bytes 786440 | tf_op jit(solution)/shard_map/ppermute | solution.py:414
  61.2 12.0 %collective-permute-start = (f32[4,16,8,128]{3,2,1,0:T(8,128)S(1)}, f32[4,16,8,128]{3,2,1,0:T(8,128)S(1)}, u32[]{:S(2)}, u32[]{:S(2)}) collective-permute-start(f32[4,16,8,128]{3,2,1,0:T(8,128)S(1)} %get-tuple-element.46), channel_id=1, source_target_pairs={{0,1},{1,0},{2,3},{3,2},{4,5},{5,4},{6,7},{7,6},{8,9},{9,8},{10,11... | collective-permute-start | bytes 786440 | tf_op jit(solution)/shard_map/ppermute | solution.py:414
  61.7 13.2 %collective-permute-start.1 = (f32[4,16,8,128]{3,2,1,0:T(8,128)S(1)}, f32[4,16,8,128]{3,2,1,0:T(8,128)S(1)}, u32[]{:S(2)}, u32[]{:S(2)}) collective-permute-start(f32[4,16,8,128]{3,2,1,0:T(8,128)S(1)} %get-tuple-element.47), channel_id=1, source_target_pairs={{0,127},{1,2},{2,1},{3,4},{4,3},{5,6},{6,5},{7,8},{8,7},{9,10},{10... | collective-permute-start | bytes 786440 | tf_op jit(solution)/shard_map/ppermute | solution.py:414
  62.1 16.7 %collective-permute-start.6 = (f32[6,16,8,128]{3,2,1,0:T(8,128)}, f32[6,16,8,128]{3,2,1,0:T(8,128)S(1)}, u32[]{:S(2)}, u32[]{:S(2)}) collective-permute-start(f32[6,16,8,128]{3,2,1,0:T(8,128)} %copy-done.10), channel_id=1, source_target_pairs={{0,1},{1,0},{2,3},{3,2},{4,5},{5,4},{6,7},{7,6},{8,9},{9,8},{10,11... | collective-permute-start | bytes 1179656 | tf_op jit(solution)/shard_map/ppermute | solution.py:414
  64.7 16.6 %collective-permute-start.7 = (f32[6,16,8,128]{3,2,1,0:T(8,128)S(1)}, f32[6,16,8,128]{3,2,1,0:T(8,128)S(1)}, u32[]{:S(2)}, u32[]{:S(2)}) collective-permute-start(f32[6,16,8,128]{3,2,1,0:T(8,128)S(1)} %get-tuple-element.63), channel_id=1, source_target_pairs={{0,127},{1,2},{2,1},{3,4},{4,3},{5,6},{6,5},{7,8},{8,7},{9,10},{10... | collective-permute-start | bytes 1179656 | tf_op jit(solution)/shard_map/ppermute | solution.py:414
  68.9 1.0 copy-start.7
  70.0 1.0 copy-start.9
  77.3 9.0 %collective-permute-start.4 = (f32[4,16,8,128]{3,2,1,0:T(8,128)S(1)}, f32[4,16,8,128]{3,2,1,0:T(8,128)S(1)}, u32[]{:S(2)}, u32[]{:S(2)}) collective-permute-start(f32[4,16,8,128]{3,2,1,0:T(8,128)S(1)} %get-tuple-element.67), channel_id=1, source_target_pairs={{0,1},{1,0},{2,3},{3,2},{4,5},{5,4},{6,7},{7,6},{8,9},{9,8},{10,11... | collective-permute-start | bytes 786440 | tf_op jit(solution)/shard_map/ppermute | solution.py:414
  77.4 13.3 %collective-permute-start.5 = (f32[4,16,8,128]{3,2,1,0:T(8,128)S(1)}, f32[4,16,8,128]{3,2,1,0:T(8,128)S(1)}, u32[]{:S(2)}, u32[]{:S(2)}) collective-permute-start(f32[4,16,8,128]{3,2,1,0:T(8,128)S(1)} %get-tuple-element.66), channel_id=1, source_target_pairs={{0,127},{1,2},{2,1},{3,4},{4,3},{5,6},{6,5},{7,8},{8,7},{9,10},{10... | collective-permute-start | bytes 786440 | tf_op jit(solution)/shard_map/ppermute | solution.py:414
  82.8 11.3 %collective-permute-start.8 = (f32[4,16,8,128]{3,2,1,0:T(8,128)S(1)}, f32[4,16,8,128]{3,2,1,0:T(8,128)S(1)}, u32[]{:S(2)}, u32[]{:S(2)}) collective-permute-start(f32[4,16,8,128]{3,2,1,0:T(8,128)S(1)} %get-tuple-element.66), channel_id=1, source_target_pairs={{0,1},{1,0},{2,3},{3,2},{4,5},{5,4},{6,7},{7,6},{8,9},{9,8},{10,11... | collective-permute-start | bytes 786440 | tf_op jit(solution)/shard_map/ppermute | solution.py:414
  82.9 11.3 %collective-permute-start.9 = (f32[4,16,8,128]{3,2,1,0:T(8,128)S(1)}, f32[4,16,8,128]{3,2,1,0:T(8,128)S(1)}, u32[]{:S(2)}, u32[]{:S(2)}) collective-permute-start(f32[4,16,8,128]{3,2,1,0:T(8,128)S(1)} %get-tuple-element.67), channel_id=1, source_target_pairs={{0,127},{1,2},{2,1},{3,4},{4,3},{5,6},{6,5},{7,8},{8,7},{9,10},{10... | collective-permute-start | bytes 786440 | tf_op jit(solution)/shard_map/ppermute | solution.py:414
  113.6 12.9 %all-to-all-start.3 = ((f32[16,8,8,128]{3,2,1,0:T(8,128)}), f32[16,8,8,128]{3,2,1,0:T(8,128)S(1)}, u32[]{:S(2)}, u32[]{:S(2)}) async-start(f32[16,8,8,128]{3,2,1,0:T(8,128)} %all_to_all.20), calls=%async_computation.3 | async-start | bytes 1048576 | tf_op jit(solution)/shard_map/all_to_all | solution.py:489

commit v5 on v4

--- a/solution.py
+++ b/solution.py
@@ -296,15 +296,15 @@
 
 def inner_kernel(source, first, second, weights, near_source, edges, middle, one, other):
     for message, side in ((first, Side(True)), (second, Side(False))):
-        at = side.at(HALF + ROWS, 0)
+        at = side.at(2 * ROWS, HALF)
         for row in range(HALF):
             near_source[at + row] = message[row] * side.there
-    near_source[HALF : HALF + ROWS] = source[...]
+    near_source[ROWS : 2 * ROWS] = source[...]
 
     @pl.loop(0, 2 * ROWS, step=2)
     def _(start):
         for row in (start, start + 1):
-            one[row] = -near_source[row]
+            one[row] = -near_source[row + HALF]
 
     now, later = one, other
     for sweep in range(1, SWEEPS):
@@ -319,23 +319,18 @@
                 def store(g, value, row=row):
                     later[row, g] = value
 
-                sweep_row(weights, row + HALF - 1, near_source.at[row], now, row, store)
+                sweep_row(weights, row + HALF - 1, near_source.at[row + HALF], now, row, store)
 
         pl.loop(sweep, 2 * ROWS - sweep, step=half)(half_sweep)
         now, later = later, now
     middle[...] = now[ROWS - 1 : ROWS + 1]
 
 
-def rim_kernel(near_source, first, second, edges, middle, weights, pressure, near_pressure, source_wide, low, high):
+def rim_kernel(near_source, first, second, edges, middle, weights, source_wide, pressure, near_pressure, low, high):
     for message, side in ((first, Side(True)), (second, Side(False))):
         at = side.at(HALF + 2 * ROWS, 0)
         for row in range(HALF):
             source_wide[at + row] = message[row] * side.there
-
-    @pl.loop(0, 2 * ROWS, step=2)
-    def _(start):
-        for row in (start, start + 1):
-            source_wide[HALF + row] = near_source[row]
 
     for row in range(HALF):
         low[0, row] = -source_wide[row]
@@ -391,7 +386,7 @@
             velocity[k, :, :, columns] = jnp.swapaxes(predicted[k, :, g] - time_step * slope, 0, 1)
 
 
-def call(kernel, args, outs, scratch=(), vmem=16, to=pltpu.VMEM, flops=0):
+def call(kernel, args, outs, scratch=(), vmem=16, to=pltpu.VMEM, flops=0, aliases={}):
     spec = pl.BlockSpec(memory_space=pltpu.VMEM)
     shapes = [jax.ShapeDtypeStruct(shape, f32) for shape in outs]
     moved = sum(arg.size for arg in args) * 4 + sum(shape.size for shape in shapes) * 4
@@ -403,6 +398,7 @@
         scratch_shapes=[pltpu.VMEM(shape, f32) if isinstance(shape, tuple) else shape for shape in scratch],
         cost_estimate=pl.CostEstimate(flops=flops, bytes_accessed=moved, transcendentals=0),
         compiler_params=pltpu.CompilerParams(vmem_limit_bytes=vmem * 1024 * 1024),
+        input_output_aliases=aliases,
         name=kernel.__name__,
     )(*args)
 
@@ -470,15 +466,16 @@
     near_source, edges, middle = call(
         inner_kernel,
         (source, first, second, weights),
-        [(2 * ROWS,) + field, (SWEEPS - 1, 4) + field, (2,) + field],
+        [(WIDE,) + field, (SWEEPS - 1, 4) + field, (2,) + field],
         [(2 * ROWS,) + field] * 2,
         flops=COVER,
     )
-    pressure, near_pressure = call(
+    _, pressure, near_pressure = call(
         rim_kernel,
         (near_source, first_far, second_far, edges, middle, weights),
-        [(GROUPS, ROWS, PLANES, LANES), near],
-        [(WIDE,) + field, (2, HALF + 2) + field, (2, HALF + 2) + field],
+        [(WIDE,) + field, (GROUPS, ROWS, PLANES, LANES), near],
+        [(2, HALF + 2) + field, (2, HALF + 2) + field],
+        aliases={0: 0},
     )
 
     velocity, slopes = call(

time: 128 us -> 128 us (level)
  no operation moved by 1% of the time
where the time goes in v5:
time: 128 us; the launch traced here: 127 us
  waiting for transfers between devices  49 us (38%)
  starting transfers between devices  35.7 us (28%)
  Pallas kernels  17.6 us (14%)
  blocking collectives  15.6 us (12%)
  local copies, waits for them, and re-layouts  8.55 us (7%)
    ppermute x10, starting transfers between devices, swap(): return (lax.ppermute(first, AXES, inner), lax.ppermute(second, AXES, outer))  19 us
    all_to_all x1, waiting for transfers between devices, shards(): slab = lax.all_to_all(blocks, 'gx', split_axis=0, concat_axis=0, tiled=True)  17.7 us
    pallas_call x9, Pallas kernels, call(): pl.pallas_call(kernel, out_shape=shapes, in_specs=[spec] * len(args), out...  17.6 us
    all_to_all x1, waiting for transfers between devices, shards(): lax.all_to_all(blocks, 'gy', split_axis=0, concat_axis=0, tiled=True)  15.7 us
    all_to_all x1, blocking collectives, shards(): lax.all_to_all(pressure, 'gx', split_axis=0, concat_axis=0, tiled=True)  15.6 us
    ppermute x10, waiting for transfers between devices, swap(): return (lax.ppermute(first, AXES, inner), lax.ppermute(second, AXES, outer))  8.83 us
    unnamed x26, local copies, waits for them, and re-layouts  7.67 us
    all_to_all x1, waiting for transfers between devices, shards(): lax.all_to_all(pressure, 'gy', split_axis=0, concat_axis=0, tiled=True)  6.79 us
  transfers between devices with their start and end apart: 13, of which 7 were waited for; matrix products, arithmetic and copies ran while one was open for 0% of the time, Pallas kernels for 10%

profile of v5, /device:TPU:0, one launch (start us, length us, event | category | flops | bytes accessed | tf_op | source)
XLA Modules:
  0.0 127.3 jit_solution(16488958977267146154)
XLA Ops:
  0.6 1.4 %copy-done = f32[3,8,128,128]{3,2,1,0:T(8,128)S(1)} copy-done((f32[3,8,128,128]{3,2,1,0:T(8,128)S(1)}, f32[3,8,128,128]{3,2,1,0:T(8,128)}, u32[]{:S(2)}) %copy-start) | copy-done | bytes 1572888
  2.0 1.2 block_kernel.1
  3.3 6.5 %all-to-all-start = ((f32[8,2,3,8,8,128]{5,4,3,2,1,0:T(8,128)}), f32[8,2,3,8,8,128]{5,4,3,2,1,0:T(8,128)}, u32[]{:S(2)}, u32[]{:S(2)}) async-start(f32[8,2,3,8,8,128]{5,4,3,2,1,0:T(8,128)} %block_kernel.1), calls=%async_computation | async-start | bytes 3145728 | tf_op jit(solution)/shard_map/all_to_all | solution.py:434
  10.5 1.1 copy-done.4
  11.6 0.8 copy-done.6
  12.4 0.8 copy-done.8
  13.2 0.7 copy-done.11
  13.9 0.7 copy-done.12
  14.6 15.7 %all-to-all-done = f32[8,2,3,8,8,128]{5,4,3,2,1,0:T(8,128)} async-done(((f32[8,2,3,8,8,128]{5,4,3,2,1,0:T(8,128)}), f32[8,2,3,8,8,128]{5,4,3,2,1,0:T(8,128)}, u32[]{:S(2)}, u32[]{:S(2)}) %all-to-all-start) | async-done | bytes 1572896 | tf_op jit(solution)/shard_map/all_to_all | solution.py:434
  30.3 6.7 %all-to-all-start.1 = ((f32[16,3,8,8,128]{4,3,2,1,0:T(8,128)}), f32[16,3,8,8,128]{4,3,2,1,0:T(8,128)S(1)}, u32[]{:S(2)}, u32[]{:S(2)}) async-start(f32[16,3,8,8,128]{4,3,2,1,0:T(8,128)} %bitcast), calls=%async_computation.1 | async-start | bytes 3145728 | tf_op jit(solution)/shard_map/all_to_all | solution.py:438
  37.1 0.9 collective-permute-start.2
  38.0 5.4 %collective-permute-start.3 = (f32[4,16,8,128]{3,2,1,0:T(8,128)}, f32[4,16,8,128]{3,2,1,0:T(8,128)}, u32[]{:S(2)}, u32[]{:S(2)}) collective-permute-start(f32[4,16,8,128]{3,2,1,0:T(8,128)} %copy-done.11), channel_id=1, source_target_pairs={{0,127},{1,2},{2,1},{3,4},{4,3},{5,6},{6,5},{7,8},{8,7},{9,10},{10... | collective-permute-start | bytes 786440 | tf_op jit(solution)/shard_map/ppermute | solution.py:410
  43.4 17.7 %all-to-all-done.1.velocity = f32[16,3,8,8,128]{4,3,2,1,0:T(8,128)S(1)} async-done(((f32[16,3,8,8,128]{4,3,2,1,0:T(8,128)}), f32[16,3,8,8,128]{4,3,2,1,0:T(8,128)S(1)}, u32[]{:S(2)}, u32[]{:S(2)}) %all-to-all-start.1) | async-done | bytes 1572896 | tf_op jit(solution)/shard_map/all_to_all | solution.py:438
  62.1 2.6 %collective-permute-start.6 = (f32[6,16,8,128]{3,2,1,0:T(8,128)}, f32[6,16,8,128]{3,2,1,0:T(8,128)S(1)}, u32[]{:S(2)}, u32[]{:S(2)}) collective-permute-start(f32[6,16,8,128]{3,2,1,0:T(8,128)} %copy-done.10), channel_id=1, source_target_pairs={{0,1},{1,0},{2,3},{3,2},{4,5},{5,4},{6,7},{7,6},{8,9},{9,8},{10,11... | collective-permute-start | bytes 1179656 | tf_op jit(solution)/shard_map/ppermute | solution.py:410
  64.7 4.2 %collective-permute-start.7 = (f32[6,16,8,128]{3,2,1,0:T(8,128)S(1)}, f32[6,16,8,128]{3,2,1,0:T(8,128)S(1)}, u32[]{:S(2)}, u32[]{:S(2)}) collective-permute-start(f32[6,16,8,128]{3,2,1,0:T(8,128)S(1)} %get-tuple-element.63), channel_id=1, source_target_pairs={{0,127},{1,2},{2,1},{3,4},{4,3},{5,6},{6,5},{7,8},{8,7},{9,10},{10... | collective-permute-start | bytes 1179656 | tf_op jit(solution)/shard_map/ppermute | solution.py:410
  68.9 1.0 copy-done.7
  70.0 1.0 copy-done.9
  71.0 2.2 %coefficient_kernel.1 = (f32[10,6,16,8,128]{4,3,2,1,0:T(8,128)S(1)}, f32[8,16,8,128]{3,2,1,0:T(8,128)S(1)}, f32[10,16,8,128]{3,2,1,0:T(8,128)S(1)}, f32[10,16,8,...) custom-call(f32[8,16,8,128]{3,2,1,0:T(8,128)S(1)} %copy-done.7, ...), custom_call_target="tpu_custom_call" | custom-call | flops 6000000000 | bytes 11665408 | tf_op jit(solution)/shard_map/coefficient_kernel/pallas_call | solution.py:393
  73.3 1.7 %collective-permute-done.1.second = f32[4,16,8,128]{3,2,1,0:T(8,128)S(1)} collective-permute-done((f32[4,16,8,128]{3,2,1,0:T(8,128)S(1)}, f32[4,16,8,128]{3,2,1,0:T(8,128)S(1)}, u32[]{:S(2)}, u32[]{:S(2)}) %collective-permute-start.1) | collective-permute-done | bytes 262176 | tf_op jit(solution)/shard_map/ppermute | solution.py:410
  75.0 2.3 %momentum_kernel.1 = (f32[3,8,16,8,128]{4,3,2,1,0:T(8,128)S(1)}, f32[8,16,8,128]{3,2,1,0:T(8,128)S(1)}, f32[4,16,8,128]{3,2,1,0:T(8,128)S(1)}, f32[4,16,8,128]{3,2,1,0:T(8,128)S(1)}) custom-call(f32[16,3,8,8,128]{4,3,2,1,0:T(8,128)S(1)} %all-to-all-done.1.velocity, f32[4,16,8,128]{3,2,1,0:T(8,128)S(1)} %collective-permute-done.first, ...), custom_call_target="tpu_custom_call" | custom-call | bytes 13238272 | tf_op jit(solution)/shard_map/momentum_kernel/pallas_call | solution.py:393
  77.4 1.3 %collective-permute-start.5 = (f32[4,16,8,128]{3,2,1,0:T(8,128)S(1)}, f32[4,16,8,128]{3,2,1,0:T(8,128)S(1)}, u32[]{:S(2)}, u32[]{:S(2)}) collective-permute-start(f32[4,16,8,128]{3,2,1,0:T(8,128)S(1)} %get-tuple-element.66), channel_id=1, source_target_pairs={{0,127},{1,2},{2,1},{3,4},{4,3},{5,6},{6,5},{7,8},{8,7},{9,10},{10... | collective-permute-start | bytes 786440 | tf_op jit(solution)/shard_map/ppermute | solution.py:410
  78.7 2.6 %collective-permute-done.7.second = f32[6,16,8,128]{3,2,1,0:T(8,128)S(1)} collective-permute-done((f32[6,16,8,128]{3,2,1,0:T(8,128)S(1)}, f32[6,16,8,128]{3,2,1,0:T(8,128)S(1)}, u32[]{:S(2)}, u32[]{:S(2)}) %collective-permute-start.7) | collective-permute-done | bytes 393248 | tf_op jit(solution)/shard_map/ppermute | solution.py:410
  81.3 1.5 %outer_kernel.1.weights = f32[22,6,16,8,128]{4,3,2,1,0:T(8,128)S(1)} custom-call(f32[12,16,8,128]{3,2,1,0:T(8,128)S(1)} %get-tuple-element.58.voids_near, f32[6,16,8,128]{3,2,1,0:T(8,128)S(1)} %collective-permute-done.6.first, f32[6,16,8,128]{3,2,1,0:T(8,128)S(1)} %collective-permute-done.7.second, ...), custom_call_target="tpu_custom_call" | custom-call | flops 6000000000 | bytes 14155776 | tf_op jit(solution)/shard_map/outer_kernel/pallas_call | solution.py:393
  82.9 3.4 %collective-permute-start.9 = (f32[4,16,8,128]{3,2,1,0:T(8,128)S(1)}, f32[4,16,8,128]{3,2,1,0:T(8,128)S(1)}, u32[]{:S(2)}, u32[]{:S(2)}) collective-permute-start(f32[4,16,8,128]{3,2,1,0:T(8,128)S(1)} %get-tuple-element.67), channel_id=1, source_target_pairs={{0,127},{1,2},{2,1},{3,4},{4,3},{5,6},{6,5},{7,8},{8,7},{9,10},{10... | collective-permute-start | bytes 786440 | tf_op jit(solution)/shard_map/ppermute | solution.py:410
  86.3 4.4 %collective-permute-done.5.second = f32[4,16,8,128]{3,2,1,0:T(8,128)S(1)} collective-permute-done((f32[4,16,8,128]{3,2,1,0:T(8,128)S(1)}, f32[4,16,8,128]{3,2,1,0:T(8,128)S(1)}, u32[]{:S(2)}, u32[]{:S(2)}) %collective-permute-start.5) | collective-permute-done | bytes 262176 | tf_op jit(solution)/shard_map/ppermute | solution.py:410
  90.7 3.4 %inner_kernel.1 = (f32[24,16,8,128]{3,2,1,0:T(8,128)S(1)}, f32[7,4,16,8,128]{4,3,2,1,0:T(8,128)S(1)}, f32[2,16,8,128]{3,2,1,0:T(8,128)S(1)}) custom-call(f32[8,16,8,128]{3,2,1,0:T(8,128)S(1)} %get-tuple-element.59.source, f32[4,16,8,128]{3,2,1,0:T(8,128)S(1)} %collective-permute-done.4.first, f32[4,16,8,128]{3,2,1,0:T(8,128)S(1)} %collective-permute-done.5.second, ...), custom_call_target="tpu_custom_call" | custom-call | flops 6000000000 | bytes 13238272 | tf_op jit(solution)/shard_map/inner_kernel/pallas_call | solution.py:393
  94.2 3.7 %rim_kernel.1 = (f32[24,16,8,128]{3,2,1,0:T(8,128)S(1)}, f32[16,8,8,128]{3,2,1,0:T(8,128)S(1)}, f32[10,16,8,128]{3,2,1,0:T(8,128)S(1)}) custom-call(f32[24,16,8,128]{3,2,1,0:T(8,128)S(1)} %get-tuple-element.65.near_source, f32[4,16,8,128]{3,2,1,0:T(8,128)S(1)} %collective-permute-done.8.first, ...), custom_call_target="tpu_custom_call", output_to_operand_aliasing={{0}: (0, {})} | custom-call | bytes 15466496 | tf_op jit(solution)/shard_map/rim_kernel/pallas_call | solution.py:393
  97.9 15.6 %all_to_all.20 = f32[16,8,8,128]{3,2,1,0:T(8,128)} all-to-all(f32[16,8,8,128]{3,2,1,0:T(8,128)S(1)} %get-tuple-element.70), channel_id=1, replica_groups=mesh['gx'=16,'gy'=8] {'gx'}, dimensions={0} | all-to-all | bytes 1048576 | tf_op jit(solution)/shard_map/all_to_all | solution.py:485
  113.6 3.5 %all-to-all-start.3 = ((f32[16,8,8,128]{3,2,1,0:T(8,128)}), f32[16,8,8,128]{3,2,1,0:T(8,128)S(1)}, u32[]{:S(2)}, u32[]{:S(2)}) async-start(f32[16,8,8,128]{3,2,1,0:T(8,128)} %all_to_all.20), calls=%async_computation.3 | async-start | bytes 1048576 | tf_op jit(solution)/shard_map/all_to_all | solution.py:486
  117.1 2.6 %correct_kernel.1 = (f32[3,8,8,2048]{3,2,1,0:T(8,128)}, f32[3,8,8,2048]{3,2,1,0:T(8,128)}) custom-call(f32[10,16,8,128]{3,2,1,0:T(8,128)S(1)} %get-tuple-element.71.near_pressure, f32[3,8,16,8,128]{4,3,2,1,0:T(8,128)S(1)} %get-tuple-element.72.predicted), custom_call_target="tpu_custom_call" | custom-call | bytes 5373952 | tf_op jit(solution)/shard_map/correct_kernel/pallas_call | solution.py:393
  119.7 6.8 %all-to-all-done.3 = f32[16,8,8,128]{3,2,1,0:T(8,128)S(1)} async-done(((f32[16,8,8,128]{3,2,1,0:T(8,128)}), f32[16,8,8,128]{3,2,1,0:T(8,128)S(1)}, u32[]{:S(2)}, u32[]{:S(2)}) %all-to-all-start.3) | async-done | bytes 524320 | tf_op jit(solution)/shard_map/all_to_all | solution.py:486
  126.5 0.9 copy.8
  (31 shorter events, 1.9 us)
Async XLA Ops:
  0.6 1.4 %copy-start = (f32[3,8,128,128]{3,2,1,0:T(8,128)S(1)}, f32[3,8,128,128]{3,2,1,0:T(8,128)}, u32[]{:S(2)}) copy-start(f32[3,8,128,128]{3,2,1,0:T(8,128)} %velocity.2) | copy-start | bytes 4718596
  3.3 6.5 %copy-start.1 = (f32[3,8,8,2048]{3,2,1,0:T(8,128)S(1)}, f32[3,8,8,2048]{3,2,1,0:T(8,128)}, u32[]{:S(2)}) copy-start(f32[3,8,8,2048]{3,2,1,0:T(8,128)} %velocity.3) | copy-start | bytes 4718596
  3.3 6.5 %copy-start.2 = (s32[8,8,2048]{2,1,0:T(8,128)S(1)}, s32[8,8,2048]{2,1,0:T(8,128)}, u32[]{:S(2)}) copy-start(s32[8,8,2048]{2,1,0:T(8,128)} %count.1) | copy-start | bytes 1572868
  3.3 6.5 %copy-start.3 = (f32[8,8,2048]{2,1,0:T(8,128)S(1)}, f32[8,8,2048]{2,1,0:T(8,128)}, u32[]{:S(2)}) copy-start(f32[8,8,2048]{2,1,0:T(8,128)} %drag.1) | copy-start | bytes 1572868
  3.3 27.0 %all-to-all-start = ((f32[8,2,3,8,8,128]{5,4,3,2,1,0:T(8,128)}), f32[8,2,3,8,8,128]{5,4,3,2,1,0:T(8,128)}, u32[]{:S(2)}, u32[]{:S(2)}) async-start(f32[8,2,3,8,8,128]{5,4,3,2,1,0:T(8,128)} %block_kernel.1), calls=%async_computation | async-start | bytes 3145728 | tf_op jit(solution)/shard_map/all_to_all | solution.py:434
  10.5 1.1 copy-start.4
  11.6 0.8 copy-start.6
  12.4 0.8 copy-start.8
  13.2 0.7 copy-start.11
  13.9 0.7 copy-start.12
  14.6 15.7 %copy-start.10 = (f32[6,16,8,128]{3,2,1,0:T(8,128)}, f32[6,16,8,128]{3,2,1,0:T(8,128)S(1)}, u32[]{:S(2)}) copy-start(f32[6,16,8,128]{3,2,1,0:T(8,128)S(1)} %get-tuple-element.62) | copy-start | bytes 1179652
  30.3 30.9 %all-to-all-start.1 = ((f32[16,3,8,8,128]{4,3,2,1,0:T(8,128)}), f32[16,3,8,8,128]{4,3,2,1,0:T(8,128)S(1)}, u32[]{:S(2)}, u32[]{:S(2)}) async-start(f32[16,3,8,8,128]{4,3,2,1,0:T(8,128)} %bitcast), calls=%async_computation.1 | async-start | bytes 3145728 | tf_op jit(solution)/shard_map/all_to_all | solution.py:438
  37.1 31.9 %copy-start.5 = (f32[3,8,16,8,128]{4,3,2,1,0:T(8,128)S(1)}, f32[3,8,16,8,128]{4,3,2,1,0:T(8,128)}, u32[]{:S(2)}) copy-start(f32[3,8,16,8,128]{4,3,2,1,0:T(8,128)} %copy-done.4) | copy-start | bytes 4718596
  37.1 27.6 %collective-permute-start.2 = (f32[4,16,8,128]{3,2,1,0:T(8,128)}, f32[4,16,8,128]{3,2,1,0:T(8,128)}, u32[]{:S(2)}, u32[]{:S(2)}) collective-permute-start(f32[4,16,8,128]{3,2,1,0:T(8,128)} %copy-done.12), channel_id=1, source_target_pairs={{0,1},{1,0},{2,3},{3,2},{4,5},{5,4},{6,7},{7,6},{8,9},{9,8},{10,11... | collective-permute-start | bytes 786440 | tf_op jit(solution)/shard_map/ppermute | solution.py:410
  38.0 30.9 %collective-permute-start.3 = (f32[4,16,8,128]{3,2,1,0:T(8,128)}, f32[4,16,8,128]{3,2,1,0:T(8,128)}, u32[]{:S(2)}, u32[]{:S(2)}) collective-permute-start(f32[4,16,8,128]{3,2,1,0:T(8,128)} %copy-done.11), channel_id=1, source_target_pairs={{0,127},{1,2},{2,1},{3,4},{4,3},{5,6},{6,5},{7,8},{8,7},{9,10},{10... | collective-permute-start | bytes 786440 | tf_op jit(solution)/shard_map/ppermute | solution.py:410
  61.2 12.0 %collective-permute-start = (f32[4,16,8,128]{3,2,1,0:T(8,128)S(1)}, f32[4,16,8,128]{3,2,1,0:T(8,128)S(1)}, u32[]{:S(2)}, u32[]{:S(2)}) collective-permute-start(f32[4,16,8,128]{3,2,1,0:T(8,128)S(1)} %get-tuple-element.46), channel_id=1, source_target_pairs={{0,1},{1,0},{2,3},{3,2},{4,5},{5,4},{6,7},{7,6},{8,9},{9,8},{10,11... | collective-permute-start | bytes 786440 | tf_op jit(solution)/shard_map/ppermute | solution.py:410
  61.7 13.2 %collective-permute-start.1 = (f32[4,16,8,128]{3,2,1,0:T(8,128)S(1)}, f32[4,16,8,128]{3,2,1,0:T(8,128)S(1)}, u32[]{:S(2)}, u32[]{:S(2)}) collective-permute-start(f32[4,16,8,128]{3,2,1,0:T(8,128)S(1)} %get-tuple-element.47), channel_id=1, source_target_pairs={{0,127},{1,2},{2,1},{3,4},{4,3},{5,6},{6,5},{7,8},{8,7},{9,10},{10... | collective-permute-start | bytes 786440 | tf_op jit(solution)/shard_map/ppermute | solution.py:410
  62.1 16.7 %collective-permute-start.6 = (f32[6,16,8,128]{3,2,1,0:T(8,128)}, f32[6,16,8,128]{3,2,1,0:T(8,128)S(1)}, u32[]{:S(2)}, u32[]{:S(2)}) collective-permute-start(f32[6,16,8,128]{3,2,1,0:T(8,128)} %copy-done.10), channel_id=1, source_target_pairs={{0,1},{1,0},{2,3},{3,2},{4,5},{5,4},{6,7},{7,6},{8,9},{9,8},{10,11... | collective-permute-start | bytes 1179656 | tf_op jit(solution)/shard_map/ppermute | solution.py:410
  64.7 16.6 %collective-permute-start.7 = (f32[6,16,8,128]{3,2,1,0:T(8,128)S(1)}, f32[6,16,8,128]{3,2,1,0:T(8,128)S(1)}, u32[]{:S(2)}, u32[]{:S(2)}) collective-permute-start(f32[6,16,8,128]{3,2,1,0:T(8,128)S(1)} %get-tuple-element.63), channel_id=1, source_target_pairs={{0,127},{1,2},{2,1},{3,4},{4,3},{5,6},{6,5},{7,8},{8,7},{9,10},{10... | collective-permute-start | bytes 1179656 | tf_op jit(solution)/shard_map/ppermute | solution.py:410
  68.9 1.0 copy-start.7
  70.0 1.0 copy-start.9
  77.3 9.0 %collective-permute-start.4 = (f32[4,16,8,128]{3,2,1,0:T(8,128)S(1)}, f32[4,16,8,128]{3,2,1,0:T(8,128)S(1)}, u32[]{:S(2)}, u32[]{:S(2)}) collective-permute-start(f32[4,16,8,128]{3,2,1,0:T(8,128)S(1)} %get-tuple-element.67), channel_id=1, source_target_pairs={{0,1},{1,0},{2,3},{3,2},{4,5},{5,4},{6,7},{7,6},{8,9},{9,8},{10,11... | collective-permute-start | bytes 786440 | tf_op jit(solution)/shard_map/ppermute | solution.py:410
  77.4 13.3 %collective-permute-start.5 = (f32[4,16,8,128]{3,2,1,0:T(8,128)S(1)}, f32[4,16,8,128]{3,2,1,0:T(8,128)S(1)}, u32[]{:S(2)}, u32[]{:S(2)}) collective-permute-start(f32[4,16,8,128]{3,2,1,0:T(8,128)S(1)} %get-tuple-element.66), channel_id=1, source_target_pairs={{0,127},{1,2},{2,1},{3,4},{4,3},{5,6},{6,5},{7,8},{8,7},{9,10},{10... | collective-permute-start | bytes 786440 | tf_op jit(solution)/shard_map/ppermute | solution.py:410
  82.8 11.3 %collective-permute-start.8 = (f32[4,16,8,128]{3,2,1,0:T(8,128)S(1)}, f32[4,16,8,128]{3,2,1,0:T(8,128)S(1)}, u32[]{:S(2)}, u32[]{:S(2)}) collective-permute-start(f32[4,16,8,128]{3,2,1,0:T(8,128)S(1)} %get-tuple-element.66), channel_id=1, source_target_pairs={{0,1},{1,0},{2,3},{3,2},{4,5},{5,4},{6,7},{7,6},{8,9},{9,8},{10,11... | collective-permute-start | bytes 786440 | tf_op jit(solution)/shard_map/ppermute | solution.py:410
  82.9 11.3 %collective-permute-start.9 = (f32[4,16,8,128]{3,2,1,0:T(8,128)S(1)}, f32[4,16,8,128]{3,2,1,0:T(8,128)S(1)}, u32[]{:S(2)}, u32[]{:S(2)}) collective-permute-start(f32[4,16,8,128]{3,2,1,0:T(8,128)S(1)} %get-tuple-element.67), channel_id=1, source_target_pairs={{0,127},{1,2},{2,1},{3,4},{4,3},{5,6},{6,5},{7,8},{8,7},{9,10},{10... | collective-permute-start | bytes 786440 | tf_op jit(solution)/shard_map/ppermute | solution.py:410
  113.6 12.9 %all-to-all-start.3 = ((f32[16,8,8,128]{3,2,1,0:T(8,128)}), f32[16,8,8,128]{3,2,1,0:T(8,128)S(1)}, u32[]{:S(2)}, u32[]{:S(2)}) async-start(f32[16,8,8,128]{3,2,1,0:T(8,128)} %all_to_all.20), calls=%async_computation.3 | async-start | bytes 1048576 | tf_op jit(solution)/shard_map/all_to_all | solution.py:486
